TPU v7x, 256 devices: a whole 4x4x8 slice. The times are simulated.
256 devices in a mesh: sp: 32 (over z, y_lo, core), flt: 8 (over x, y_hi).
Axes of the slice: x: 4, y: 4 (y_hi: 2, y_lo: 2; y = y_hi * 2 + y_lo), z: 8, core: 2. Of those that a mesh axis runs over, the one named last changes fastest.
Arguments:
- activations: bfloat16 [64, 64, 8, 256], P('sp', 'flt'), may hold values from -6 to 6
- w_first: bfloat16 [256, 3, 3, 3, 256], P('flt'), may hold values from -0.078125 to 0.078125
- w_second: bfloat16 [256, 3, 3, 3, 256], P('flt'), may hold values from -0.078125 to 0.078125
- cotangent: bfloat16 [32, 32, 4, 256], P('sp', 'flt'), may hold values from -6 to 6
Outputs:
- section_out: float32 [32, 32, 4, 256], P('sp', 'flt')
- grad_input: float32 [64, 64, 8, 256], P('sp', 'flt')
- grad_first: float32 [256, 3, 3, 3, 256], P('flt')
- grad_second: float32 [256, 3, 3, 3, 256], P('flt')
All inputs are finite; a program needn't handle non-finite values.
Results may differ from a plain program's by a relative error of at most 0.0045.
Values may be sent and summed in bfloat16 or wider, within the bound.
No kernel may reach another device: no remote copies, remote signals or barrier semaphores. Data moves between devices by JAX's collectives and lax.ppermute only.
A program may use at most 64 MiB of HBM per device.

v0:
```python
import jax
import jax.numpy as jnp
from jax import lax
from jax.experimental import pallas as pl
from jax.experimental.pallas import tpu as pltpu
from jax.sharding import Mesh
from jax.sharding import PartitionSpec as P

SP = ("sp_z", "sp_y", "core")
CHIPS = ("sp_z", "sp_y")
bf16, f32 = jnp.bfloat16, jnp.float32

ROWS = 256
X_ROWS, COT_ROWS, W_ROWS = 256, 32, 288
PACK = X_ROWS + COT_ROWS + W_ROWS
GRAD_ROWS, GRAD_PAD = 1728, 1792
NT = (((1,), (1,)), ((), ()))
NN = (((1,), (0,)), ((), ()))
TN = (((0,), (0,)), ((), ()))


def dot(a, b, dims):
    return lax.dot_general(a, b, dims, preferred_element_type=f32)


def kernel_call(body, outs, flops, *args, scratch=()):
    vmem = pl.BlockSpec(memory_space=pltpu.VMEM)
    moved = sum(a.size * a.dtype.itemsize for a in (*args, *outs))
    return pl.pallas_call(
        body,
        out_shape=outs,
        in_specs=[vmem] * len(args),
        out_specs=[vmem] * len(outs),
        scratch_shapes=scratch,
        compiler_params=pltpu.CompilerParams(vmem_limit_bytes=32 << 20),
        cost_estimate=pl.CostEstimate(flops=flops, bytes_accessed=moved, transcendentals=0),
    )(*args)


def shape(dims, dtype):
    return jax.ShapeDtypeStruct(dims, dtype)


def lanes(rows):
    return lax.broadcasted_iota(jnp.int32, (rows, 128), 1)


def cells(rows):
    return lax.rem(lax.broadcasted_iota(jnp.int32, (rows, 128), 0), 8)


def before(v):
    return jnp.where(cells(v.shape[0]) == 0, 0.0, pltpu.roll(v, 1, 0))


def after(v):
    return jnp.where(cells(v.shape[0]) == 7, 0.0, pltpu.roll(v, v.shape[0] - 1, 0))


def rotated(v, slots):
    by = (32 * slots) % 128
    return pltpu.roll(v, by, 1) if by else v


def three(a, b, c):
    lane = lanes(a.shape[0])
    return jnp.where(lane < 32, a, jnp.where(lane < 64, b, jnp.where(lane < 96, c, 0.0)))


def row_down(v):
    return jnp.concatenate([jnp.zeros((8, v.shape[1]), v.dtype), v[:-8]], 0)


def row_up(v):
    return jnp.concatenate([v[8:], jnp.zeros((8, v.shape[1]), v.dtype)], 0)


def tap_sum(first, middle, last):
    lane = lanes(ROWS)
    t = jnp.where(lane < 32, first, jnp.where(lane < 64, middle, last))
    return t + rotated(t, -1) + rotated(t, -2)


def pair_of(pieces):
    lane = lanes(ROWS)
    v = pieces[0]
    for slot in (1, 2, 3):
        v = jnp.where(lane < 32 * slot, v, rotated(pieces[slot], slot))
    return v


def sigmoid(v):
    return jax.nn.sigmoid(v)


def silu_slope(v):
    s = sigmoid(v)
    return s * (1.0 + v * (1.0 - s))


def pack_inputs(x, w, cot, out):
    for f in range(8):
        for h in (0, 1):
            out[f, h * 128 : h * 128 + 128, :] = x[:, h * 128 : h * 128 + 128]
            at = X_ROWS + h * 16
            out[f, at : at + 16, :] = cot[:, h * 128 : h * 128 + 128]
    for k in range(9):
        for h in (0, 1):
            taps = [
                w[(3 * k + t) * 32 : (3 * k + t) * 32 + 32, h * 128 : h * 128 + 128].astype(f32)
                for t in range(3)
            ]
            for m in range(4):
                v = three(*(rotated(taps[t], t - m) for t in range(3)))
                at = X_ROWS + COT_ROWS + k * 32
                out[4 * h + m, at : at + 32, :] = v.astype(bf16)


def prepare_first(w, wide, tall):
    zero = jnp.zeros((32, 256), bf16)
    for k0 in range(3):
        for k1 in range(3):
            for t in range(4):
                at = ((k0 * 3 + k1) * 3 + t) * 32
                v = w[at : at + 32, :] if t < 3 else zero
                wide[k0 * 128 + t * 32 : k0 * 128 + t * 32 + 32, k1 * 256 : k1 * 256 + 256] = v
                row = (k0 * 3 + k1) * 128 + t * 32
                tall[row : row + 32, :] = v


def first_conv(got, wide, low, high, field, window):
    parts = {}
    for h in (0, 1):
        for p in (0, 1):
            blocks = ([], [])
            for g in range(8):
                at = h * 128 + p * 64
                v = got[g, at : at + 64, :].astype(f32).reshape(4, 2, 8, 128)
                for par in (0, 1):
                    blocks[par].append(v[:, par].reshape(32, 128))
            for par in (0, 1):
                parts[p, par, h] = jnp.concatenate(blocks[par], 0)
    for p in (0, 1):
        for h in (0, 1):
            even, odd = parts[p, 0, h], parts[p, 1, h]
            sources = ((row_down(odd), even, odd), (even, odd, row_up(even)))
            for par in (0, 1):
                at = (2 * p + par) * ROWS
                for k1 in range(3):
                    lane = k1 * 256 + h * 128
                    window[at : at + ROWS, lane : lane + 128] = sources[par][k1].astype(bf16)
                field[at : at + ROWS, h * 128 : h * 128 + 128] = sources[par][1].astype(bf16)
    sums = [dot(window[i * ROWS : i * ROWS + ROWS, :], wide[...], NT) for i in range(4)]
    pieces = []
    for plane in range(4):
        for par in (0, 1):
            terms = [
                sums[2 * p + par][:, k0 * 128 : k0 * 128 + 128]
                for p in (0, 1)
                for k0 in range(3)
                if p - k0 + 2 == plane
            ]
            v = terms[0] if len(terms) == 1 else terms[0] + terms[1]
            pieces.append(tap_sum(before(v), v, after(v)))
    low[...] = pair_of(pieces[:4])
    high[...] = pair_of(pieces[4:])


def gather_second(got, w2):
    for g in range(8):
        for k in range(9):
            at = X_ROWS + COT_ROWS + k * 32
            w2[g * 32 : g * 32 + 32, k * 128 : k * 128 + 128] = got[g, at : at + 32, :]


def at_first_plane():
    return sum(lax.axis_index(name) for name in SP) == 0


def without_edge(v):
    return jnp.where(jnp.logical_and(at_first_plane(), lanes(ROWS) < 64), 0.0, v)


def second_conv(low, high, below, above, w2, pre, window, out, full):
    pairs = [low[...] + below[...], high[...] + above[...]]
    pre[0:ROWS, :] = pairs[0]
    pre[ROWS:, :] = pairs[1]
    hidden = [v * sigmoid(v) for v in pairs]
    hidden[0] = without_edge(hidden[0])
    hidden = [v.astype(bf16).astype(f32) for v in hidden]
    shifted = [(before(v), v, after(v)) for v in hidden]
    for plane in range(3):
        pair = shifted[plane // 2]
        for par in (0, 1):
            slot = (plane % 2) * 2 + par
            v = three(*(rotated(pair[t], t - slot) for t in range(3)))
            at = (plane * 3 + 1 + par) * 128
            window[:, at : at + 128] = v.astype(bf16)
            if par:
                window[:, plane * 384 : plane * 384 + 128] = row_down(v).astype(bf16)
    total = dot(window[...], w2[...], NT)
    for h in (0, 1):
        full[h] = total[:, h * 128 : h * 128 + 128]
        v = full[h, pl.ds(0, 128, 2), :].astype(bf16)
        for g in range(8):
            out[g, :, h * 128 : h * 128 + 128] = v


def second_error(parts, got, section, err):
    for h in (0, 1):
        lane = slice(h * 128, h * 128 + 128)
        v = parts[0, :, lane].astype(f32)
        for g in range(1, 8):
            v = v + parts[g, :, lane].astype(f32)
        cot = jnp.concatenate(
            [got[g, X_ROWS + h * 16 : X_ROWS + h * 16 + 16, :].astype(f32) for g in range(8)], 0
        )
        section[:, lane] = v * sigmoid(v)
        err[:, lane] = (cot * silu_slope(v)).astype(bf16)


def spread_out(err, full):
    halves = []
    for h in (0, 1):
        full[h] = jnp.zeros((ROWS, 128), f32)
        full[h, pl.ds(0, 128, 2), :] = err[:, h * 128 : h * 128 + 128].astype(f32)
        halves.append(full[h])
    return jnp.concatenate(halves, 1)


def second_grad(err, window, out, full):
    spread = spread_out(err, full).astype(bf16)
    grad = dot(spread, window[...], TN)
    for g in range(8):
        for k in range(9):
            v = grad[g * 32 : g * 32 + 32, k * 128 : k * 128 + 128]
            out[g, k * 32 : k * 32 + 32, :] = v.astype(bf16)


def first_error(own, below, above, w2, pre, field, window, out, full):
    spread, ahead = [], []
    for err in (below, own, above):
        v = spread_out(err, full)
        spread.append(v.astype(bf16))
        ahead.append(row_up(v).astype(bf16))
    pieces = []
    for plane in range(4):
        both, extra = None, None
        for q, k0 in (((0, 2), (1, 0)), ((1, 1),), ((1, 2), (2, 0)), ((2, 1),))[plane]:
            at = k0 * 384
            a = dot(spread[q], w2[:, at + 128 : at + 384], NN)
            b = dot(ahead[q], w2[:, at : at + 128], NN)
            both = a if both is None else both + a
            extra = b if extra is None else extra + b
        for v in (both[:, :128], both[:, 128:] + extra):
            pieces.append(tap_sum(after(v), v, before(v)))
    errs = [pair_of(pieces[:4]), pair_of(pieces[4:])]
    errs = [errs[i] * silu_slope(pre[i * ROWS : i * ROWS + ROWS, :]) for i in (0, 1)]
    errs[0] = without_edge(errs[0])
    errs = [v.astype(bf16).astype(f32) for v in errs]
    shifted = [(after(v), v, before(v)) for v in errs]
    for plane in range(4):
        pair = shifted[plane // 2]
        taps = [
            three(*(rotated(pair[t], t - (plane % 2) * 2 - par) for t in range(3)))
            for par in (0, 1)
        ]
        even, odd = taps
        sources = ((odd, even, row_down(odd)), (row_up(even), odd, even))
        for par in (0, 1):
            for k1 in range(3):
                v = sources[par][k1].astype(bf16)
                for k0 in range(3):
                    target = plane + k0 - 1
                    if target in (1, 2):
                        at = (2 * (target - 1) + par) * ROWS
                        lane = (k0 * 3 + k1) * 128
                        window[at : at + ROWS, lane : lane + 128] = v
    grad = dot(window[...], field[...], TN)
    for h in (0, 1):
        for k in range(9):
            at = h * 864 + k * 96
            v = grad[k * 128 : k * 128 + 96, h * 128 : h * 128 + 128]
            out[at : at + 96, :] = v.astype(bf16)
    out[GRAD_ROWS:, :] = jnp.zeros((GRAD_PAD - GRAD_ROWS, 128), bf16)


def input_grad(window, tall, out):
    for p in (0, 1):
        even = dot(window[2 * p * ROWS : (2 * p + 1) * ROWS, :], tall[...], NN)
        odd = dot(window[(2 * p + 1) * ROWS : (2 * p + 2) * ROWS, :], tall[...], NN)
        for g in range(8):
            a = even[g * 32 : g * 32 + 32].reshape(4, 1, 8, 256)
            b = odd[g * 32 : g * 32 + 32].reshape(4, 1, 8, 256)
            v = jnp.concatenate([a, b], 1).reshape(64, 256)
            out[g, p * 64 : p * 64 + 64, :] = v.astype(bf16)


def split_grads(first, second, kept, sent):
    lane = lanes(32)
    core = lax.axis_index("core")

    def store(at, size, a, b):
        kept[at : at + size, :] = jnp.where(core == 0, a, b).astype(bf16)
        sent[at : at + size, :] = jnp.where(core == 0, b, a).astype(bf16)

    for h in (0, 1):
        for k in range(9):
            blocks = [second[4 * h + m, k * 32 : k * 32 + 32, :].astype(f32) for m in range(4)]
            for t in range(3):
                v = rotated(blocks[0], -t)
                for m in (1, 2, 3):
                    v = jnp.where(lane < 32 * m, v, rotated(blocks[m], m - t))
                at = h * 864 + (3 * k + t) * 32
                store(at, 32, first[at : at + 32, :].astype(f32), v)
    kept[GRAD_ROWS:, :] = jnp.zeros((GRAD_PAD - GRAD_ROWS, 128), bf16)
    sent[GRAD_ROWS:, :] = jnp.zeros((GRAD_PAD - GRAD_ROWS, 128), bf16)


def add_core(kept, came, out):
    v = kept[...].astype(f32) + came[...].astype(f32)
    out[...] = v.astype(bf16).reshape(16, GRAD_PAD // 16, 128)


def add_chips(parts, out):
    v = parts[0].astype(f32)
    for i in range(1, 16):
        v = v + parts[i].astype(f32)
    v = v.astype(bf16)
    for i in range(16):
        out[i] = v


def finish_grads(own, other, first, second):
    core = lax.axis_index("core")
    for h in (0, 1):
        lane = slice(h * 128, h * 128 + 128)
        a = own[h * 864 : h * 864 + 864, :].astype(f32)
        b = other[h * 864 : h * 864 + 864, :].astype(f32)
        first[:, lane] = jnp.where(core == 0, a, b)
        second[:, lane] = jnp.where(core == 0, b, a)


def add_parts(parts, out):
    v = parts[0].astype(f32)
    for g in range(1, 8):
        v = v + parts[g].astype(f32)
    out[...] = v


def exchange(v, axis):
    return lax.all_to_all(v, axis, 0, 0, tiled=True)


def upward(v):
    n = lax.axis_size(SP)
    return lax.ppermute(v, SP, [(i, i + 1) for i in range(n - 1)])


def downward(v):
    n = lax.axis_size(SP)
    return lax.ppermute(v, SP, [(i + 1, i) for i in range(n - 1)])


def swapped(v):
    return lax.ppermute(v, "core", [(0, 1), (1, 0)])


def as_rows(w):
    return jnp.transpose(w, (1, 2, 3, 0, 4)).reshape(864, 256)


def as_filters(rows):
    return jnp.transpose(rows.reshape(3, 3, 3, 32, 256), (3, 0, 1, 2, 4))


def per_device(activations, w_first, w_second, cotangent):
    spread_scratch = [pltpu.VMEM((2, ROWS, 128), f32)]
    wide, tall = kernel_call(
        prepare_first, [shape((384, 768), bf16), shape((1152, 256), bf16)], 0, as_rows(w_first)
    )
    (packed,) = kernel_call(
        pack_inputs,
        [shape((8, PACK, 128), bf16)],
        0,
        activations.reshape(128, 256),
        as_rows(w_second),
        cotangent.reshape(16, 256),
    )
    got = exchange(packed, "flt")
    low, high, field = kernel_call(
        first_conv,
        [shape((ROWS, 128), f32), shape((ROWS, 128), f32), shape((1024, 256), bf16)],
        2 * 1024 * 768 * 384,
        got,
        wide,
        scratch=[pltpu.VMEM((1024, 768), bf16)],
    )
    below, above = upward(high), downward(low)
    (w2,) = kernel_call(gather_second, [shape((256, 1152), bf16)], 0, got)
    pre, hidden_window, partial = kernel_call(
        second_conv,
        [shape((512, 128), f32), shape((ROWS, 1152), bf16), shape((8, 128, 256), bf16)],
        2 * 256 * 1152 * 256,
        low,
        high,
        below,
        above,
        w2,
        scratch=spread_scratch,
    )
    parts = exchange(partial, "flt")
    section, err = kernel_call(
        second_error, [shape((128, 256), f32), shape((128, 256), bf16)], 0, parts, got
    )
    err_below, err_above = upward(err), downward(err)
    (grad_second,) = kernel_call(
        second_grad,
        [shape((8, 288, 128), bf16)],
        2 * 256 * 1152 * 256,
        err,
        hidden_window,
        scratch=spread_scratch,
    )
    grad_second = exchange(grad_second, "flt")
    window, grad_first = kernel_call(
        first_error,
        [shape((1024, 1152), bf16), shape((GRAD_PAD, 128), bf16)],
        2 * 1024 * 1152 * 256 + 2 * 256 * 256 * 384 * 6,
        err,
        err_below,
        err_above,
        w2,
        pre,
        field,
        scratch=spread_scratch,
    )
    kept, sent = kernel_call(
        split_grads, [shape((GRAD_PAD, 128), bf16)] * 2, 0, grad_first, grad_second
    )
    came = swapped(sent)
    (inner,) = kernel_call(
        input_grad, [shape((8, 128, 256), bf16)], 2 * 1024 * 1152 * 256, window, tall
    )
    chunk = shape((16, GRAD_PAD // 16, 128), bf16)
    (mine,) = kernel_call(add_core, [chunk], 0, kept, came)
    (mine,) = kernel_call(add_chips, [chunk], 0, exchange(mine, CHIPS))
    inner = exchange(inner, "flt")
    mine = exchange(mine, CHIPS).reshape(GRAD_PAD, 128)
    grads = kernel_call(
        finish_grads, [shape((864, 256), f32)] * 2, 0, mine, swapped(mine)
    )
    (grad_input,) = kernel_call(add_parts, [shape((128, 256), f32)], 0, inner)
    row = lax.axis_index("flt") * 16
    section_out = lax.dynamic_slice_in_dim(section, row, 16, 0).reshape(1, 4, 4, 256)
    return (section_out, grad_input.reshape(2, 8, 8, 256), *(as_filters(g) for g in grads))


def solution(mesh):
    torus = Mesh(mesh.devices.reshape(8, 2, 2, mesh.shape["flt"]), (*SP, "flt"))
    whole = P("flt", None, None, None, None)
    rows = P(SP, "flt", None, None)
    return jax.shard_map(
        per_device,
        mesh=torus,
        in_specs=(rows, whole, whole, rows),
        out_specs=(rows, rows, whole, whole),
        check_vma=False,
    )
```

profile of v0, /device:TPU:2, one launch (start us, length us, event | category | flops | bytes accessed | tf_op | source)
XLA Modules:
  0.0 138.6 jit_solution(9558105230427373336)
XLA Ops:
  0.6 0.7 reshape.37.cot
  1.3 1.0 copy-done.2
  2.4 0.8 copy-done.4
  3.2 1.5 %shard_map.75 = bf16[8,576,128]{2,1,0:T(8,128)(2,1)} custom-call(bf16[128,256]{1,0:T(8,128)(2,1)S(1)} %bitcast.19, bf16[864,256]{1,0:T(8,128)(2,1)S(1)} %bitcast.17, bf16[16,256]{1,0:T(8,128)(2,1)S(1)} %reshape.37.cot), custom_call_target="tpu_custom_call" | custom-call | bytes 1695744 | tf_op jit(solution)/shard_map/pallas_call | solution.py:29
  4.7 7.6 %all-to-all-start = ((bf16[8,576,128]{2,1,0:T(8,128)(2,1)}), bf16[8,576,128]{2,1,0:T(8,128)(2,1)S(1)}, u32[]{:S(2)}, u32[]{:S(2)}) async-start(bf16[8,576,128]{2,1,0:T(8,128)(2,1)} %shard_map.75), calls=%async_computation | async-start | bytes 2359296 | tf_op jit(solution)/shard_map/all_to_all | solution.py:352
  12.4 16.0 %all-to-all-done.got = bf16[8,576,128]{2,1,0:T(8,128)(2,1)S(1)} async-done(((bf16[8,576,128]{2,1,0:T(8,128)(2,1)}), bf16[8,576,128]{2,1,0:T(8,128)(2,1)S(1)}, u32[]{:S(2)}, u32[]{:S(2)}) %all-to-all-start) | async-done | bytes 1179680 | tf_op jit(solution)/shard_map/all_to_all | solution.py:352
  28.4 1.5 %shard_map.77 = (f32[256,128]{1,0:T(8,128)S(1)}, f32[256,128]{1,0:T(8,128)S(1)}, bf16[1024,256]{1,0:T(8,128)(2,1)S(1)}) custom-call(bf16[8,576,128]{2,1,0:T(8,128)(2,1)S(1)} %all-to-all-done.got, bf16[384,768]{1,0:T(8,128)(2,1)S(1)} %get-tuple-element.20.wide), custom_call_target="tpu_custom_call" | custom-call | flops 603979776 | bytes 2555904 | tf_op jit(solution)/shard_map/pallas_call | solution.py:29
  29.9 1.3 collective-permute-start.1
  31.2 3.0 %collective-permute-start = (f32[256,128]{1,0:T(8,128)S(1)}, f32[256,128]{1,0:T(8,128)S(1)}, u32[]{:S(2)}, u32[]{:S(2)}) collective-permute-start(f32[256,128]{1,0:T(8,128)S(1)} %get-tuple-element.22.high), channel_id=1, source_target_pairs={{0,8},{8,16},{16,24},{24,32},{32,40},{40,48},{48,56},{56,64},{64,7... | collective-permute-start | bytes 393224 | tf_op jit(solution)/shard_map/ppermute | solution.py:357
  34.3 0.8 collective-permute-done.below
  35.2 0.6 shard_map.79
  35.8 14.5 %all_to_all.30.parts = bf16[8,128,256]{2,1,0:T(8,128)(2,1)S(1)} all-to-all(bf16[8,128,256]{2,1,0:T(8,128)(2,1)S(1)} %get-tuple-element.23), channel_id=1, replica_groups=mesh['sp_z'=8,'sp_y'=2,'core'=2,'flt'=8] {'flt'}, dimensions={0} | all-to-all | bytes 1048576 | tf_op jit(solution)/shard_map/all_to_all | solution.py:352
  50.5 1.2 shard_map.84
  51.7 6.0 %all-to-all-start.3 = ((bf16[8,288,128]{2,1,0:T(8,128)(2,1)}), bf16[8,288,128]{2,1,0:T(8,128)(2,1)S(1)}, u32[]{:S(2)}, u32[]{:S(2)}) async-start(bf16[8,288,128]{2,1,0:T(8,128)(2,1)} %shard_map.84), calls=%async_computation.3 | async-start | bytes 1179648 | tf_op jit(solution)/shard_map/all_to_all | solution.py:352
  57.7 1.3 collective-permute-start.3
  59.0 3.0 %collective-permute-start.2 = (bf16[128,256]{1,0:T(8,128)(2,1)S(1)}, bf16[128,256]{1,0:T(8,128)(2,1)S(1)}, u32[]{:S(2)}, u32[]{:S(2)}) collective-permute-start(bf16[128,256]{1,0:T(8,128)(2,1)S(1)} %get-tuple-element.25.own.err), channel_id=1, source_target_pairs={{0,8},{8,16},{16,24},{24,32},{32,40},{40,48},{48,56},{56,64},{64,7... | collective-permute-start | bytes 196616 | tf_op jit(solution)/shard_map/ppermute | solution.py:357
  62.1 0.9 collective-permute-done.2.below
  62.9 2.5 %shard_map.81 = (bf16[1024,1152]{1,0:T(8,128)(2,1)S(1)}, bf16[1792,128]{1,0:T(8,128)(2,1)S(1)}) custom-call(bf16[128,256]{1,0:T(8,128)(2,1)S(1)} %get-tuple-element.25.own.err, bf16[128,256]{1,0:T(8,128)(2,1)S(1)} %collective-permute-done.2.below, bf16[128,256]{1,0:T(8,128)(2,1)S(1)} %collective-permute-done.3.above, bf16[256,1152]{1,0:T(8,128)(2,1)S(1)} %shard_map.78.w2, ...), custom_call_target="tpu_custom_call" | custom-call | flops 905969664 | bytes 4390912 | tf_op jit(solution)/shard_map/pallas_call | solution.py:29
  65.4 1.4 %copy-done = bf16[1024,1152]{1,0:T(8,128)(2,1)} copy-done((bf16[1024,1152]{1,0:T(8,128)(2,1)}, bf16[1024,1152]{1,0:T(8,128)(2,1)S(1)}, u32[]{:S(2)}) %copy-start) | copy-done | bytes 2359320
  66.8 2.2 %all-to-all-done.3.second = bf16[8,288,128]{2,1,0:T(8,128)(2,1)S(1)} async-done(((bf16[8,288,128]{2,1,0:T(8,128)(2,1)}), bf16[8,288,128]{2,1,0:T(8,128)(2,1)S(1)}, u32[]{:S(2)}, u32[]{:S(2)}) %all-to-all-start.3) | async-done | bytes 589856 | tf_op jit(solution)/shard_map/all_to_all | solution.py:352
  69.5 1.9 %collective-permute-start.4 = (bf16[1792,128]{1,0:T(8,128)(2,1)S(1)}, bf16[1792,128]{1,0:T(8,128)(2,1)S(1)}, u32[]{:S(2)}, u32[]{:S(2)}) collective-permute-start(bf16[1792,128]{1,0:T(8,128)(2,1)S(1)} %get-tuple-element.33), channel_id=1, source_target_pairs={{0,8},{8,0},{1,9},{9,1},{2,10},{10,2},{3,11},{11,3},{4,12},{12,4},... | collective-permute-start | bytes 1376264 | tf_op jit(solution)/shard_map/ppermute | solution.py:366
  71.4 1.4 %collective-permute-done.4.came = bf16[1792,128]{1,0:T(8,128)(2,1)S(1)} collective-permute-done((bf16[1792,128]{1,0:T(8,128)(2,1)S(1)}, bf16[1792,128]{1,0:T(8,128)(2,1)S(1)}, u32[]{:S(2)}, u32[]{:S(2)}) %collective-permute-start.4) | collective-permute-done | bytes 458784 | tf_op jit(solution)/shard_map/ppermute | solution.py:366
  72.9 28.7 %all_to_all.31.parts = bf16[16,112,128]{2,1,0:T(8,128)(2,1)S(1)} all-to-all(bf16[16,112,128]{2,1,0:T(8,128)(2,1)S(1)} %shard_map.86), channel_id=1, replica_groups=mesh['sp_z'=8,'sp_y'=2,'core'=2,'flt'=8] {'sp_z','sp_y'}, dimensions={0} | all-to-all | bytes 917504 | tf_op jit(solution)/shard_map/all_to_all | solution.py:352
  101.6 0.8 shard_map.87
  102.5 3.6 %all-to-all-start.5 = ((bf16[16,112,128]{2,1,0:T(8,128)(2,1)}), bf16[16,112,128]{2,1,0:T(8,128)(2,1)S(1)}, u32[]{:S(2)}, u32[]{:S(2)}) async-start(bf16[16,112,128]{2,1,0:T(8,128)(2,1)} %shard_map.87), calls=%async_computation.5 | async-start | bytes 917504 | tf_op jit(solution)/shard_map/all_to_all | solution.py:352
  106.1 1.6 %shard_map.82 = bf16[8,128,256]{2,1,0:T(8,128)(2,1)} custom-call(bf16[1024,1152]{1,0:T(8,128)(2,1)S(1)} %copy-done.1, bf16[1152,256]{1,0:T(8,128)(2,1)S(1)} %get-tuple-element.29.tall), custom_call_target="tpu_custom_call" | custom-call | flops 603979776 | bytes 3473408 | tf_op jit(solution)/shard_map/pallas_call | solution.py:29
  107.7 13.4 %all-to-all-done.5 = bf16[16,112,128]{2,1,0:T(8,128)(2,1)S(1)} async-done(((bf16[16,112,128]{2,1,0:T(8,128)(2,1)}), bf16[16,112,128]{2,1,0:T(8,128)(2,1)S(1)}, u32[]{:S(2)}, u32[]{:S(2)}) %all-to-all-start.5) | async-done | bytes 458784 | tf_op jit(solution)/shard_map/all_to_all | solution.py:352
  121.1 7.2 %all-to-all-start.2 = ((bf16[8,128,256]{2,1,0:T(8,128)(2,1)}), bf16[8,128,256]{2,1,0:T(8,128)(2,1)S(1)}, u32[]{:S(2)}, u32[]{:S(2)}) async-start(bf16[8,128,256]{2,1,0:T(8,128)(2,1)} %shard_map.82), calls=%async_computation.2 | async-start | bytes 1048576 | tf_op jit(solution)/shard_map/all_to_all | solution.py:352
  128.3 0.6 reshape.39
  128.9 7.6 %all-to-all-done.2.parts = bf16[8,128,256]{2,1,0:T(8,128)(2,1)S(1)} async-done(((bf16[8,128,256]{2,1,0:T(8,128)(2,1)}), bf16[8,128,256]{2,1,0:T(8,128)(2,1)S(1)}, u32[]{:S(2)}, u32[]{:S(2)}) %all-to-all-start.2) | async-done | bytes 524320 | tf_op jit(solution)/shard_map/all_to_all | solution.py:352
  136.5 0.7 shard_map.83
  137.2 1.4 shard_map.88
  (21 shorter events, 0.9 us)
Async XLA Ops:
  1.3 1.0 copy-start.2
  2.4 0.8 copy-start.4
  4.7 7.6 %copy-start.3 = (bf16[32,3,3,3,256]{4,0,3,2,1:T(8,128)(2,1)S(1)}, bf16[32,3,3,3,256]{4,0,3,2,1:T(8,128)(2,1)}, u32[]{:S(2)}) copy-start(bf16[32,3,3,3,256]{4,0,3,2,1:T(8,128)(2,1)} %param.5) | copy-start | bytes 1327108
  4.7 23.7 %all-to-all-start = ((bf16[8,576,128]{2,1,0:T(8,128)(2,1)}), bf16[8,576,128]{2,1,0:T(8,128)(2,1)S(1)}, u32[]{:S(2)}, u32[]{:S(2)}) async-start(bf16[8,576,128]{2,1,0:T(8,128)(2,1)} %shard_map.75), calls=%async_computation | async-start | bytes 2359296 | tf_op jit(solution)/shard_map/all_to_all | solution.py:352
  29.9 5.9 %copy-start.5 = (bf16[1024,256]{1,0:T(8,128)(2,1)}, bf16[1024,256]{1,0:T(8,128)(2,1)S(1)}, u32[]{:S(2)}) copy-start(bf16[1024,256]{1,0:T(8,128)(2,1)S(1)} %get-tuple-element.27.field) | copy-start | bytes 1572868
  29.9 4.5 %collective-permute-start.1 = (f32[256,128]{1,0:T(8,128)S(1)}, f32[256,128]{1,0:T(8,128)S(1)}, u32[]{:S(2)}, u32[]{:S(2)}) collective-permute-start(f32[256,128]{1,0:T(8,128)S(1)} %get-tuple-element.21.low), channel_id=1, source_target_pairs={{8,0},{16,8},{24,16},{32,24},{40,32},{48,40},{56,48},{64,56},{72,6... | collective-permute-start | bytes 393224 | tf_op jit(solution)/shard_map/ppermute | solution.py:362
  31.2 4.0 %collective-permute-start = (f32[256,128]{1,0:T(8,128)S(1)}, f32[256,128]{1,0:T(8,128)S(1)}, u32[]{:S(2)}, u32[]{:S(2)}) collective-permute-start(f32[256,128]{1,0:T(8,128)S(1)} %get-tuple-element.22.high), channel_id=1, source_target_pairs={{0,8},{8,16},{16,24},{24,32},{32,40},{40,48},{48,56},{56,64},{64,7... | collective-permute-start | bytes 393224 | tf_op jit(solution)/shard_map/ppermute | solution.py:357
  50.5 12.5 %copy-start.6 = (bf16[1024,256]{1,0:T(8,128)(2,1)S(1)}, bf16[1024,256]{1,0:T(8,128)(2,1)}, u32[]{:S(2)}) copy-start(bf16[1024,256]{1,0:T(8,128)(2,1)} %copy-done.5) | copy-start | bytes 1572868
  51.7 17.3 %all-to-all-start.3 = ((bf16[8,288,128]{2,1,0:T(8,128)(2,1)}), bf16[8,288,128]{2,1,0:T(8,128)(2,1)S(1)}, u32[]{:S(2)}, u32[]{:S(2)}) async-start(bf16[8,288,128]{2,1,0:T(8,128)(2,1)} %shard_map.84), calls=%async_computation.3 | async-start | bytes 1179648 | tf_op jit(solution)/shard_map/all_to_all | solution.py:352
  57.7 4.3 %collective-permute-start.3 = (bf16[128,256]{1,0:T(8,128)(2,1)S(1)}, bf16[128,256]{1,0:T(8,128)(2,1)S(1)}, u32[]{:S(2)}, u32[]{:S(2)}) collective-permute-start(bf16[128,256]{1,0:T(8,128)(2,1)S(1)} %get-tuple-element.25.own.err), channel_id=1, source_target_pairs={{8,0},{16,8},{24,16},{32,24},{40,32},{48,40},{56,48},{64,56},{72,6... | collective-permute-start | bytes 196616 | tf_op jit(solution)/shard_map/ppermute | solution.py:362
  59.0 3.9 %collective-permute-start.2 = (bf16[128,256]{1,0:T(8,128)(2,1)S(1)}, bf16[128,256]{1,0:T(8,128)(2,1)S(1)}, u32[]{:S(2)}, u32[]{:S(2)}) collective-permute-start(bf16[128,256]{1,0:T(8,128)(2,1)S(1)} %get-tuple-element.25.own.err), channel_id=1, source_target_pairs={{0,8},{8,16},{16,24},{24,32},{32,40},{40,48},{48,56},{56,64},{64,7... | collective-permute-start | bytes 196616 | tf_op jit(solution)/shard_map/ppermute | solution.py:357
  65.4 1.4 %copy-start = (bf16[1024,1152]{1,0:T(8,128)(2,1)}, bf16[1024,1152]{1,0:T(8,128)(2,1)S(1)}, u32[]{:S(2)}) copy-start(bf16[1024,1152]{1,0:T(8,128)(2,1)S(1)} %get-tuple-element.28.window) | copy-start | bytes 7077892
  69.5 3.3 %collective-permute-start.4 = (bf16[1792,128]{1,0:T(8,128)(2,1)S(1)}, bf16[1792,128]{1,0:T(8,128)(2,1)S(1)}, u32[]{:S(2)}, u32[]{:S(2)}) collective-permute-start(bf16[1792,128]{1,0:T(8,128)(2,1)S(1)} %get-tuple-element.33), channel_id=1, source_target_pairs={{0,8},{8,0},{1,9},{9,1},{2,10},{10,2},{3,11},{11,3},{4,12},{12,4},... | collective-permute-start | bytes 1376264 | tf_op jit(solution)/shard_map/ppermute | solution.py:366
  72.9 33.1 %copy-start.1 = (bf16[1024,1152]{1,0:T(8,128)(2,1)S(1)}, bf16[1024,1152]{1,0:T(8,128)(2,1)}, u32[]{:S(2)}) copy-start(bf16[1024,1152]{1,0:T(8,128)(2,1)} %copy-done) | copy-start | bytes 7077892
  102.5 18.6 %all-to-all-start.5 = ((bf16[16,112,128]{2,1,0:T(8,128)(2,1)}), bf16[16,112,128]{2,1,0:T(8,128)(2,1)S(1)}, u32[]{:S(2)}, u32[]{:S(2)}) async-start(bf16[16,112,128]{2,1,0:T(8,128)(2,1)} %shard_map.87), calls=%async_computation.5 | async-start | bytes 917504 | tf_op jit(solution)/shard_map/all_to_all | solution.py:352
  121.1 15.4 %all-to-all-start.2 = ((bf16[8,128,256]{2,1,0:T(8,128)(2,1)}), bf16[8,128,256]{2,1,0:T(8,128)(2,1)S(1)}, u32[]{:S(2)}, u32[]{:S(2)}) async-start(bf16[8,128,256]{2,1,0:T(8,128)(2,1)} %shard_map.82), calls=%async_computation.2 | async-start | bytes 1048576 | tf_op jit(solution)/shard_map/all_to_all | solution.py:352
  128.3 8.9 %collective-permute-start.5 = (bf16[1792,128]{1,0:T(8,128)(2,1)S(1)}, bf16[1792,128]{1,0:T(8,128)(2,1)S(1)}, u32[]{:S(2)}, u32[]{:S(2)}) collective-permute-start(bf16[1792,128]{1,0:T(8,128)(2,1)S(1)} %bitcast.15), channel_id=1, source_target_pairs={{0,8},{8,0},{1,9},{9,1},{2,10},{10,2},{3,11},{11,3},{4,12},{12,4},... | collective-permute-start | bytes 1376264 | tf_op jit(solution)/shard_map/ppermute | solution.py:366
where the time goes:
time: 139 us
  blocking collectives  43.2 us (31%)
  waiting for transfers between devices  42.3 us (30%)
  starting transfers between devices  35 us (25%)
  Pallas kernels  12.7 us (9%)
  local copies, waits for them, and re-layouts  4.63 us (3%)
    all_to_all x2, blocking collectives, exchange(): return lax.all_to_all(v, axis, 0, 0, tiled=True)  43.2 us
    all_to_all x4, waiting for transfers between devices, exchange(): return lax.all_to_all(v, axis, 0, 0, tiled=True)  39.1 us
    all_to_all x4, starting transfers between devices, exchange(): return lax.all_to_all(v, axis, 0, 0, tiled=True)  24.4 us
    pallas_call x14, Pallas kernels, kernel_call(): pl.pallas_call(body, out_shape=outs, in_specs=[vmem] * len(args), out_spe...  12.7 us
    ppermute x2, starting transfers between devices, upward(): return lax.ppermute(v, SP, [(i, i + 1) for i in range(n - 1)])  6.07 us
    unnamed x14, local copies, waits for them, and re-layouts  3.3 us
  transfers between devices with their start and end apart: 10, of which 7 were waited for; matrix products, arithmetic and copies ran while one was open for 0% of the time, Pallas kernels for 4%

commit v1 on v0

--- a/solution.py
+++ b/solution.py
@@ -8,6 +8,7 @@
 
 SP = ("sp_z", "sp_y", "core")
 CHIPS = ("sp_z", "sp_y")
+FLT = ("flt_x", "flt_y")
 bf16, f32 = jnp.bfloat16, jnp.float32
 
 ROWS = 256
@@ -23,16 +24,16 @@
     return lax.dot_general(a, b, dims, preferred_element_type=f32)
 
 
-def kernel_call(body, outs, flops, *args, scratch=()):
+def kernel_call(body, outs, flops, *args, scratch=(), space=pltpu.VMEM, limit=16):
     vmem = pl.BlockSpec(memory_space=pltpu.VMEM)
     moved = sum(a.size * a.dtype.itemsize for a in (*args, *outs))
     return pl.pallas_call(
         body,
         out_shape=outs,
-        in_specs=[vmem] * len(args),
+        in_specs=[pl.BlockSpec(memory_space=space)] * len(args),
         out_specs=[vmem] * len(outs),
         scratch_shapes=scratch,
-        compiler_params=pltpu.CompilerParams(vmem_limit_bytes=32 << 20),
+        compiler_params=pltpu.CompilerParams(vmem_limit_bytes=limit << 20),
         cost_estimate=pl.CostEstimate(flops=flops, bytes_accessed=moved, transcendentals=0),
     )(*args)
 
@@ -98,12 +99,22 @@
     return s * (1.0 + v * (1.0 - s))
 
 
-def pack_inputs(x, w, cot, out):
+def pack_inputs(x_far, w_far, cot_far, out, x, w, cot_near, sems):
+    copies = [
+        pltpu.make_async_copy(far, near, sems.at[i])
+        for i, (far, near) in enumerate(((x_far, x), (cot_far, cot_near), (w_far, w)))
+    ]
+    for copy in copies:
+        copy.start()
+    copies[0].wait()
+    copies[1].wait()
+    cot = jnp.concatenate([cot_near[0, i].astype(f32) for i in range(4)], 0).astype(bf16)
     for f in range(8):
         for h in (0, 1):
             out[f, h * 128 : h * 128 + 128, :] = x[:, h * 128 : h * 128 + 128]
             at = X_ROWS + h * 16
             out[f, at : at + 16, :] = cot[:, h * 128 : h * 128 + 128]
+    copies[2].wait()
     for k in range(9):
         for h in (0, 1):
             taps = [
@@ -128,7 +139,7 @@
                 tall[row : row + 32, :] = v
 
 
-def first_conv(got, wide, low, high, field, window):
+def first_conv(got, wide, low, high, within, across, field, window):
     parts = {}
     for h in (0, 1):
         for p in (0, 1):
@@ -162,8 +173,12 @@
             ]
             v = terms[0] if len(terms) == 1 else terms[0] + terms[1]
             pieces.append(tap_sum(before(v), v, after(v)))
-    low[...] = pair_of(pieces[:4])
-    high[...] = pair_of(pieces[4:])
+    a, b = pair_of(pieces[:4]), pair_of(pieces[4:])
+    first_core = lax.axis_index("core") == 0
+    low[...] = a
+    high[...] = b
+    within[...] = jnp.where(first_core, b, a)
+    across[...] = jnp.where(first_core, a, b)
 
 
 def gather_second(got, w2):
@@ -181,11 +196,21 @@
     return jnp.where(jnp.logical_and(at_first_plane(), lanes(ROWS) < 64), 0.0, v)
 
 
-def second_conv(low, high, below, above, w2, pre, window, out, full):
-    pairs = [low[...] + below[...], high[...] + above[...]]
+def below_above(within, across):
+    first_core = lax.axis_index("core") == 0
+    a, b = within[...], across[...]
+    return jnp.where(first_core, b, a), jnp.where(first_core, a, b)
+
+
+def second_conv(low, high, within, across, w2, pre, out, window, full):
+    below, above = below_above(within, across)
+    pairs = [low[...] + below, high[...] + above]
     pre[0:ROWS, :] = pairs[0]
     pre[ROWS:, :] = pairs[1]
     hidden = [v * sigmoid(v) for v in pairs]
+    own = jnp.where(lanes(ROWS) < 64, rotated(hidden[0], 2), rotated(hidden[1], 2)).astype(bf16)
+    for g in range(8):
+        out[g, ROWS:, :] = own
     hidden[0] = without_edge(hidden[0])
     hidden = [v.astype(bf16).astype(f32) for v in hidden]
     shifted = [(before(v), v, after(v)) for v in hidden]
@@ -203,15 +228,27 @@
         full[h] = total[:, h * 128 : h * 128 + 128]
         v = full[h, pl.ds(0, 128, 2), :].astype(bf16)
         for g in range(8):
-            out[g, :, h * 128 : h * 128 + 128] = v
+            out[g, h * 128 : h * 128 + 128, :] = v
+
+
+def gather_hidden(parts, field):
+    lane = lanes(ROWS)
+    for h in (0, 1):
+        blocks = [parts[4 * h + m, ROWS:, :].astype(f32) for m in range(4)]
+        for slot in range(4):
+            v = rotated(blocks[0], -slot)
+            for m in (1, 2, 3):
+                v = jnp.where(lane < 32 * m, v, rotated(blocks[m], m - slot))
+            field[slot * ROWS : slot * ROWS + ROWS, h * 128 : h * 128 + 128] = v.astype(bf16)
 
 
 def second_error(parts, got, section, err):
     for h in (0, 1):
         lane = slice(h * 128, h * 128 + 128)
-        v = parts[0, :, lane].astype(f32)
+        row = slice(h * 128, h * 128 + 128)
+        v = parts[0, row, :].astype(f32)
         for g in range(1, 8):
-            v = v + parts[g, :, lane].astype(f32)
+            v = v + parts[g, row, :].astype(f32)
         cot = jnp.concatenate(
             [got[g, X_ROWS + h * 16 : X_ROWS + h * 16 + 16, :].astype(f32) for g in range(8)], 0
         )
@@ -220,27 +257,37 @@
 
 
 def spread_out(err, full):
-    halves = []
-    for h in (0, 1):
-        full[h] = jnp.zeros((ROWS, 128), f32)
-        full[h, pl.ds(0, 128, 2), :] = err[:, h * 128 : h * 128 + 128].astype(f32)
-        halves.append(full[h])
-    return jnp.concatenate(halves, 1)
-
-
-def second_grad(err, window, out, full):
-    spread = spread_out(err, full).astype(bf16)
-    grad = dot(spread, window[...], TN)
-    for g in range(8):
-        for k in range(9):
-            v = grad[g * 32 : g * 32 + 32, k * 128 : k * 128 + 128]
-            out[g, k * 32 : k * 32 + 32, :] = v.astype(bf16)
-
-
-def first_error(own, below, above, w2, pre, field, window, out, full):
-    spread, ahead = [], []
-    for err in (below, own, above):
-        v = spread_out(err, full)
+    full[...] = jnp.zeros((ROWS, 128), f32)
+    full[pl.ds(0, 128, 2), :] = err
+    return full[...]
+
+
+def second_grad(spread, hidden):
+    flt = lax.axis_index("flt_x") * 2 + lax.axis_index("flt_y")
+    turn = lax.rem(8 - flt, 4) * 32
+    plain, ahead = [], []
+    for left, right in spread:
+        v = pltpu.roll(jnp.where(flt < 4, left, right), turn, 1)
+        v = three(after(v), rotated(v, 1), rotated(before(v), 2))
+        plain.append(v.astype(bf16))
+        ahead.append(row_up(v).astype(bf16))
+    grads = []
+    for k0 in range(3):
+        q = 1 if k0 == 0 else 0
+        for k1 in range(3):
+            at = ((1 if k0 == 1 else 3) - (1 if k1 == 1 else 0)) * ROWS
+            errs = (ahead if k1 == 0 else plain)[q]
+            grads.append(dot(errs, hidden[at : at + ROWS, :], TN))
+    return grads
+
+
+def backward(own, within, across, w2, pre, field, hidden, window, kept, sent, full):
+    below, above = below_above(within, across)
+    spread, ahead, halves = [], [], []
+    for err in (below, own[...], above):
+        both = [spread_out(err[:, h * 128 : h * 128 + 128].astype(f32), full) for h in (0, 1)]
+        halves.append(both)
+        v = jnp.concatenate(both, 1)
         spread.append(v.astype(bf16))
         ahead.append(row_up(v).astype(bf16))
     pieces = []
@@ -276,49 +323,57 @@
                         at = (2 * (target - 1) + par) * ROWS
                         lane = (k0 * 3 + k1) * 128
                         window[at : at + ROWS, lane : lane + 128] = v
-    grad = dot(window[...], field[...], TN)
+    first = dot(window[...], field[...], TN)
+    second = second_grad(halves[1:], hidden)
+    first_core = lax.axis_index("core") == 0
     for h in (0, 1):
+        lane = slice(h * 128, h * 128 + 128)
         for k in range(9):
             at = h * 864 + k * 96
-            v = grad[k * 128 : k * 128 + 96, h * 128 : h * 128 + 128]
-            out[at : at + 96, :] = v.astype(bf16)
-    out[GRAD_ROWS:, :] = jnp.zeros((GRAD_PAD - GRAD_ROWS, 128), bf16)
-
-
-def input_grad(window, tall, out):
+            a, b = first[k * 128 : k * 128 + 96, lane], second[k][:96, lane]
+            kept[at : at + 96, :] = jnp.where(first_core, a, b)
+            sent[at : at + 96, :] = jnp.where(first_core, b, a).astype(bf16)
+    kept[GRAD_ROWS:, :] = jnp.zeros((GRAD_PAD - GRAD_ROWS, 128), f32)
+    sent[GRAD_ROWS:, :] = jnp.zeros((GRAD_PAD - GRAD_ROWS, 128), bf16)
+
+
+def input_grad(window, tall, kept, sent):
+    near = lax.axis_index("flt_y") == 0
     for p in (0, 1):
         even = dot(window[2 * p * ROWS : (2 * p + 1) * ROWS, :], tall[...], NN)
         odd = dot(window[(2 * p + 1) * ROWS : (2 * p + 2) * ROWS, :], tall[...], NN)
+        blocks = []
         for g in range(8):
             a = even[g * 32 : g * 32 + 32].reshape(4, 1, 8, 256)
             b = odd[g * 32 : g * 32 + 32].reshape(4, 1, 8, 256)
-            v = jnp.concatenate([a, b], 1).reshape(64, 256)
-            out[g, p * 64 : p * 64 + 64, :] = v.astype(bf16)
-
-
-def split_grads(first, second, kept, sent):
-    lane = lanes(32)
-    core = lax.axis_index("core")
-
-    def store(at, size, a, b):
-        kept[at : at + size, :] = jnp.where(core == 0, a, b).astype(bf16)
-        sent[at : at + size, :] = jnp.where(core == 0, b, a).astype(bf16)
-
-    for h in (0, 1):
-        for k in range(9):
-            blocks = [second[4 * h + m, k * 32 : k * 32 + 32, :].astype(f32) for m in range(4)]
-            for t in range(3):
-                v = rotated(blocks[0], -t)
-                for m in (1, 2, 3):
-                    v = jnp.where(lane < 32 * m, v, rotated(blocks[m], m - t))
-                at = h * 864 + (3 * k + t) * 32
-                store(at, 32, first[at : at + 32, :].astype(f32), v)
-    kept[GRAD_ROWS:, :] = jnp.zeros((GRAD_PAD - GRAD_ROWS, 128), bf16)
-    sent[GRAD_ROWS:, :] = jnp.zeros((GRAD_PAD - GRAD_ROWS, 128), bf16)
+            blocks.append(jnp.concatenate([a, b], 1).reshape(64, 256))
+        row = slice(p * 64, p * 64 + 64)
+        for x in range(4):
+            a, b = blocks[2 * x], blocks[2 * x + 1]
+            kept[x, row, :] = jnp.where(near, a, b)
+            sent[x, row, :] = jnp.where(near, b, a).astype(bf16)
+
+
+def add_second_axis(kept, came, still, sent):
+    x = lax.axis_index("flt_x")
+    still[0] = kept[x] + came[x].astype(f32)
+    still[1] = kept[3 - x] + came[3 - x].astype(f32)
+    next_to = x + 1 - 2 * lax.rem(x, 2)
+    sent[0] = (kept[next_to] + came[next_to].astype(f32)).astype(bf16)
+    sent[1] = (kept[3 - next_to] + came[3 - next_to].astype(f32)).astype(bf16)
+
+
+def add_pairs(kept, came, still, sent):
+    still[...] = kept[0] + came[0].astype(f32)
+    sent[...] = (kept[1] + came[1].astype(f32)).astype(bf16)
+
+
+def add_last(kept, came, out):
+    out[...] = kept[...] + came[...].astype(f32)
 
 
 def add_core(kept, came, out):
-    v = kept[...].astype(f32) + came[...].astype(f32)
+    v = kept[...] + came[...].astype(f32)
     out[...] = v.astype(bf16).reshape(16, GRAD_PAD // 16, 128)
 
 
@@ -341,29 +396,23 @@
         second[:, lane] = jnp.where(core == 0, b, a)
 
 
-def add_parts(parts, out):
-    v = parts[0].astype(f32)
-    for g in range(1, 8):
-        v = v + parts[g].astype(f32)
-    out[...] = v
-
-
 def exchange(v, axis):
     return lax.all_to_all(v, axis, 0, 0, tiled=True)
 
 
-def upward(v):
-    n = lax.axis_size(SP)
-    return lax.ppermute(v, SP, [(i, i + 1) for i in range(n - 1)])
-
-
-def downward(v):
-    n = lax.axis_size(SP)
-    return lax.ppermute(v, SP, [(i + 1, i) for i in range(n - 1)])
-
-
-def swapped(v):
-    return lax.ppermute(v, "core", [(0, 1), (1, 0)])
+def swapped(v, axis="core"):
+    n = lax.axis_size(axis)
+    return lax.ppermute(v, axis, [(i, i ^ 1) for i in range(n)])
+
+
+def mirrored(v, axis):
+    n = lax.axis_size(axis)
+    return lax.ppermute(v, axis, [(i, n - 1 - i) for i in range(n)])
+
+
+def next_chip(v):
+    pairs = [(i, i + 1) for i in range(1, lax.axis_size(SP) - 1, 2)]
+    return lax.ppermute(v, SP, pairs + [(b, a) for a, b in pairs])
 
 
 def as_rows(w):
@@ -375,7 +424,6 @@
 
 
 def per_device(activations, w_first, w_second, cotangent):
-    spread_scratch = [pltpu.VMEM((2, ROWS, 128), f32)]
     wide, tall = kernel_call(
         prepare_first, [shape((384, 768), bf16), shape((1152, 256), bf16)], 0, as_rows(w_first)
     )
@@ -385,81 +433,99 @@
         0,
         activations.reshape(128, 256),
         as_rows(w_second),
-        cotangent.reshape(16, 256),
-    )
-    got = exchange(packed, "flt")
-    low, high, field = kernel_call(
+        cotangent,
+        scratch=[
+            pltpu.VMEM((128, 256), bf16),
+            pltpu.VMEM((864, 256), bf16),
+            pltpu.VMEM((1, 4, 4, 256), bf16),
+            pltpu.SemaphoreType.DMA((3,)),
+        ],
+        space=pltpu.HBM,
+        limit=60,
+    )
+    got = exchange(packed, FLT)
+    pair = shape((ROWS, 128), f32)
+    low, high, within, across, field = kernel_call(
         first_conv,
-        [shape((ROWS, 128), f32), shape((ROWS, 128), f32), shape((1024, 256), bf16)],
+        [pair, pair, pair, pair, shape((1024, 256), bf16)],
         2 * 1024 * 768 * 384,
         got,
         wide,
         scratch=[pltpu.VMEM((1024, 768), bf16)],
     )
-    below, above = upward(high), downward(low)
+    across, within = next_chip(across), swapped(within)
     (w2,) = kernel_call(gather_second, [shape((256, 1152), bf16)], 0, got)
-    pre, hidden_window, partial = kernel_call(
+    pre, partial = kernel_call(
         second_conv,
-        [shape((512, 128), f32), shape((ROWS, 1152), bf16), shape((8, 128, 256), bf16)],
+        [shape((512, 128), f32), shape((8, 512, 128), bf16)],
         2 * 256 * 1152 * 256,
         low,
         high,
-        below,
-        above,
+        within,
+        across,
         w2,
-        scratch=spread_scratch,
-    )
-    parts = exchange(partial, "flt")
+        scratch=[pltpu.VMEM((ROWS, 1152), bf16), pltpu.VMEM((2, ROWS, 128), f32)],
+    )
+    parts = exchange(partial, FLT)
     section, err = kernel_call(
         second_error, [shape((128, 256), f32), shape((128, 256), bf16)], 0, parts, got
     )
-    err_below, err_above = upward(err), downward(err)
-    (grad_second,) = kernel_call(
-        second_grad,
-        [shape((8, 288, 128), bf16)],
-        2 * 256 * 1152 * 256,
-        err,
-        hidden_window,
-        scratch=spread_scratch,
-    )
-    grad_second = exchange(grad_second, "flt")
-    window, grad_first = kernel_call(
-        first_error,
-        [shape((1024, 1152), bf16), shape((GRAD_PAD, 128), bf16)],
+    across, within = next_chip(err), swapped(err)
+    (hidden,) = kernel_call(gather_hidden, [shape((1024, 256), bf16)], 0, parts)
+    window, kept, sent = kernel_call(
+        backward,
+        [shape((1024, 1152), bf16), shape((GRAD_PAD, 128), f32), shape((GRAD_PAD, 128), bf16)],
         2 * 1024 * 1152 * 256 + 2 * 256 * 256 * 384 * 6,
         err,
-        err_below,
-        err_above,
+        within,
+        across,
         w2,
         pre,
         field,
-        scratch=spread_scratch,
-    )
-    kept, sent = kernel_call(
-        split_grads, [shape((GRAD_PAD, 128), bf16)] * 2, 0, grad_first, grad_second
+        hidden,
+        scratch=[pltpu.VMEM((ROWS, 128), f32)],
     )
     came = swapped(sent)
-    (inner,) = kernel_call(
-        input_grad, [shape((8, 128, 256), bf16)], 2 * 1024 * 1152 * 256, window, tall
+    kept_in, sent_in = kernel_call(
+        input_grad,
+        [shape((4, 128, 256), f32), shape((4, 128, 256), bf16)],
+        2 * 1024 * 1152 * 256,
+        window,
+        tall,
     )
     chunk = shape((16, GRAD_PAD // 16, 128), bf16)
     (mine,) = kernel_call(add_core, [chunk], 0, kept, came)
+    mine, sent_in = lax.optimization_barrier((mine, sent_in))
+    came_in = swapped(sent_in, "flt_y")
     (mine,) = kernel_call(add_chips, [chunk], 0, exchange(mine, CHIPS))
-    inner = exchange(inner, "flt")
+    kept_in, sent_in = kernel_call(
+        add_second_axis,
+        [shape((2, 128, 256), f32), shape((2, 128, 256), bf16)],
+        0,
+        kept_in,
+        came_in,
+    )
+    mine, sent_in = lax.optimization_barrier((mine, sent_in))
+    came_in = swapped(sent_in, "flt_x")
     mine = exchange(mine, CHIPS).reshape(GRAD_PAD, 128)
+    kept_in, sent_in = kernel_call(
+        add_pairs, [shape((128, 256), f32), shape((128, 256), bf16)], 0, kept_in, came_in
+    )
+    came_in = mirrored(sent_in, "flt_x")
+    (grad_input,) = kernel_call(add_last, [shape((128, 256), f32)], 0, kept_in, came_in)
+    mine, grad_input = lax.optimization_barrier((mine, grad_input))
     grads = kernel_call(
         finish_grads, [shape((864, 256), f32)] * 2, 0, mine, swapped(mine)
     )
-    (grad_input,) = kernel_call(add_parts, [shape((128, 256), f32)], 0, inner)
-    row = lax.axis_index("flt") * 16
+    row = lax.axis_index(FLT) * 16
     section_out = lax.dynamic_slice_in_dim(section, row, 16, 0).reshape(1, 4, 4, 256)
     return (section_out, grad_input.reshape(2, 8, 8, 256), *(as_filters(g) for g in grads))
 
 
 def solution(mesh):
-    torus = Mesh(mesh.devices.reshape(8, 2, 2, mesh.shape["flt"]), (*SP, "flt"))
-    whole = P("flt", None, None, None, None)
-    rows = P(SP, "flt", None, None)
+    torus = Mesh(mesh.devices.reshape(8, 2, 2, 4, 2), (*SP, *FLT))
+    whole = P(FLT, None, None, None, None)
+    rows = P(SP, FLT, None, None)
     return jax.shard_map(
         per_device,
         mesh=torus,

time: 139 us -> 122 us (0.88)
  the two profiles are of different devices: /device:TPU:2 before, /device:TPU:1 now
where the time goes in v1:
time: 122 us
  waiting for transfers between devices  49.1 us (40%)
  starting transfers between devices  41.9 us (34%)
  blocking collectives  15.9 us (13%)
  Pallas kernels  13.4 us (11%)
    all_to_all x3, waiting for transfers between devices, exchange(): return lax.all_to_all(v, axis, 0, 0, tiled=True)  25.8 us
    all_to_all x3, starting transfers between devices, exchange(): return lax.all_to_all(v, axis, 0, 0, tiled=True)  24.4 us
    all_to_all x1, blocking collectives, exchange(): return lax.all_to_all(v, axis, 0, 0, tiled=True)  15.9 us
    ppermute x6, waiting for transfers between devices, swapped(): return lax.ppermute(v, axis, [(i, i ^ 1) for i in range(n)])  14.3 us
    pallas_call x15, Pallas kernels, kernel_call(): pl.pallas_call(body, out_shape=outs, in_specs=[pl.BlockSpec(memory_space=...  13.4 us
    ppermute x2, starting transfers between devices, next_chip(): return lax.ppermute(v, SP, pairs + [(b, a) for a, b in pairs])  9.81 us
    ppermute x6, starting transfers between devices, swapped(): return lax.ppermute(v, axis, [(i, i ^ 1) for i in range(n)])  6.75 us
    ppermute x2, waiting for transfers between devices, next_chip(): return lax.ppermute(v, SP, pairs + [(b, a) for a, b in pairs])  5.27 us
  transfers between devices with their start and end apart: 12, of which 10 were waited for; matrix products, arithmetic and copies ran while one was open for 1% of the time, Pallas kernels for 2%

profile of v1, /device:TPU:1, one launch (start us, length us, event | category | flops | bytes accessed | tf_op | source)
XLA Modules:
  0.0 121.8 jit_solution(12420720586028117905)
XLA Ops:
  0.6 2.5 %shard_map.75 = bf16[8,576,128]{2,1,0:T(8,128)(2,1)} custom-call(bf16[128,256]{1,0:T(8,128)(2,1)} %bitcast.20, bf16[864,256]{1,0:T(8,128)(2,1)} %bitcast.18, bf16[1,4,4,256]{3,2,1,0:T(4,128)(2,1)} %cot_far.1), custom_call_target="tpu_custom_call" | custom-call | bytes 1695744 | tf_op jit(solution)/shard_map/pallas_call | solution.py:30
  3.2 7.6 %all-to-all-start = ((bf16[8,576,128]{2,1,0:T(8,128)(2,1)}), bf16[8,576,128]{2,1,0:T(8,128)(2,1)S(1)}, u32[]{:S(2)}, u32[]{:S(2)}) async-start(bf16[8,576,128]{2,1,0:T(8,128)(2,1)} %shard_map.75), calls=%async_computation | async-start | bytes 2359296 | tf_op jit(solution)/shard_map/all_to_all | solution.py:400
  10.9 17.1 %all-to-all-done.got = bf16[8,576,128]{2,1,0:T(8,128)(2,1)S(1)} async-done(((bf16[8,576,128]{2,1,0:T(8,128)(2,1)}), bf16[8,576,128]{2,1,0:T(8,128)(2,1)S(1)}, u32[]{:S(2)}, u32[]{:S(2)}) %all-to-all-start) | async-done | bytes 1179680 | tf_op jit(solution)/shard_map/all_to_all | solution.py:400
  28.0 1.5 %shard_map.77 = (f32[256,128]{1,0:T(8,128)S(1)}, f32[256,128]{1,0:T(8,128)S(1)}, f32[256,128]{1,0:T(8,128)S(1)}, f32[256,128]{1,0:T(8,128)S(1)}, bf16[1024,256]{1,0:T(8,128)(2,1)S(1)}) custom-call(bf16[8,576,128]{2,1,0:T(8,128)(2,1)S(1)} %all-to-all-done.got, bf16[384,768]{1,0:T(8,128)(2,1)S(1)} %get-tuple-element.32.wide), custom_call_target="tpu_custom_call" | custom-call | flops 603979776 | bytes 2818048 | tf_op jit(solution)/shard_map/pallas_call | solution.py:30
  29.5 1.7 %collective-permute-start = (f32[256,128]{1,0:T(8,128)S(1)}, f32[256,128]{1,0:T(8,128)S(1)}, u32[]{:S(2)}, u32[]{:S(2)}) collective-permute-start(f32[256,128]{1,0:T(8,128)S(1)} %get-tuple-element.35), channel_id=1, source_target_pairs={{0,8},{8,0},{1,9},{9,1},{2,10},{10,2},{3,11},{11,3},{4,12},{12,4},... | collective-permute-start | bytes 393224 | tf_op jit(solution)/shard_map/ppermute | solution.py:405
  31.2 2.2 %collective-permute-start.1 = (f32[256,128]{1,0:T(8,128)S(1)}, f32[256,128]{1,0:T(8,128)S(1)}, u32[]{:S(2)}, u32[]{:S(2)}) collective-permute-start(f32[256,128]{1,0:T(8,128)S(1)} %get-tuple-element.36), channel_id=1, source_target_pairs={{8,16},{24,32},{40,48},{56,64},{72,80},{88,96},{104,112},{120,128}... | collective-permute-start | bytes 393224 | tf_op jit(solution)/shard_map/ppermute | solution.py:415
  33.6 3.9 %collective-permute-done.1.across = f32[256,128]{1,0:T(8,128)S(1)} collective-permute-done((f32[256,128]{1,0:T(8,128)S(1)}, f32[256,128]{1,0:T(8,128)S(1)}, u32[]{:S(2)}, u32[]{:S(2)}) %collective-permute-start.1) | collective-permute-done | bytes 131104 | tf_op jit(solution)/shard_map/ppermute | solution.py:415
  37.5 0.6 shard_map.79
  38.2 15.9 %all_to_all.20.parts = bf16[8,512,128]{2,1,0:T(8,128)(2,1)S(1)} all-to-all(bf16[8,512,128]{2,1,0:T(8,128)(2,1)S(1)} %get-tuple-element.37), channel_id=1, replica_groups=mesh['sp_z'=8,'sp_y'=2,'core'=2,'flt_x'=4,'flt_y'=2] {'flt_x','flt_y'}, dimensions={0} | all-to-all | bytes 2097152 | tf_op jit(solution)/shard_map/all_to_all | solution.py:400
  54.2 7.6 %collective-permute-start.3 = (bf16[128,256]{1,0:T(8,128)(2,1)S(1)}, bf16[128,256]{1,0:T(8,128)(2,1)S(1)}, u32[]{:S(2)}, u32[]{:S(2)}) collective-permute-start(bf16[128,256]{1,0:T(8,128)(2,1)S(1)} %get-tuple-element.39.own), channel_id=1, source_target_pairs={{8,16},{24,32},{40,48},{56,64},{72,80},{88,96},{104,112},{120,128}... | collective-permute-start | bytes 196616 | tf_op jit(solution)/shard_map/ppermute | solution.py:415
  61.9 0.5 shard_map.81.hidden
  62.4 1.3 %collective-permute-done.3.across = bf16[128,256]{1,0:T(8,128)(2,1)S(1)} collective-permute-done((bf16[128,256]{1,0:T(8,128)(2,1)S(1)}, bf16[128,256]{1,0:T(8,128)(2,1)S(1)}, u32[]{:S(2)}, u32[]{:S(2)}) %collective-permute-start.3) | collective-permute-done | bytes 65568 | tf_op jit(solution)/shard_map/ppermute | solution.py:415
  63.8 3.3 %shard_map.82 = (bf16[1024,1152]{1,0:T(8,128)(2,1)S(1)}, f32[1792,128]{1,0:T(8,128)S(1)}, bf16[1792,128]{1,0:T(8,128)(2,1)S(1)}) custom-call(bf16[128,256]{1,0:T(8,128)(2,1)S(1)} %get-tuple-element.39.own, bf16[128,256]{1,0:T(8,128)(2,1)S(1)} %collective-permute-done.2.within, bf16[128,256]{1,0:T(8,128)(2,1)S(1)} %collective-permute-done.3.across, ...), custom_call_target="tpu_custom_call" | custom-call | flops 905969664 | bytes 5832704 | tf_op jit(solution)/shard_map/pallas_call | solution.py:30
  67.2 0.8 shard_map.84
  68.1 1.0 collective-permute-done.4.came
  69.0 0.8 shard_map.83
  69.9 10.9 %all-to-all-start.2 = ((bf16[16,112,128]{2,1,0:T(8,128)(2,1)}), bf16[16,112,128]{2,1,0:T(8,128)(2,1)S(1)}, u32[]{:S(2)}, u32[]{:S(2)}) async-start(bf16[16,112,128]{2,1,0:T(8,128)(2,1)} %shard_map.83), calls=%async_computation.2 | async-start | bytes 917504 | tf_op jit(solution)/shard_map/all_to_all | solution.py:400
  80.8 1.3 %collective-permute-start.5 = (bf16[4,128,256]{2,1,0:T(8,128)(2,1)S(1)}, bf16[4,128,256]{2,1,0:T(8,128)(2,1)S(1)}, u32[]{:S(2)}, u32[]{:S(2)}) collective-permute-start(bf16[4,128,256]{2,1,0:T(8,128)(2,1)S(1)} %get-tuple-element.49), channel_id=1, source_target_pairs={{0,1},{1,0},{2,3},{3,2},{4,5},{5,4},{6,7},{7,6},{8,9},{9,8},{10,11... | collective-permute-start | bytes 786440 | tf_op jit(solution)/shard_map/ppermute | solution.py:405
  82.1 8.8 %collective-permute-done.5.came = bf16[4,128,256]{2,1,0:T(8,128)(2,1)S(1)} collective-permute-done((bf16[4,128,256]{2,1,0:T(8,128)(2,1)S(1)}, bf16[4,128,256]{2,1,0:T(8,128)(2,1)S(1)}, u32[]{:S(2)}, u32[]{:S(2)}) %collective-permute-start.5) | collective-permute-done | bytes 262176 | tf_op jit(solution)/shard_map/ppermute | solution.py:405
  90.9 4.6 %all-to-all-done.2.parts = bf16[16,112,128]{2,1,0:T(8,128)(2,1)S(1)} async-done(((bf16[16,112,128]{2,1,0:T(8,128)(2,1)}), bf16[16,112,128]{2,1,0:T(8,128)(2,1)S(1)}, u32[]{:S(2)}, u32[]{:S(2)}) %all-to-all-start.2) | async-done | bytes 458784 | tf_op jit(solution)/shard_map/all_to_all | solution.py:400
  95.5 0.8 shard_map.85
  96.4 5.8 %all-to-all-start.3 = ((bf16[16,112,128]{2,1,0:T(8,128)(2,1)}), bf16[16,112,128]{2,1,0:T(8,128)(2,1)S(1)}, u32[]{:S(2)}, u32[]{:S(2)}) async-start(bf16[16,112,128]{2,1,0:T(8,128)(2,1)} %shard_map.85), calls=%async_computation.3 | async-start | bytes 917504 | tf_op jit(solution)/shard_map/all_to_all | solution.py:400
  102.2 0.1 collective-permute-start.6
  102.3 3.8 %collective-permute-done.6.came = bf16[2,128,256]{2,1,0:T(8,128)(2,1)S(1)} collective-permute-done((bf16[2,128,256]{2,1,0:T(8,128)(2,1)S(1)}, bf16[2,128,256]{2,1,0:T(8,128)(2,1)S(1)}, u32[]{:S(2)}, u32[]{:S(2)}) %collective-permute-start.6) | collective-permute-done | bytes 131104 | tf_op jit(solution)/shard_map/ppermute | solution.py:405
  106.1 1.0 collective-permute-start.7
  107.1 3.7 %collective-permute-done.7.came = bf16[128,256]{1,0:T(8,128)(2,1)S(1)} collective-permute-done((bf16[128,256]{1,0:T(8,128)(2,1)S(1)}, bf16[128,256]{1,0:T(8,128)(2,1)S(1)}, u32[]{:S(2)}, u32[]{:S(2)}) %collective-permute-start.7) | collective-permute-done | bytes 65568 | tf_op jit(solution)/shard_map/ppermute | solution.py:410
  110.8 0.7 shard_map.88
  111.5 4.0 %all-to-all-done.3 = bf16[16,112,128]{2,1,0:T(8,128)(2,1)S(1)} async-done(((bf16[16,112,128]{2,1,0:T(8,128)(2,1)}), bf16[16,112,128]{2,1,0:T(8,128)(2,1)S(1)}, u32[]{:S(2)}, u32[]{:S(2)}) %all-to-all-start.3) | async-done | bytes 458784 | tf_op jit(solution)/shard_map/all_to_all | solution.py:400
  115.5 3.5 %collective-permute-start.8 = (bf16[1792,128]{1,0:T(8,128)(2,1)S(1)}, bf16[1792,128]{1,0:T(8,128)(2,1)S(1)}, u32[]{:S(2)}, u32[]{:S(2)}) collective-permute-start(bf16[1792,128]{1,0:T(8,128)(2,1)S(1)} %bitcast.15), channel_id=1, source_target_pairs={{0,8},{8,0},{1,9},{9,1},{2,10},{10,2},{3,11},{11,3},{4,12},{12,4},... | collective-permute-start | bytes 1376264 | tf_op jit(solution)/shard_map/ppermute | solution.py:405
  119.0 0.6 reshape.35
  119.6 0.8 collective-permute-done.8.other
  120.4 1.4 %shard_map.89 = (f32[864,256]{1,0:T(8,128)}, f32[864,256]{1,0:T(8,128)}) custom-call(bf16[1792,128]{1,0:T(8,128)(2,1)S(1)} %bitcast.16, bf16[1792,128]{1,0:T(8,128)(2,1)S(1)} %collective-permute-done.8.other), custom_call_target="tpu_custom_call" | custom-call | bytes 2686976 | tf_op jit(solution)/shard_map/pallas_call | solution.py:30
  (12 shorter events, 0.6 us)
Async XLA Ops:
  3.2 7.6 %copy-start = (bf16[32,3,3,3,256]{4,0,3,2,1:T(8,128)(2,1)S(1)}, bf16[32,3,3,3,256]{4,0,3,2,1:T(8,128)(2,1)}, u32[]{:S(2)}) copy-start(bf16[32,3,3,3,256]{4,0,3,2,1:T(8,128)(2,1)} %param.5) | copy-start | bytes 1327108
  3.2 24.9 %all-to-all-start = ((bf16[8,576,128]{2,1,0:T(8,128)(2,1)}), bf16[8,576,128]{2,1,0:T(8,128)(2,1)S(1)}, u32[]{:S(2)}, u32[]{:S(2)}) async-start(bf16[8,576,128]{2,1,0:T(8,128)(2,1)} %shard_map.75), calls=%async_computation | async-start | bytes 2359296 | tf_op jit(solution)/shard_map/all_to_all | solution.py:400
  29.5 4.0 %collective-permute-start = (f32[256,128]{1,0:T(8,128)S(1)}, f32[256,128]{1,0:T(8,128)S(1)}, u32[]{:S(2)}, u32[]{:S(2)}) collective-permute-start(f32[256,128]{1,0:T(8,128)S(1)} %get-tuple-element.35), channel_id=1, source_target_pairs={{0,8},{8,0},{1,9},{9,1},{2,10},{10,2},{3,11},{11,3},{4,12},{12,4},... | collective-permute-start | bytes 393224 | tf_op jit(solution)/shard_map/ppermute | solution.py:405
  31.2 6.3 %collective-permute-start.1 = (f32[256,128]{1,0:T(8,128)S(1)}, f32[256,128]{1,0:T(8,128)S(1)}, u32[]{:S(2)}, u32[]{:S(2)}) collective-permute-start(f32[256,128]{1,0:T(8,128)S(1)} %get-tuple-element.36), channel_id=1, source_target_pairs={{8,16},{24,32},{40,48},{56,64},{72,80},{88,96},{104,112},{120,128}... | collective-permute-start | bytes 393224 | tf_op jit(solution)/shard_map/ppermute | solution.py:415
  54.2 9.6 %collective-permute-start.3 = (bf16[128,256]{1,0:T(8,128)(2,1)S(1)}, bf16[128,256]{1,0:T(8,128)(2,1)S(1)}, u32[]{:S(2)}, u32[]{:S(2)}) collective-permute-start(bf16[128,256]{1,0:T(8,128)(2,1)S(1)} %get-tuple-element.39.own), channel_id=1, source_target_pairs={{8,16},{24,32},{40,48},{56,64},{72,80},{88,96},{104,112},{120,128}... | collective-permute-start | bytes 196616 | tf_op jit(solution)/shard_map/ppermute | solution.py:415
  61.8 1.9 %collective-permute-start.2 = (bf16[128,256]{1,0:T(8,128)(2,1)S(1)}, bf16[128,256]{1,0:T(8,128)(2,1)S(1)}, u32[]{:S(2)}, u32[]{:S(2)}) collective-permute-start(bf16[128,256]{1,0:T(8,128)(2,1)S(1)} %get-tuple-element.39.own), channel_id=1, source_target_pairs={{0,8},{8,0},{1,9},{9,1},{2,10},{10,2},{3,11},{11,3},{4,12},{12,4},... | collective-permute-start | bytes 196616 | tf_op jit(solution)/shard_map/ppermute | solution.py:405
  67.1 1.9 %collective-permute-start.4 = (bf16[1792,128]{1,0:T(8,128)(2,1)S(1)}, bf16[1792,128]{1,0:T(8,128)(2,1)S(1)}, u32[]{:S(2)}, u32[]{:S(2)}) collective-permute-start(bf16[1792,128]{1,0:T(8,128)(2,1)S(1)} %get-tuple-element.43), channel_id=1, source_target_pairs={{0,8},{8,0},{1,9},{9,1},{2,10},{10,2},{3,11},{11,3},{4,12},{12,4},... | collective-permute-start | bytes 1376264 | tf_op jit(solution)/shard_map/ppermute | solution.py:405
  69.9 25.6 %all-to-all-start.2 = ((bf16[16,112,128]{2,1,0:T(8,128)(2,1)}), bf16[16,112,128]{2,1,0:T(8,128)(2,1)S(1)}, u32[]{:S(2)}, u32[]{:S(2)}) async-start(bf16[16,112,128]{2,1,0:T(8,128)(2,1)} %shard_map.83), calls=%async_computation.2 | async-start | bytes 917504 | tf_op jit(solution)/shard_map/all_to_all | solution.py:400
  80.8 10.0 %collective-permute-start.5 = (bf16[4,128,256]{2,1,0:T(8,128)(2,1)S(1)}, bf16[4,128,256]{2,1,0:T(8,128)(2,1)S(1)}, u32[]{:S(2)}, u32[]{:S(2)}) collective-permute-start(bf16[4,128,256]{2,1,0:T(8,128)(2,1)S(1)} %get-tuple-element.49), channel_id=1, source_target_pairs={{0,1},{1,0},{2,3},{3,2},{4,5},{5,4},{6,7},{7,6},{8,9},{9,8},{10,11... | collective-permute-start | bytes 786440 | tf_op jit(solution)/shard_map/ppermute | solution.py:405
  96.4 19.1 %all-to-all-start.3 = ((bf16[16,112,128]{2,1,0:T(8,128)(2,1)}), bf16[16,112,128]{2,1,0:T(8,128)(2,1)S(1)}, u32[]{:S(2)}, u32[]{:S(2)}) async-start(bf16[16,112,128]{2,1,0:T(8,128)(2,1)} %shard_map.85), calls=%async_computation.3 | async-start | bytes 917504 | tf_op jit(solution)/shard_map/all_to_all | solution.py:400
  102.2 3.9 %collective-permute-start.6 = (bf16[2,128,256]{2,1,0:T(8,128)(2,1)S(1)}, bf16[2,128,256]{2,1,0:T(8,128)(2,1)S(1)}, u32[]{:S(2)}, u32[]{:S(2)}) collective-permute-start(bf16[2,128,256]{2,1,0:T(8,128)(2,1)S(1)} %get-tuple-element.53), channel_id=1, source_target_pairs={{0,2},{2,0},{4,6},{6,4},{1,3},{3,1},{5,7},{7,5},{8,10},{10,8},{12,... | collective-permute-start | bytes 393224 | tf_op jit(solution)/shard_map/ppermute | solution.py:405
  106.1 4.7 %collective-permute-start.7 = (bf16[128,256]{1,0:T(8,128)(2,1)S(1)}, bf16[128,256]{1,0:T(8,128)(2,1)S(1)}, u32[]{:S(2)}, u32[]{:S(2)}) collective-permute-start(bf16[128,256]{1,0:T(8,128)(2,1)S(1)} %get-tuple-element.55), channel_id=1, source_target_pairs={{0,6},{2,4},{4,2},{6,0},{1,7},{3,5},{5,3},{7,1},{8,14},{10,12},{12... | collective-permute-start | bytes 196616 | tf_op jit(solution)/shard_map/ppermute | solution.py:410
  115.5 4.9 %collective-permute-start.8 = (bf16[1792,128]{1,0:T(8,128)(2,1)S(1)}, bf16[1792,128]{1,0:T(8,128)(2,1)S(1)}, u32[]{:S(2)}, u32[]{:S(2)}) collective-permute-start(bf16[1792,128]{1,0:T(8,128)(2,1)S(1)} %bitcast.15), channel_id=1, source_target_pairs={{0,8},{8,0},{1,9},{9,1},{2,10},{10,2},{3,11},{11,3},{4,12},{12,4},... | collective-permute-start | bytes 1376264 | tf_op jit(solution)/shard_map/ppermute | solution.py:405

commit v2 on v1

--- a/solution.py
+++ b/solution.py
@@ -12,7 +12,7 @@
 bf16, f32 = jnp.bfloat16, jnp.float32
 
 ROWS = 256
-X_ROWS, COT_ROWS, W_ROWS = 256, 32, 288
+X_ROWS, COT_ROWS, W_ROWS = 256, 32, 128
 PACK = X_ROWS + COT_ROWS + W_ROWS
 GRAD_ROWS, GRAD_PAD = 1728, 1792
 NT = (((1,), (1,)), ((), ()))
@@ -24,14 +24,13 @@
     return lax.dot_general(a, b, dims, preferred_element_type=f32)
 
 
-def kernel_call(body, outs, flops, *args, scratch=(), space=pltpu.VMEM, limit=16):
-    vmem = pl.BlockSpec(memory_space=pltpu.VMEM)
+def kernel_call(body, outs, flops, *args, scratch=(), space=pltpu.VMEM, target=pltpu.VMEM, limit=16):
     moved = sum(a.size * a.dtype.itemsize for a in (*args, *outs))
     return pl.pallas_call(
         body,
         out_shape=outs,
         in_specs=[pl.BlockSpec(memory_space=space)] * len(args),
-        out_specs=[vmem] * len(outs),
+        out_specs=[pl.BlockSpec(memory_space=target)] * len(outs),
         scratch_shapes=scratch,
         compiler_params=pltpu.CompilerParams(vmem_limit_bytes=limit << 20),
         cost_estimate=pl.CostEstimate(flops=flops, bytes_accessed=moved, transcendentals=0),
@@ -115,15 +114,22 @@
             at = X_ROWS + h * 16
             out[f, at : at + 16, :] = cot[:, h * 128 : h * 128 + 128]
     copies[2].wait()
-    for k in range(9):
+    first_core = lax.axis_index("core") == 0
+    lane = lanes(32)
+
+    def block(k, m, h):
+        at = pl.multiple_of(96 * k, 32)
+        taps = [w[pl.ds(at + 32 * t, 32), h * 128 : h * 128 + 128].astype(f32) for t in range(3)]
+        return three(*(rotated(taps[t], t - m) for t in range(3)))
+
+    for b in range(4):
         for h in (0, 1):
-            taps = [
-                w[(3 * k + t) * 32 : (3 * k + t) * 32 + 32, h * 128 : h * 128 + 128].astype(f32)
-                for t in range(3)
-            ]
+            extra = w[(12 + min(b, 2)) * 32 : (13 + min(b, 2)) * 32, h * 128 : h * 128 + 128]
+            extra = extra.astype(f32)
             for m in range(4):
-                v = three(*(rotated(taps[t], t - m) for t in range(3)))
-                at = X_ROWS + COT_ROWS + k * 32
+                v = block(jnp.where(first_core, b, b + 5), m, h)
+                v = jnp.where(lane < 96, v, rotated(extra, 3 - m))
+                at = X_ROWS + COT_ROWS + b * 32
                 out[4 * h + m, at : at + 32, :] = v.astype(bf16)
 
 
@@ -139,7 +145,8 @@
                 tall[row : row + 32, :] = v
 
 
-def first_conv(got, wide, low, high, within, across, field, window):
+def first_conv(got, wide, low, high, within, across, field, part, window):
+    part[...] = got[:, X_ROWS + COT_ROWS :, :]
     parts = {}
     for h in (0, 1):
         for p in (0, 1):
@@ -181,11 +188,20 @@
     across[...] = jnp.where(first_core, a, b)
 
 
-def gather_second(got, w2):
+def gather_second(own, other, w2):
+    first_core = lax.axis_index("core") == 0
     for g in range(8):
-        for k in range(9):
-            at = X_ROWS + COT_ROWS + k * 32
-            w2[g * 32 : g * 32 + 32, k * 128 : k * 128 + 128] = got[g, at : at + 32, :]
+        row = slice(g * 32, g * 32 + 32)
+        blocks = []
+        for b in range(4):
+            at = slice(b * 32, b * 32 + 32)
+            x, y = own[g, at, :].astype(f32), other[g, at, :].astype(f32)
+            early, late = jnp.where(first_core, x, y), jnp.where(first_core, y, x)
+            w2[row, b * 128 : b * 128 + 128] = early.astype(bf16)
+            w2[row, (b + 5) * 128 : (b + 6) * 128] = late.astype(bf16)
+            blocks.append(early)
+        v = three(*(rotated(blocks[t], t - 3) for t in range(3)))
+        w2[row, 512:640] = v.astype(bf16)
 
 
 def at_first_plane():
@@ -337,35 +353,32 @@
     sent[GRAD_ROWS:, :] = jnp.zeros((GRAD_PAD - GRAD_ROWS, 128), bf16)
 
 
-def input_grad(window, tall, kept, sent):
-    near = lax.axis_index("flt_y") == 0
+def input_grad(window, tall, kept, sent, blocks):
     for p in (0, 1):
         even = dot(window[2 * p * ROWS : (2 * p + 1) * ROWS, :], tall[...], NN)
         odd = dot(window[(2 * p + 1) * ROWS : (2 * p + 2) * ROWS, :], tall[...], NN)
-        blocks = []
         for g in range(8):
             a = even[g * 32 : g * 32 + 32].reshape(4, 1, 8, 256)
             b = odd[g * 32 : g * 32 + 32].reshape(4, 1, 8, 256)
-            blocks.append(jnp.concatenate([a, b], 1).reshape(64, 256))
-        row = slice(p * 64, p * 64 + 64)
-        for x in range(4):
-            a, b = blocks[2 * x], blocks[2 * x + 1]
-            kept[x, row, :] = jnp.where(near, a, b)
-            sent[x, row, :] = jnp.where(near, b, a).astype(bf16)
-
-
-def add_second_axis(kept, came, still, sent):
+            v = jnp.concatenate([a, b], 1).reshape(64, 256)
+            blocks[g // 2, g % 2, p * 64 : p * 64 + 64, :] = v
     x = lax.axis_index("flt_x")
-    still[0] = kept[x] + came[x].astype(f32)
-    still[1] = kept[3 - x] + came[3 - x].astype(f32)
-    next_to = x + 1 - 2 * lax.rem(x, 2)
-    sent[0] = (kept[next_to] + came[next_to].astype(f32)).astype(bf16)
-    sent[1] = (kept[3 - next_to] + came[3 - next_to].astype(f32)).astype(bf16)
+    partner = x + 1 - 2 * lax.rem(x, 2)
+    kept[0] = blocks[x]
+    kept[1] = blocks[3 - x]
+    sent[0] = blocks[partner].astype(bf16)
+    sent[1] = blocks[3 - partner].astype(bf16)
 
 
 def add_pairs(kept, came, still, sent):
     still[...] = kept[0] + came[0].astype(f32)
     sent[...] = (kept[1] + came[1].astype(f32)).astype(bf16)
+
+
+def add_halves(kept, came, still, sent):
+    y = lax.axis_index("flt_y")
+    still[...] = kept[y] + came[y].astype(f32)
+    sent[...] = (kept[1 - y] + came[1 - y].astype(f32)).astype(bf16)
 
 
 def add_last(kept, came, out):
@@ -386,14 +399,26 @@
         out[i] = v
 
 
-def finish_grads(own, other, first, second):
+def finish_grads(own, other, first, second, near, sems):
     core = lax.axis_index("core")
-    for h in (0, 1):
-        lane = slice(h * 128, h * 128 + 128)
-        a = own[h * 864 : h * 864 + 864, :].astype(f32)
-        b = other[h * 864 : h * 864 + 864, :].astype(f32)
-        first[:, lane] = jnp.where(core == 0, a, b)
-        second[:, lane] = jnp.where(core == 0, b, a)
+
+    for i, source in enumerate((own, other)):
+        for h in (0, 1):
+            near[i, :, h * 128 : h * 128 + 128] = source[h * 864 : h * 864 + 864, :].astype(f32)
+        for c in (0, 1):
+
+            @pl.when(core == c)
+            def _(i=i, c=c):
+                target = first if i == c else second
+                pltpu.make_async_copy(near.at[i], target, sems.at[i]).start()
+
+    for c in (0, 1):
+
+        @pl.when(core == c)
+        def _(c=c):
+            for i in (0, 1):
+                target = first if i == c else second
+                pltpu.make_async_copy(near.at[i], target, sems.at[i]).wait()
 
 
 def exchange(v, axis):
@@ -445,16 +470,16 @@
     )
     got = exchange(packed, FLT)
     pair = shape((ROWS, 128), f32)
-    low, high, within, across, field = kernel_call(
+    low, high, within, across, field, part = kernel_call(
         first_conv,
-        [pair, pair, pair, pair, shape((1024, 256), bf16)],
+        [pair, pair, pair, pair, shape((1024, 256), bf16), shape((8, W_ROWS, 128), bf16)],
         2 * 1024 * 768 * 384,
         got,
         wide,
         scratch=[pltpu.VMEM((1024, 768), bf16)],
     )
     across, within = next_chip(across), swapped(within)
-    (w2,) = kernel_call(gather_second, [shape((256, 1152), bf16)], 0, got)
+    (w2,) = kernel_call(gather_second, [shape((256, 1152), bf16)], 0, part, swapped(part))
     pre, partial = kernel_call(
         second_conv,
         [shape((512, 128), f32), shape((8, 512, 128), bf16)],
@@ -488,34 +513,37 @@
     came = swapped(sent)
     kept_in, sent_in = kernel_call(
         input_grad,
-        [shape((4, 128, 256), f32), shape((4, 128, 256), bf16)],
+        [shape((2, 2, 128, 256), f32), shape((2, 2, 128, 256), bf16)],
         2 * 1024 * 1152 * 256,
         window,
         tall,
+        scratch=[pltpu.VMEM((4, 2, 128, 256), f32)],
     )
     chunk = shape((16, GRAD_PAD // 16, 128), bf16)
     (mine,) = kernel_call(add_core, [chunk], 0, kept, came)
     mine, sent_in = lax.optimization_barrier((mine, sent_in))
-    came_in = swapped(sent_in, "flt_y")
+    came_in = swapped(sent_in, "flt_x")
     (mine,) = kernel_call(add_chips, [chunk], 0, exchange(mine, CHIPS))
     kept_in, sent_in = kernel_call(
-        add_second_axis,
-        [shape((2, 128, 256), f32), shape((2, 128, 256), bf16)],
-        0,
-        kept_in,
-        came_in,
+        add_pairs, [shape((2, 128, 256), f32), shape((2, 128, 256), bf16)], 0, kept_in, came_in
     )
     mine, sent_in = lax.optimization_barrier((mine, sent_in))
-    came_in = swapped(sent_in, "flt_x")
+    came_in = mirrored(sent_in, "flt_x")
     mine = exchange(mine, CHIPS).reshape(GRAD_PAD, 128)
     kept_in, sent_in = kernel_call(
-        add_pairs, [shape((128, 256), f32), shape((128, 256), bf16)], 0, kept_in, came_in
-    )
-    came_in = mirrored(sent_in, "flt_x")
+        add_halves, [shape((128, 256), f32), shape((128, 256), bf16)], 0, kept_in, came_in
+    )
+    came_in = swapped(sent_in, "flt_y")
     (grad_input,) = kernel_call(add_last, [shape((128, 256), f32)], 0, kept_in, came_in)
     mine, grad_input = lax.optimization_barrier((mine, grad_input))
     grads = kernel_call(
-        finish_grads, [shape((864, 256), f32)] * 2, 0, mine, swapped(mine)
+        finish_grads,
+        [shape((864, 256), f32)] * 2,
+        0,
+        mine,
+        swapped(mine),
+        scratch=[pltpu.VMEM((2, 864, 256), f32), pltpu.SemaphoreType.DMA((2,))],
+        target=pltpu.HBM,
     )
     row = lax.axis_index(FLT) * 16
     section_out = lax.dynamic_slice_in_dim(section, row, 16, 0).reshape(1, 4, 4, 256)

time: 122 us -> 117 us (0.959)
  waiting for transfers between devices: 49.1 us -> 45.3 us
  starting transfers between devices: 41.9 us -> 39.7 us
    all_to_all x3, waiting for transfers between devices: 25.8 us -> 23.5 us  [exchange(): return lax.all_to_all(v, axis, 0, 0, tiled=True)]
    all_to_all x3, starting transfers between devices: 24.4 us -> 22.3 us  [exchange(): return lax.all_to_all(v, axis, 0, 0, tiled=True)]
    ppermute x6 -> x7, waiting for transfers between devices: 14.3 us -> 12.8 us  [swapped(): return lax.ppermute(v, axis, [(i, i ^ 1) for i in range(n)])]
    ppermute x6 -> x7, starting transfers between devices: 6.75 us -> 6.17 us  [swapped(): return lax.ppermute(v, axis, [(i, i ^ 1) for i in range(n)])]
  transfers between devices with their start and end apart: 12 -> 13, of which waited for: 10 -> 10; matrix products, arithmetic and copies ran while one was open for 1% -> 1% of each run, Pallas kernels for 2% -> 2%
where the time goes in v2:
time: 117 us; the launch traced here: 116 us
  waiting for transfers between devices  45.3 us (39%)
  starting transfers between devices  39.7 us (34%)
  blocking collectives  16.7 us (14%)
  Pallas kernels  13.3 us (11%)
    all_to_all x3, waiting for transfers between devices, exchange(): return lax.all_to_all(v, axis, 0, 0, tiled=True)  23.5 us
    all_to_all x3, starting transfers between devices, exchange(): return lax.all_to_all(v, axis, 0, 0, tiled=True)  22.3 us
    all_to_all x1, blocking collectives, exchange(): return lax.all_to_all(v, axis, 0, 0, tiled=True)  16.7 us
    pallas_call x15, Pallas kernels, kernel_call(): pl.pallas_call(body, out_shape=outs, in_specs=[pl.BlockSpec(memory_space=...  13.3 us
    ppermute x7, waiting for transfers between devices, swapped(): return lax.ppermute(v, axis, [(i, i ^ 1) for i in range(n)])  12.8 us
    ppermute x2, starting transfers between devices, next_chip(): return lax.ppermute(v, SP, pairs + [(b, a) for a, b in pairs])  10.4 us
    ppermute x7, starting transfers between devices, swapped(): return lax.ppermute(v, axis, [(i, i ^ 1) for i in range(n)])  6.17 us
    ppermute x2, waiting for transfers between devices, next_chip(): return lax.ppermute(v, SP, pairs + [(b, a) for a, b in pairs])  4.8 us
  transfers between devices with their start and end apart: 13, of which 10 were waited for; matrix products, arithmetic and copies ran while one was open for 1% of the time, Pallas kernels for 2%

profile of v2, /device:TPU:1, one launch (start us, length us, event | category | flops | bytes accessed | tf_op | source)
XLA Modules:
  0.0 116.4 jit_solution(14255483906384857897)
XLA Ops:
  0.6 2.3 %shard_map.75 = bf16[8,416,128]{2,1,0:T(8,128)(2,1)} custom-call(bf16[128,256]{1,0:T(8,128)(2,1)} %bitcast.20, bf16[864,256]{1,0:T(8,128)(2,1)} %bitcast.18, bf16[1,4,4,256]{3,2,1,0:T(4,128)(2,1)} %cot_far.1), custom_call_target="tpu_custom_call" | custom-call | bytes 1368064 | tf_op jit(solution)/shard_map/pallas_call | solution.py:29
  3.0 7.5 %all-to-all-start = ((bf16[8,416,128]{2,1,0:T(8,128)(2,1)}), bf16[8,416,128]{2,1,0:T(8,128)(2,1)S(1)}, u32[]{:S(2)}, u32[]{:S(2)}) async-start(bf16[8,416,128]{2,1,0:T(8,128)(2,1)} %shard_map.75), calls=%async_computation | async-start | bytes 1703936 | tf_op jit(solution)/shard_map/all_to_all | solution.py:425
  10.6 13.6 %all-to-all-done.got = bf16[8,416,128]{2,1,0:T(8,128)(2,1)S(1)} async-done(((bf16[8,416,128]{2,1,0:T(8,128)(2,1)}), bf16[8,416,128]{2,1,0:T(8,128)(2,1)S(1)}, u32[]{:S(2)}, u32[]{:S(2)}) %all-to-all-start) | async-done | bytes 852000 | tf_op jit(solution)/shard_map/all_to_all | solution.py:425
  24.1 1.5 %shard_map.77 = (f32[256,128]{1,0:T(8,128)S(1)}, f32[256,128]{1,0:T(8,128)S(1)}, f32[256,128]{1,0:T(8,128)S(1)}, f32[256,128]{1,0:T(8,128)S(1)}, bf16[1024,256]{...) custom-call(bf16[8,416,128]{2,1,0:T(8,128)(2,1)S(1)} %all-to-all-done.got, bf16[384,768]{1,0:T(8,128)(2,1)S(1)} %get-tuple-element.33.wide), custom_call_target="tpu_custom_call" | custom-call | flops 603979776 | bytes 2752512 | tf_op jit(solution)/shard_map/pallas_call | solution.py:29
  25.6 1.3 %collective-permute-start.2 = (bf16[8,128,128]{2,1,0:T(8,128)(2,1)S(1)}, bf16[8,128,128]{2,1,0:T(8,128)(2,1)S(1)}, u32[]{:S(2)}, u32[]{:S(2)}) collective-permute-start(bf16[8,128,128]{2,1,0:T(8,128)(2,1)S(1)} %get-tuple-element.38.own), channel_id=1, source_target_pairs={{0,8},{8,0},{1,9},{9,1},{2,10},{10,2},{3,11},{11,3},{4,12},{12,4},... | collective-permute-start | bytes 786440 | tf_op jit(solution)/shard_map/ppermute | solution.py:430
  27.0 2.6 %collective-permute-start.1 = (f32[256,128]{1,0:T(8,128)S(1)}, f32[256,128]{1,0:T(8,128)S(1)}, u32[]{:S(2)}, u32[]{:S(2)}) collective-permute-start(f32[256,128]{1,0:T(8,128)S(1)} %get-tuple-element.37), channel_id=1, source_target_pairs={{8,16},{24,32},{40,48},{56,64},{72,80},{88,96},{104,112},{120,128}... | collective-permute-start | bytes 393224 | tf_op jit(solution)/shard_map/ppermute | solution.py:440
  29.6 0.2 shard_map.78.w2
  29.8 3.5 %collective-permute-done.1.across = f32[256,128]{1,0:T(8,128)S(1)} collective-permute-done((f32[256,128]{1,0:T(8,128)S(1)}, f32[256,128]{1,0:T(8,128)S(1)}, u32[]{:S(2)}, u32[]{:S(2)}) %collective-permute-start.1) | collective-permute-done | bytes 131104 | tf_op jit(solution)/shard_map/ppermute | solution.py:440
  33.3 0.6 shard_map.79
  33.9 16.7 %all_to_all.20.parts = bf16[8,512,128]{2,1,0:T(8,128)(2,1)S(1)} all-to-all(bf16[8,512,128]{2,1,0:T(8,128)(2,1)S(1)} %get-tuple-element.39), channel_id=1, replica_groups=mesh['sp_z'=8,'sp_y'=2,'core'=2,'flt_x'=4,'flt_y'=2] {'flt_x','flt_y'}, dimensions={0} | all-to-all | bytes 2097152 | tf_op jit(solution)/shard_map/all_to_all | solution.py:425
  50.8 7.8 %collective-permute-start.4 = (bf16[128,256]{1,0:T(8,128)(2,1)S(1)}, bf16[128,256]{1,0:T(8,128)(2,1)S(1)}, u32[]{:S(2)}, u32[]{:S(2)}) collective-permute-start(bf16[128,256]{1,0:T(8,128)(2,1)S(1)} %get-tuple-element.41.own), channel_id=1, source_target_pairs={{8,16},{24,32},{40,48},{56,64},{72,80},{88,96},{104,112},{120,128}... | collective-permute-start | bytes 196616 | tf_op jit(solution)/shard_map/ppermute | solution.py:440
  58.6 0.5 shard_map.81.hidden
  59.1 1.3 %collective-permute-done.4.across = bf16[128,256]{1,0:T(8,128)(2,1)S(1)} collective-permute-done((bf16[128,256]{1,0:T(8,128)(2,1)S(1)}, bf16[128,256]{1,0:T(8,128)(2,1)S(1)}, u32[]{:S(2)}, u32[]{:S(2)}) %collective-permute-start.4) | collective-permute-done | bytes 65568 | tf_op jit(solution)/shard_map/ppermute | solution.py:440
  60.5 3.3 %shard_map.82 = (bf16[1024,1152]{1,0:T(8,128)(2,1)S(1)}, f32[1792,128]{1,0:T(8,128)S(1)}, bf16[1792,128]{1,0:T(8,128)(2,1)S(1)}) custom-call(bf16[128,256]{1,0:T(8,128)(2,1)S(1)} %get-tuple-element.41.own, bf16[128,256]{1,0:T(8,128)(2,1)S(1)} %collective-permute-done.3.within, bf16[128,256]{1,0:T(8,128)(2,1)S(1)} %collective-permute-done.4.across, ...), custom_call_target="tpu_custom_call" | custom-call | flops 905969664 | bytes 5832704 | tf_op jit(solution)/shard_map/pallas_call | solution.py:29
  63.9 0.9 shard_map.84
  64.8 0.9 collective-permute-done.5.came
  65.7 0.8 shard_map.83
  66.6 10.5 %all-to-all-start.2 = ((bf16[16,112,128]{2,1,0:T(8,128)(2,1)}), bf16[16,112,128]{2,1,0:T(8,128)(2,1)S(1)}, u32[]{:S(2)}, u32[]{:S(2)}) async-start(bf16[16,112,128]{2,1,0:T(8,128)(2,1)} %shard_map.83), calls=%async_computation.2 | async-start | bytes 917504 | tf_op jit(solution)/shard_map/all_to_all | solution.py:425
  77.2 7.2 %collective-permute-done.6.came = bf16[2,2,128,256]{3,2,1,0:T(8,128)(2,1)S(1)} collective-permute-done((bf16[2,2,128,256]{3,2,1,0:T(8,128)(2,1)S(1)}, bf16[2,2,128,256]{3,2,1,0:T(8,128)(2,1)S(1)}, u32[]{:S(2)}, u32[]{:S(2)}) %collective-permute-start.6) | collective-permute-done | bytes 262176 | tf_op jit(solution)/shard_map/ppermute | solution.py:430
  84.4 7.4 %all-to-all-done.2.parts = bf16[16,112,128]{2,1,0:T(8,128)(2,1)S(1)} async-done(((bf16[16,112,128]{2,1,0:T(8,128)(2,1)}), bf16[16,112,128]{2,1,0:T(8,128)(2,1)S(1)}, u32[]{:S(2)}, u32[]{:S(2)}) %all-to-all-start.2) | async-done | bytes 458784 | tf_op jit(solution)/shard_map/all_to_all | solution.py:425
  91.8 0.8 shard_map.85
  92.6 4.3 %all-to-all-start.3 = ((bf16[16,112,128]{2,1,0:T(8,128)(2,1)}), bf16[16,112,128]{2,1,0:T(8,128)(2,1)S(1)}, u32[]{:S(2)}, u32[]{:S(2)}) async-start(bf16[16,112,128]{2,1,0:T(8,128)(2,1)} %shard_map.85), calls=%async_computation.3 | async-start | bytes 917504 | tf_op jit(solution)/shard_map/all_to_all | solution.py:425
  96.9 0.9 collective-permute-start.7
  97.8 4.2 %collective-permute-done.7.came = bf16[2,128,256]{2,1,0:T(8,128)(2,1)S(1)} collective-permute-done((bf16[2,128,256]{2,1,0:T(8,128)(2,1)S(1)}, bf16[2,128,256]{2,1,0:T(8,128)(2,1)S(1)}, u32[]{:S(2)}, u32[]{:S(2)}) %collective-permute-start.7) | collective-permute-done | bytes 131104 | tf_op jit(solution)/shard_map/ppermute | solution.py:435
  102.1 1.3 %collective-permute-start.8 = (bf16[128,256]{1,0:T(8,128)(2,1)S(1)}, bf16[128,256]{1,0:T(8,128)(2,1)S(1)}, u32[]{:S(2)}, u32[]{:S(2)}) collective-permute-start(bf16[128,256]{1,0:T(8,128)(2,1)S(1)} %get-tuple-element.57), channel_id=1, source_target_pairs={{0,1},{1,0},{2,3},{3,2},{4,5},{5,4},{6,7},{7,6},{8,9},{9,8},{10,11... | collective-permute-start | bytes 196616 | tf_op jit(solution)/shard_map/ppermute | solution.py:430
  103.4 3.9 %collective-permute-done.8.came = bf16[128,256]{1,0:T(8,128)(2,1)S(1)} collective-permute-done((bf16[128,256]{1,0:T(8,128)(2,1)S(1)}, bf16[128,256]{1,0:T(8,128)(2,1)S(1)}, u32[]{:S(2)}, u32[]{:S(2)}) %collective-permute-start.8) | collective-permute-done | bytes 65568 | tf_op jit(solution)/shard_map/ppermute | solution.py:430
  107.3 0.7 shard_map.88
  107.9 2.6 %all-to-all-done.3 = bf16[16,112,128]{2,1,0:T(8,128)(2,1)S(1)} async-done(((bf16[16,112,128]{2,1,0:T(8,128)(2,1)}), bf16[16,112,128]{2,1,0:T(8,128)(2,1)S(1)}, u32[]{:S(2)}, u32[]{:S(2)}) %all-to-all-start.3) | async-done | bytes 458784 | tf_op jit(solution)/shard_map/all_to_all | solution.py:425
  110.5 3.2 %collective-permute-start.9 = (bf16[1792,128]{1,0:T(8,128)(2,1)S(1)}, bf16[1792,128]{1,0:T(8,128)(2,1)S(1)}, u32[]{:S(2)}, u32[]{:S(2)}) collective-permute-start(bf16[1792,128]{1,0:T(8,128)(2,1)S(1)} %bitcast.15), channel_id=1, source_target_pairs={{0,8},{8,0},{1,9},{9,1},{2,10},{10,2},{3,11},{11,3},{4,12},{12,4},... | collective-permute-start | bytes 1376264 | tf_op jit(solution)/shard_map/ppermute | solution.py:430
  113.7 0.6 reshape.35
  114.3 0.8 collective-permute-done.9.other
  115.1 1.3 %shard_map.89 = (f32[864,256]{1,0:T(8,128)}, f32[864,256]{1,0:T(8,128)}) custom-call(bf16[1792,128]{1,0:T(8,128)(2,1)S(1)} %bitcast.16, bf16[1792,128]{1,0:T(8,128)(2,1)S(1)} %collective-permute-done.9.other), custom_call_target="tpu_custom_call" | custom-call | bytes 2686976 | tf_op jit(solution)/shard_map/pallas_call | solution.py:29
  (14 shorter events, 0.7 us)
Async XLA Ops:
  0.6 9.8 %copy-start = (bf16[32,3,3,3,256]{4,0,3,2,1:T(8,128)(2,1)S(1)}, bf16[32,3,3,3,256]{4,0,3,2,1:T(8,128)(2,1)}, u32[]{:S(2)}) copy-start(bf16[32,3,3,3,256]{4,0,3,2,1:T(8,128)(2,1)} %param.5) | copy-start | bytes 1327108
  3.0 21.2 %all-to-all-start = ((bf16[8,416,128]{2,1,0:T(8,128)(2,1)}), bf16[8,416,128]{2,1,0:T(8,128)(2,1)S(1)}, u32[]{:S(2)}, u32[]{:S(2)}) async-start(bf16[8,416,128]{2,1,0:T(8,128)(2,1)} %shard_map.75), calls=%async_computation | async-start | bytes 1703936 | tf_op jit(solution)/shard_map/all_to_all | solution.py:425
  25.6 4.0 %collective-permute-start.2 = (bf16[8,128,128]{2,1,0:T(8,128)(2,1)S(1)}, bf16[8,128,128]{2,1,0:T(8,128)(2,1)S(1)}, u32[]{:S(2)}, u32[]{:S(2)}) collective-permute-start(bf16[8,128,128]{2,1,0:T(8,128)(2,1)S(1)} %get-tuple-element.38.own), channel_id=1, source_target_pairs={{0,8},{8,0},{1,9},{9,1},{2,10},{10,2},{3,11},{11,3},{4,12},{12,4},... | collective-permute-start | bytes 786440 | tf_op jit(solution)/shard_map/ppermute | solution.py:430
  26.9 2.9 %collective-permute-start = (f32[256,128]{1,0:T(8,128)S(1)}, f32[256,128]{1,0:T(8,128)S(1)}, u32[]{:S(2)}, u32[]{:S(2)}) collective-permute-start(f32[256,128]{1,0:T(8,128)S(1)} %get-tuple-element.36), channel_id=1, source_target_pairs={{0,8},{8,0},{1,9},{9,1},{2,10},{10,2},{3,11},{11,3},{4,12},{12,4},... | collective-permute-start | bytes 393224 | tf_op jit(solution)/shard_map/ppermute | solution.py:430
  27.0 6.3 %collective-permute-start.1 = (f32[256,128]{1,0:T(8,128)S(1)}, f32[256,128]{1,0:T(8,128)S(1)}, u32[]{:S(2)}, u32[]{:S(2)}) collective-permute-start(f32[256,128]{1,0:T(8,128)S(1)} %get-tuple-element.37), channel_id=1, source_target_pairs={{8,16},{24,32},{40,48},{56,64},{72,80},{88,96},{104,112},{120,128}... | collective-permute-start | bytes 393224 | tf_op jit(solution)/shard_map/ppermute | solution.py:440
  50.8 9.7 %collective-permute-start.4 = (bf16[128,256]{1,0:T(8,128)(2,1)S(1)}, bf16[128,256]{1,0:T(8,128)(2,1)S(1)}, u32[]{:S(2)}, u32[]{:S(2)}) collective-permute-start(bf16[128,256]{1,0:T(8,128)(2,1)S(1)} %get-tuple-element.41.own), channel_id=1, source_target_pairs={{8,16},{24,32},{40,48},{56,64},{72,80},{88,96},{104,112},{120,128}... | collective-permute-start | bytes 196616 | tf_op jit(solution)/shard_map/ppermute | solution.py:440
  58.5 1.9 %collective-permute-start.3 = (bf16[128,256]{1,0:T(8,128)(2,1)S(1)}, bf16[128,256]{1,0:T(8,128)(2,1)S(1)}, u32[]{:S(2)}, u32[]{:S(2)}) collective-permute-start(bf16[128,256]{1,0:T(8,128)(2,1)S(1)} %get-tuple-element.41.own), channel_id=1, source_target_pairs={{0,8},{8,0},{1,9},{9,1},{2,10},{10,2},{3,11},{11,3},{4,12},{12,4},... | collective-permute-start | bytes 196616 | tf_op jit(solution)/shard_map/ppermute | solution.py:430
  63.8 1.9 %collective-permute-start.5 = (bf16[1792,128]{1,0:T(8,128)(2,1)S(1)}, bf16[1792,128]{1,0:T(8,128)(2,1)S(1)}, u32[]{:S(2)}, u32[]{:S(2)}) collective-permute-start(bf16[1792,128]{1,0:T(8,128)(2,1)S(1)} %get-tuple-element.45), channel_id=1, source_target_pairs={{0,8},{8,0},{1,9},{9,1},{2,10},{10,2},{3,11},{11,3},{4,12},{12,4},... | collective-permute-start | bytes 1376264 | tf_op jit(solution)/shard_map/ppermute | solution.py:430
  66.6 25.2 %all-to-all-start.2 = ((bf16[16,112,128]{2,1,0:T(8,128)(2,1)}), bf16[16,112,128]{2,1,0:T(8,128)(2,1)S(1)}, u32[]{:S(2)}, u32[]{:S(2)}) async-start(bf16[16,112,128]{2,1,0:T(8,128)(2,1)} %shard_map.83), calls=%async_computation.2 | async-start | bytes 917504 | tf_op jit(solution)/shard_map/all_to_all | solution.py:425
  77.1 7.3 %collective-permute-start.6 = (bf16[2,2,128,256]{3,2,1,0:T(8,128)(2,1)S(1)}, bf16[2,2,128,256]{3,2,1,0:T(8,128)(2,1)S(1)}, u32[]{:S(2)}, u32[]{:S(2)}) collective-permute-start(bf16[2,2,128,256]{3,2,1,0:T(8,128)(2,1)S(1)} %get-tuple-element.51), channel_id=1, source_target_pairs={{0,2},{2,0},{4,6},{6,4},{1,3},{3,1},{5,7},{7,5},{8,10},{10,8},{12,... | collective-permute-start | bytes 786440 | tf_op jit(solution)/shard_map/ppermute | solution.py:430
  92.6 17.9 %all-to-all-start.3 = ((bf16[16,112,128]{2,1,0:T(8,128)(2,1)}), bf16[16,112,128]{2,1,0:T(8,128)(2,1)S(1)}, u32[]{:S(2)}, u32[]{:S(2)}) async-start(bf16[16,112,128]{2,1,0:T(8,128)(2,1)} %shard_map.85), calls=%async_computation.3 | async-start | bytes 917504 | tf_op jit(solution)/shard_map/all_to_all | solution.py:425
  96.9 5.1 %collective-permute-start.7 = (bf16[2,128,256]{2,1,0:T(8,128)(2,1)S(1)}, bf16[2,128,256]{2,1,0:T(8,128)(2,1)S(1)}, u32[]{:S(2)}, u32[]{:S(2)}) collective-permute-start(bf16[2,128,256]{2,1,0:T(8,128)(2,1)S(1)} %get-tuple-element.55), channel_id=1, source_target_pairs={{0,6},{2,4},{4,2},{6,0},{1,7},{3,5},{5,3},{7,1},{8,14},{10,12},{12... | collective-permute-start | bytes 393224 | tf_op jit(solution)/shard_map/ppermute | solution.py:435
  102.1 5.2 %collective-permute-start.8 = (bf16[128,256]{1,0:T(8,128)(2,1)S(1)}, bf16[128,256]{1,0:T(8,128)(2,1)S(1)}, u32[]{:S(2)}, u32[]{:S(2)}) collective-permute-start(bf16[128,256]{1,0:T(8,128)(2,1)S(1)} %get-tuple-element.57), channel_id=1, source_target_pairs={{0,1},{1,0},{2,3},{3,2},{4,5},{5,4},{6,7},{7,6},{8,9},{9,8},{10,11... | collective-permute-start | bytes 196616 | tf_op jit(solution)/shard_map/ppermute | solution.py:430
  110.5 4.6 %collective-permute-start.9 = (bf16[1792,128]{1,0:T(8,128)(2,1)S(1)}, bf16[1792,128]{1,0:T(8,128)(2,1)S(1)}, u32[]{:S(2)}, u32[]{:S(2)}) collective-permute-start(bf16[1792,128]{1,0:T(8,128)(2,1)S(1)} %bitcast.15), channel_id=1, source_target_pairs={{0,8},{8,0},{1,9},{9,1},{2,10},{10,2},{3,11},{11,3},{4,12},{12,4},... | collective-permute-start | bytes 1376264 | tf_op jit(solution)/shard_map/ppermute | solution.py:430

commit v3 on v2

--- a/solution.py
+++ b/solution.py
@@ -24,14 +24,18 @@
     return lax.dot_general(a, b, dims, preferred_element_type=f32)
 
 
-def kernel_call(body, outs, flops, *args, scratch=(), space=pltpu.VMEM, target=pltpu.VMEM, limit=16):
+def kernel_call(
+    body, outs, flops, *args, scratch=(), space=pltpu.VMEM, target=pltpu.VMEM, limit=16, alias={}
+):
+    spaces = [pltpu.HBM if i in alias else space for i in range(len(args))]
     moved = sum(a.size * a.dtype.itemsize for a in (*args, *outs))
     return pl.pallas_call(
         body,
         out_shape=outs,
-        in_specs=[pl.BlockSpec(memory_space=space)] * len(args),
+        in_specs=[pl.BlockSpec(memory_space=s) for s in spaces],
         out_specs=[pl.BlockSpec(memory_space=target)] * len(outs),
         scratch_shapes=scratch,
+        input_output_aliases=alias,
         compiler_params=pltpu.CompilerParams(vmem_limit_bytes=limit << 20),
         cost_estimate=pl.CostEstimate(flops=flops, bytes_accessed=moved, transcendentals=0),
     )(*args)
@@ -98,22 +102,33 @@
     return s * (1.0 + v * (1.0 - s))
 
 
-def pack_inputs(x_far, w_far, cot_far, out, x, w, cot_near, sems):
-    copies = [
-        pltpu.make_async_copy(far, near, sems.at[i])
-        for i, (far, near) in enumerate(((x_far, x), (cot_far, cot_near), (w_far, w)))
+def pack_inputs(x_far, w_far, cot_far, out, x, w, cot_near, cot, blocks, sems):
+    loads = [
+        pltpu.make_async_copy(x_far, x, sems.at[0]),
+        pltpu.make_async_copy(cot_far, cot_near, sems.at[1]),
+        pltpu.make_async_copy(w_far, w, sems.at[2]),
     ]
-    for copy in copies:
+    for copy in loads:
         copy.start()
-    copies[0].wait()
-    copies[1].wait()
-    cot = jnp.concatenate([cot_near[0, i].astype(f32) for i in range(4)], 0).astype(bf16)
+    sent = []
+
+    def send(source, f, at, size):
+        target = out.at[f, pl.ds(at, size), :]
+        copy = pltpu.make_async_copy(source, target, sems.at[3 + len(sent)])
+        copy.start()
+        sent.append(copy)
+
+    loads[0].wait()
     for f in range(8):
         for h in (0, 1):
-            out[f, h * 128 : h * 128 + 128, :] = x[:, h * 128 : h * 128 + 128]
-            at = X_ROWS + h * 16
-            out[f, at : at + 16, :] = cot[:, h * 128 : h * 128 + 128]
-    copies[2].wait()
+            send(x.at[:, pl.ds(h * 128, 128)], f, h * 128, 128)
+    loads[1].wait()
+    for h in (0, 1):
+        rows = [cot_near[0, i, :, h * 128 : h * 128 + 128].astype(f32) for i in range(4)]
+        cot[h * 16 : h * 16 + 16, :] = jnp.concatenate(rows, 0).astype(bf16)
+    for f in range(8):
+        send(cot, f, X_ROWS, COT_ROWS)
+    loads[2].wait()
     first_core = lax.axis_index("core") == 0
     lane = lanes(32)
 
@@ -122,15 +137,18 @@
         taps = [w[pl.ds(at + 32 * t, 32), h * 128 : h * 128 + 128].astype(f32) for t in range(3)]
         return three(*(rotated(taps[t], t - m) for t in range(3)))
 
-    for b in range(4):
-        for h in (0, 1):
+    for h in (0, 1):
+        for b in range(4):
             extra = w[(12 + min(b, 2)) * 32 : (13 + min(b, 2)) * 32, h * 128 : h * 128 + 128]
             extra = extra.astype(f32)
             for m in range(4):
                 v = block(jnp.where(first_core, b, b + 5), m, h)
                 v = jnp.where(lane < 96, v, rotated(extra, 3 - m))
-                at = X_ROWS + COT_ROWS + b * 32
-                out[4 * h + m, at : at + 32, :] = v.astype(bf16)
+                blocks[4 * h + m, b * 32 : b * 32 + 32, :] = v.astype(bf16)
+        for m in range(4):
+            send(blocks.at[4 * h + m], 4 * h + m, X_ROWS + COT_ROWS, W_ROWS)
+    for copy in sent:
+        copy.wait()
 
 
 def prepare_first(w, wide, tall):
@@ -258,7 +276,7 @@
             field[slot * ROWS : slot * ROWS + ROWS, h * 128 : h * 128 + 128] = v.astype(bf16)
 
 
-def second_error(parts, got, section, err):
+def second_error(parts, got, section, err, full):
     for h in (0, 1):
         lane = slice(h * 128, h * 128 + 128)
         row = slice(h * 128, h * 128 + 128)
@@ -268,8 +286,12 @@
         cot = jnp.concatenate(
             [got[g, X_ROWS + h * 16 : X_ROWS + h * 16 + 16, :].astype(f32) for g in range(8)], 0
         )
-        section[:, lane] = v * sigmoid(v)
+        full[:, lane] = v * sigmoid(v)
         err[:, lane] = (cot * silu_slope(v)).astype(bf16)
+    flt = lax.axis_index("flt_x") * 2 + lax.axis_index("flt_y")
+    own = full[pl.ds(pl.multiple_of(flt * 16, 16), 16), :]
+    for i in range(4):
+        section[0, i] = own[4 * i : 4 * i + 4]
 
 
 def spread_out(err, full):
@@ -399,26 +421,32 @@
         out[i] = v
 
 
-def finish_grads(own, other, first, second, near, sems):
-    core = lax.axis_index("core")
-
-    for i, source in enumerate((own, other)):
+def finish_part(rows, first, second, near, sems, to_first):
+    pieces = [pl.ds(i * 144, 144) for i in range(6)]
+    for i, piece in enumerate(pieces):
         for h in (0, 1):
-            near[i, :, h * 128 : h * 128 + 128] = source[h * 864 : h * 864 + 864, :].astype(f32)
-        for c in (0, 1):
-
-            @pl.when(core == c)
-            def _(i=i, c=c):
-                target = first if i == c else second
-                pltpu.make_async_copy(near.at[i], target, sems.at[i]).start()
-
-    for c in (0, 1):
-
-        @pl.when(core == c)
-        def _(c=c):
-            for i in (0, 1):
-                target = first if i == c else second
-                pltpu.make_async_copy(near.at[i], target, sems.at[i]).wait()
+            at = h * 864 + i * 144
+            near[piece, h * 128 : h * 128 + 128] = rows[at : at + 144, :].astype(f32)
+        for target, wanted in ((first, to_first), (second, jnp.logical_not(to_first))):
+
+            @pl.when(wanted)
+            def _(target=target):
+                pltpu.make_async_copy(near.at[piece], target.at[piece], sems.at[i]).start()
+
+    for target, wanted in ((first, to_first), (second, jnp.logical_not(to_first))):
+
+        @pl.when(wanted)
+        def _(target=target):
+            for i, piece in enumerate(pieces):
+                pltpu.make_async_copy(near.at[piece], target.at[piece], sems.at[i]).wait()
+
+
+def finish_own(rows, first, second, near, sems):
+    finish_part(rows, first, second, near, sems, lax.axis_index("core") == 0)
+
+
+def finish_other(rows, first_in, second_in, first, second, near, sems):
+    finish_part(rows, first, second, near, sems, lax.axis_index("core") == 1)
 
 
 def exchange(v, axis):
@@ -463,9 +491,12 @@
             pltpu.VMEM((128, 256), bf16),
             pltpu.VMEM((864, 256), bf16),
             pltpu.VMEM((1, 4, 4, 256), bf16),
-            pltpu.SemaphoreType.DMA((3,)),
+            pltpu.VMEM((COT_ROWS, 128), bf16),
+            pltpu.VMEM((8, W_ROWS, 128), bf16),
+            pltpu.SemaphoreType.DMA((35,)),
         ],
         space=pltpu.HBM,
+        target=pltpu.HBM,
         limit=60,
     )
     got = exchange(packed, FLT)
@@ -492,8 +523,13 @@
         scratch=[pltpu.VMEM((ROWS, 1152), bf16), pltpu.VMEM((2, ROWS, 128), f32)],
     )
     parts = exchange(partial, FLT)
-    section, err = kernel_call(
-        second_error, [shape((128, 256), f32), shape((128, 256), bf16)], 0, parts, got
+    section_out, err = kernel_call(
+        second_error,
+        [shape((1, 4, 4, 256), f32), shape((128, 256), bf16)],
+        0,
+        parts,
+        got,
+        scratch=[pltpu.VMEM((128, 256), f32)],
     )
     across, within = next_chip(err), swapped(err)
     (hidden,) = kernel_call(gather_hidden, [shape((1024, 256), bf16)], 0, parts)
@@ -527,26 +563,22 @@
     kept_in, sent_in = kernel_call(
         add_pairs, [shape((2, 128, 256), f32), shape((2, 128, 256), bf16)], 0, kept_in, came_in
     )
-    mine, sent_in = lax.optimization_barrier((mine, sent_in))
     came_in = mirrored(sent_in, "flt_x")
-    mine = exchange(mine, CHIPS).reshape(GRAD_PAD, 128)
     kept_in, sent_in = kernel_call(
         add_halves, [shape((128, 256), f32), shape((128, 256), bf16)], 0, kept_in, came_in
     )
+    mine, sent_in = lax.optimization_barrier((mine, sent_in))
     came_in = swapped(sent_in, "flt_y")
+    mine = exchange(mine, CHIPS).reshape(GRAD_PAD, 128)
     (grad_input,) = kernel_call(add_last, [shape((128, 256), f32)], 0, kept_in, came_in)
     mine, grad_input = lax.optimization_barrier((mine, grad_input))
+    full = [shape((864, 256), f32)] * 2
+    scratch = [pltpu.VMEM((864, 256), f32), pltpu.SemaphoreType.DMA((6,))]
+    other = swapped(mine)
+    grads = kernel_call(finish_own, full, 0, mine, scratch=scratch, target=pltpu.HBM)
     grads = kernel_call(
-        finish_grads,
-        [shape((864, 256), f32)] * 2,
-        0,
-        mine,
-        swapped(mine),
-        scratch=[pltpu.VMEM((2, 864, 256), f32), pltpu.SemaphoreType.DMA((2,))],
-        target=pltpu.HBM,
-    )
-    row = lax.axis_index(FLT) * 16
-    section_out = lax.dynamic_slice_in_dim(section, row, 16, 0).reshape(1, 4, 4, 256)
+        finish_other, full, 0, other, *grads, scratch=scratch, target=pltpu.HBM, alias={1: 0, 2: 1}
+    )
     return (section_out, grad_input.reshape(2, 8, 8, 256), *(as_filters(g) for g in grads))
 
 

time: 117 us -> 118 us (level)
  starting transfers between devices: 39.7 us -> 42.5 us
  waiting for transfers between devices: 45.3 us -> 42.9 us
  Pallas kernels: 13.3 us -> 14.5 us
    ppermute x7, starting transfers between devices: 6.17 us -> 8.38 us  [swapped(): return lax.ppermute(v, axis, [(i, i ^ 1) for i in range(n)])]
    all_to_all x3, waiting for transfers between devices: 23.5 us -> 21.7 us  [exchange(): return lax.all_to_all(v, axis, 0, 0, tiled=True)]
    pallas_call x15 -> x16, Pallas kernels: 13.3 us -> 14.5 us  [kernel_call(): pl.pallas_call(body, out_shape=outs, in_specs=[pl.BlockSpec(memory_space=...]
  transfers between devices with their start and end apart: 13 -> 13, of which waited for: 10 -> 10; matrix products, arithmetic and copies ran while one was open for 1% -> 0% of each run, Pallas kernels for 2% -> 3%
where the time goes in v3:
time: 118 us; the launch traced here: 117 us
  waiting for transfers between devices  42.9 us (36%)
  starting transfers between devices  42.5 us (36%)
  blocking collectives  16.7 us (14%)
  Pallas kernels  14.5 us (12%)
    all_to_all x3, starting transfers between devices, exchange(): return lax.all_to_all(v, axis, 0, 0, tiled=True)  22.9 us
    all_to_all x3, waiting for transfers between devices, exchange(): return lax.all_to_all(v, axis, 0, 0, tiled=True)  21.7 us
    all_to_all x1, blocking collectives, exchange(): return lax.all_to_all(v, axis, 0, 0, tiled=True)  16.7 us
    pallas_call x16, Pallas kernels, kernel_call(): pl.pallas_call(body, out_shape=outs, in_specs=[pl.BlockSpec(memory_space=...  14.5 us
    ppermute x7, waiting for transfers between devices, swapped(): return lax.ppermute(v, axis, [(i, i ^ 1) for i in range(n)])  11.9 us
    ppermute x2, starting transfers between devices, next_chip(): return lax.ppermute(v, SP, pairs + [(b, a) for a, b in pairs])  10.4 us
    ppermute x7, starting transfers between devices, swapped(): return lax.ppermute(v, axis, [(i, i ^ 1) for i in range(n)])  8.38 us
    ppermute x2, waiting for transfers between devices, next_chip(): return lax.ppermute(v, SP, pairs + [(b, a) for a, b in pairs])  4.8 us
  transfers between devices with their start and end apart: 13, of which 10 were waited for; matrix products, arithmetic and copies ran while one was open for 0% of the time, Pallas kernels for 3%

profile of v3, /device:TPU:1, one launch (start us, length us, event | category | flops | bytes accessed | tf_op | source)
XLA Modules:
  0.0 117.5 jit_solution(15656310351108692471)
XLA Ops:
  0.6 2.4 %shard_map.75 = bf16[8,416,128]{2,1,0:T(8,128)(2,1)} custom-call(bf16[128,256]{1,0:T(8,128)(2,1)} %bitcast.22, bf16[864,256]{1,0:T(8,128)(2,1)} %bitcast.20, bf16[1,4,4,256]{3,2,1,0:T(4,128)(2,1)} %cot_far.1), custom_call_target="tpu_custom_call" | custom-call | bytes 1368064 | tf_op jit(solution)/shard_map/pallas_call | solution.py:32
  3.0 7.5 %all-to-all-start = ((bf16[8,416,128]{2,1,0:T(8,128)(2,1)}), bf16[8,416,128]{2,1,0:T(8,128)(2,1)S(1)}, u32[]{:S(2)}, u32[]{:S(2)}) async-start(bf16[8,416,128]{2,1,0:T(8,128)(2,1)} %shard_map.75), calls=%async_computation | async-start | bytes 1703936 | tf_op jit(solution)/shard_map/all_to_all | solution.py:453
  10.6 13.6 %all-to-all-done.got = bf16[8,416,128]{2,1,0:T(8,128)(2,1)S(1)} async-done(((bf16[8,416,128]{2,1,0:T(8,128)(2,1)}), bf16[8,416,128]{2,1,0:T(8,128)(2,1)S(1)}, u32[]{:S(2)}, u32[]{:S(2)}) %all-to-all-start) | async-done | bytes 852000 | tf_op jit(solution)/shard_map/all_to_all | solution.py:453
  24.2 1.5 %shard_map.77 = (f32[256,128]{1,0:T(8,128)S(1)}, f32[256,128]{1,0:T(8,128)S(1)}, f32[256,128]{1,0:T(8,128)S(1)}, f32[256,128]{1,0:T(8,128)S(1)}, bf16[1024,256]{...) custom-call(bf16[8,416,128]{2,1,0:T(8,128)(2,1)S(1)} %all-to-all-done.got, bf16[384,768]{1,0:T(8,128)(2,1)S(1)} %get-tuple-element.35.wide), custom_call_target="tpu_custom_call" | custom-call | flops 603979776 | bytes 2752512 | tf_op jit(solution)/shard_map/pallas_call | solution.py:32
  25.7 1.3 %collective-permute-start.2 = (bf16[8,128,128]{2,1,0:T(8,128)(2,1)S(1)}, bf16[8,128,128]{2,1,0:T(8,128)(2,1)S(1)}, u32[]{:S(2)}, u32[]{:S(2)}) collective-permute-start(bf16[8,128,128]{2,1,0:T(8,128)(2,1)S(1)} %get-tuple-element.40.own), channel_id=1, source_target_pairs={{0,8},{8,0},{1,9},{9,1},{2,10},{10,2},{3,11},{11,3},{4,12},{12,4},... | collective-permute-start | bytes 786440 | tf_op jit(solution)/shard_map/ppermute | solution.py:458
  27.0 2.6 %collective-permute-start.1 = (f32[256,128]{1,0:T(8,128)S(1)}, f32[256,128]{1,0:T(8,128)S(1)}, u32[]{:S(2)}, u32[]{:S(2)}) collective-permute-start(f32[256,128]{1,0:T(8,128)S(1)} %get-tuple-element.39), channel_id=1, source_target_pairs={{8,16},{24,32},{40,48},{56,64},{72,80},{88,96},{104,112},{120,128}... | collective-permute-start | bytes 393224 | tf_op jit(solution)/shard_map/ppermute | solution.py:468
  29.8 3.5 %collective-permute-done.1.across = f32[256,128]{1,0:T(8,128)S(1)} collective-permute-done((f32[256,128]{1,0:T(8,128)S(1)}, f32[256,128]{1,0:T(8,128)S(1)}, u32[]{:S(2)}, u32[]{:S(2)}) %collective-permute-start.1) | collective-permute-done | bytes 131104 | tf_op jit(solution)/shard_map/ppermute | solution.py:468
  33.3 0.6 shard_map.79
  33.9 16.7 %all_to_all.20.parts = bf16[8,512,128]{2,1,0:T(8,128)(2,1)S(1)} all-to-all(bf16[8,512,128]{2,1,0:T(8,128)(2,1)S(1)} %get-tuple-element.41), channel_id=1, replica_groups=mesh['sp_z'=8,'sp_y'=2,'core'=2,'flt_x'=4,'flt_y'=2] {'flt_x','flt_y'}, dimensions={0} | all-to-all | bytes 2097152 | tf_op jit(solution)/shard_map/all_to_all | solution.py:453
  50.7 0.7 shard_map.80
  51.4 7.8 %collective-permute-start.4 = (bf16[128,256]{1,0:T(8,128)(2,1)S(1)}, bf16[128,256]{1,0:T(8,128)(2,1)S(1)}, u32[]{:S(2)}, u32[]{:S(2)}) collective-permute-start(bf16[128,256]{1,0:T(8,128)(2,1)S(1)} %get-tuple-element.43.own), channel_id=1, source_target_pairs={{8,16},{24,32},{40,48},{56,64},{72,80},{88,96},{104,112},{120,128}... | collective-permute-start | bytes 196616 | tf_op jit(solution)/shard_map/ppermute | solution.py:468
  59.3 0.5 shard_map.81.hidden
  59.8 1.3 %collective-permute-done.4.across = bf16[128,256]{1,0:T(8,128)(2,1)S(1)} collective-permute-done((bf16[128,256]{1,0:T(8,128)(2,1)S(1)}, bf16[128,256]{1,0:T(8,128)(2,1)S(1)}, u32[]{:S(2)}, u32[]{:S(2)}) %collective-permute-start.4) | collective-permute-done | bytes 65568 | tf_op jit(solution)/shard_map/ppermute | solution.py:468
  61.1 3.3 %shard_map.82 = (bf16[1024,1152]{1,0:T(8,128)(2,1)S(1)}, f32[1792,128]{1,0:T(8,128)S(1)}, bf16[1792,128]{1,0:T(8,128)(2,1)S(1)}) custom-call(bf16[128,256]{1,0:T(8,128)(2,1)S(1)} %get-tuple-element.43.own, bf16[128,256]{1,0:T(8,128)(2,1)S(1)} %collective-permute-done.3.within, bf16[128,256]{1,0:T(8,128)(2,1)S(1)} %collective-permute-done.4.across, ...), custom_call_target="tpu_custom_call" | custom-call | flops 905969664 | bytes 5832704 | tf_op jit(solution)/shard_map/pallas_call | solution.py:32
  64.5 0.9 shard_map.84
  65.5 0.9 collective-permute-done.5.came
  66.4 0.8 shard_map.83
  67.2 10.5 %all-to-all-start.2 = ((bf16[16,112,128]{2,1,0:T(8,128)(2,1)}), bf16[16,112,128]{2,1,0:T(8,128)(2,1)S(1)}, u32[]{:S(2)}, u32[]{:S(2)}) async-start(bf16[16,112,128]{2,1,0:T(8,128)(2,1)} %shard_map.83), calls=%async_computation.2 | async-start | bytes 917504 | tf_op jit(solution)/shard_map/all_to_all | solution.py:453
  77.8 7.2 %collective-permute-done.6.came = bf16[2,2,128,256]{3,2,1,0:T(8,128)(2,1)S(1)} collective-permute-done((bf16[2,2,128,256]{3,2,1,0:T(8,128)(2,1)S(1)}, bf16[2,2,128,256]{3,2,1,0:T(8,128)(2,1)S(1)}, u32[]{:S(2)}, u32[]{:S(2)}) %collective-permute-start.6) | collective-permute-done | bytes 262176 | tf_op jit(solution)/shard_map/ppermute | solution.py:458
  85.0 0.9 collective-permute-start.7
  85.9 4.5 %collective-permute-done.7.came = bf16[2,128,256]{2,1,0:T(8,128)(2,1)S(1)} collective-permute-done((bf16[2,128,256]{2,1,0:T(8,128)(2,1)S(1)}, bf16[2,128,256]{2,1,0:T(8,128)(2,1)S(1)}, u32[]{:S(2)}, u32[]{:S(2)}) %collective-permute-start.7) | collective-permute-done | bytes 131104 | tf_op jit(solution)/shard_map/ppermute | solution.py:463
  90.5 1.9 %all-to-all-done.2.parts = bf16[16,112,128]{2,1,0:T(8,128)(2,1)S(1)} async-done(((bf16[16,112,128]{2,1,0:T(8,128)(2,1)}), bf16[16,112,128]{2,1,0:T(8,128)(2,1)S(1)}, u32[]{:S(2)}, u32[]{:S(2)}) %all-to-all-start.2) | async-done | bytes 458784 | tf_op jit(solution)/shard_map/all_to_all | solution.py:453
  92.4 0.8 shard_map.85
  93.2 4.9 %all-to-all-start.3 = ((bf16[16,112,128]{2,1,0:T(8,128)(2,1)}), bf16[16,112,128]{2,1,0:T(8,128)(2,1)S(1)}, u32[]{:S(2)}, u32[]{:S(2)}) async-start(bf16[16,112,128]{2,1,0:T(8,128)(2,1)} %shard_map.85), calls=%async_computation.3 | async-start | bytes 917504 | tf_op jit(solution)/shard_map/all_to_all | solution.py:453
  98.2 1.3 %collective-permute-start.8 = (bf16[128,256]{1,0:T(8,128)(2,1)S(1)}, bf16[128,256]{1,0:T(8,128)(2,1)S(1)}, u32[]{:S(2)}, u32[]{:S(2)}) collective-permute-start(bf16[128,256]{1,0:T(8,128)(2,1)S(1)} %get-tuple-element.59), channel_id=1, source_target_pairs={{0,1},{1,0},{2,3},{3,2},{4,5},{5,4},{6,7},{7,6},{8,9},{9,8},{10,11... | collective-permute-start | bytes 196616 | tf_op jit(solution)/shard_map/ppermute | solution.py:458
  99.5 3.4 %collective-permute-done.8.came = bf16[128,256]{1,0:T(8,128)(2,1)S(1)} collective-permute-done((bf16[128,256]{1,0:T(8,128)(2,1)S(1)}, bf16[128,256]{1,0:T(8,128)(2,1)S(1)}, u32[]{:S(2)}, u32[]{:S(2)}) %collective-permute-start.8) | collective-permute-done | bytes 65568 | tf_op jit(solution)/shard_map/ppermute | solution.py:458
  102.9 0.7 shard_map.88
  103.5 6.1 %all-to-all-done.3 = bf16[16,112,128]{2,1,0:T(8,128)(2,1)S(1)} async-done(((bf16[16,112,128]{2,1,0:T(8,128)(2,1)}), bf16[16,112,128]{2,1,0:T(8,128)(2,1)S(1)}, u32[]{:S(2)}, u32[]{:S(2)}) %all-to-all-start.3) | async-done | bytes 458784 | tf_op jit(solution)/shard_map/all_to_all | solution.py:453
  109.7 5.4 %collective-permute-start.9 = (bf16[1792,128]{1,0:T(8,128)(2,1)S(1)}, bf16[1792,128]{1,0:T(8,128)(2,1)S(1)}, u32[]{:S(2)}, u32[]{:S(2)}) collective-permute-start(bf16[1792,128]{1,0:T(8,128)(2,1)S(1)} %bitcast.15), channel_id=1, source_target_pairs={{0,8},{8,0},{1,9},{9,1},{2,10},{10,2},{3,11},{11,3},{4,12},{12,4},... | collective-permute-start | bytes 1376264 | tf_op jit(solution)/shard_map/ppermute | solution.py:458
  115.1 1.0 shard_map.89
  116.1 0.5 collective-permute-done.9.rows
  116.5 1.0 shard_map.90
  (13 shorter events, 0.7 us)
Async XLA Ops:
  0.6 9.9 %copy-start = (bf16[32,3,3,3,256]{4,0,3,2,1:T(8,128)(2,1)S(1)}, bf16[32,3,3,3,256]{4,0,3,2,1:T(8,128)(2,1)}, u32[]{:S(2)}) copy-start(bf16[32,3,3,3,256]{4,0,3,2,1:T(8,128)(2,1)} %param.5) | copy-start | bytes 1327108
  3.0 21.2 %all-to-all-start = ((bf16[8,416,128]{2,1,0:T(8,128)(2,1)}), bf16[8,416,128]{2,1,0:T(8,128)(2,1)S(1)}, u32[]{:S(2)}, u32[]{:S(2)}) async-start(bf16[8,416,128]{2,1,0:T(8,128)(2,1)} %shard_map.75), calls=%async_computation | async-start | bytes 1703936 | tf_op jit(solution)/shard_map/all_to_all | solution.py:453
  25.7 4.0 %collective-permute-start.2 = (bf16[8,128,128]{2,1,0:T(8,128)(2,1)S(1)}, bf16[8,128,128]{2,1,0:T(8,128)(2,1)S(1)}, u32[]{:S(2)}, u32[]{:S(2)}) collective-permute-start(bf16[8,128,128]{2,1,0:T(8,128)(2,1)S(1)} %get-tuple-element.40.own), channel_id=1, source_target_pairs={{0,8},{8,0},{1,9},{9,1},{2,10},{10,2},{3,11},{11,3},{4,12},{12,4},... | collective-permute-start | bytes 786440 | tf_op jit(solution)/shard_map/ppermute | solution.py:458
  26.9 2.9 %collective-permute-start = (f32[256,128]{1,0:T(8,128)S(1)}, f32[256,128]{1,0:T(8,128)S(1)}, u32[]{:S(2)}, u32[]{:S(2)}) collective-permute-start(f32[256,128]{1,0:T(8,128)S(1)} %get-tuple-element.38), channel_id=1, source_target_pairs={{0,8},{8,0},{1,9},{9,1},{2,10},{10,2},{3,11},{11,3},{4,12},{12,4},... | collective-permute-start | bytes 393224 | tf_op jit(solution)/shard_map/ppermute | solution.py:458
  27.0 6.3 %collective-permute-start.1 = (f32[256,128]{1,0:T(8,128)S(1)}, f32[256,128]{1,0:T(8,128)S(1)}, u32[]{:S(2)}, u32[]{:S(2)}) collective-permute-start(f32[256,128]{1,0:T(8,128)S(1)} %get-tuple-element.39), channel_id=1, source_target_pairs={{8,16},{24,32},{40,48},{56,64},{72,80},{88,96},{104,112},{120,128}... | collective-permute-start | bytes 393224 | tf_op jit(solution)/shard_map/ppermute | solution.py:468
  51.4 9.7 %collective-permute-start.4 = (bf16[128,256]{1,0:T(8,128)(2,1)S(1)}, bf16[128,256]{1,0:T(8,128)(2,1)S(1)}, u32[]{:S(2)}, u32[]{:S(2)}) collective-permute-start(bf16[128,256]{1,0:T(8,128)(2,1)S(1)} %get-tuple-element.43.own), channel_id=1, source_target_pairs={{8,16},{24,32},{40,48},{56,64},{72,80},{88,96},{104,112},{120,128}... | collective-permute-start | bytes 196616 | tf_op jit(solution)/shard_map/ppermute | solution.py:468
  59.2 1.9 %collective-permute-start.3 = (bf16[128,256]{1,0:T(8,128)(2,1)S(1)}, bf16[128,256]{1,0:T(8,128)(2,1)S(1)}, u32[]{:S(2)}, u32[]{:S(2)}) collective-permute-start(bf16[128,256]{1,0:T(8,128)(2,1)S(1)} %get-tuple-element.43.own), channel_id=1, source_target_pairs={{0,8},{8,0},{1,9},{9,1},{2,10},{10,2},{3,11},{11,3},{4,12},{12,4},... | collective-permute-start | bytes 196616 | tf_op jit(solution)/shard_map/ppermute | solution.py:458
  64.4 1.9 %collective-permute-start.5 = (bf16[1792,128]{1,0:T(8,128)(2,1)S(1)}, bf16[1792,128]{1,0:T(8,128)(2,1)S(1)}, u32[]{:S(2)}, u32[]{:S(2)}) collective-permute-start(bf16[1792,128]{1,0:T(8,128)(2,1)S(1)} %get-tuple-element.47), channel_id=1, source_target_pairs={{0,8},{8,0},{1,9},{9,1},{2,10},{10,2},{3,11},{11,3},{4,12},{12,4},... | collective-permute-start | bytes 1376264 | tf_op jit(solution)/shard_map/ppermute | solution.py:458
  67.2 25.2 %all-to-all-start.2 = ((bf16[16,112,128]{2,1,0:T(8,128)(2,1)}), bf16[16,112,128]{2,1,0:T(8,128)(2,1)S(1)}, u32[]{:S(2)}, u32[]{:S(2)}) async-start(bf16[16,112,128]{2,1,0:T(8,128)(2,1)} %shard_map.83), calls=%async_computation.2 | async-start | bytes 917504 | tf_op jit(solution)/shard_map/all_to_all | solution.py:453
  77.7 7.3 %collective-permute-start.6 = (bf16[2,2,128,256]{3,2,1,0:T(8,128)(2,1)S(1)}, bf16[2,2,128,256]{3,2,1,0:T(8,128)(2,1)S(1)}, u32[]{:S(2)}, u32[]{:S(2)}) collective-permute-start(bf16[2,2,128,256]{3,2,1,0:T(8,128)(2,1)S(1)} %get-tuple-element.53), channel_id=1, source_target_pairs={{0,2},{2,0},{4,6},{6,4},{1,3},{3,1},{5,7},{7,5},{8,10},{10,8},{12,... | collective-permute-start | bytes 786440 | tf_op jit(solution)/shard_map/ppermute | solution.py:458
  85.0 5.4 %collective-permute-start.7 = (bf16[2,128,256]{2,1,0:T(8,128)(2,1)S(1)}, bf16[2,128,256]{2,1,0:T(8,128)(2,1)S(1)}, u32[]{:S(2)}, u32[]{:S(2)}) collective-permute-start(bf16[2,128,256]{2,1,0:T(8,128)(2,1)S(1)} %get-tuple-element.55), channel_id=1, source_target_pairs={{0,6},{2,4},{4,2},{6,0},{1,7},{3,5},{5,3},{7,1},{8,14},{10,12},{12... | collective-permute-start | bytes 393224 | tf_op jit(solution)/shard_map/ppermute | solution.py:463
  93.2 16.4 %all-to-all-start.3 = ((bf16[16,112,128]{2,1,0:T(8,128)(2,1)}), bf16[16,112,128]{2,1,0:T(8,128)(2,1)S(1)}, u32[]{:S(2)}, u32[]{:S(2)}) async-start(bf16[16,112,128]{2,1,0:T(8,128)(2,1)} %shard_map.85), calls=%async_computation.3 | async-start | bytes 917504 | tf_op jit(solution)/shard_map/all_to_all | solution.py:453
  98.2 4.7 %collective-permute-start.8 = (bf16[128,256]{1,0:T(8,128)(2,1)S(1)}, bf16[128,256]{1,0:T(8,128)(2,1)S(1)}, u32[]{:S(2)}, u32[]{:S(2)}) collective-permute-start(bf16[128,256]{1,0:T(8,128)(2,1)S(1)} %get-tuple-element.59), channel_id=1, source_target_pairs={{0,1},{1,0},{2,3},{3,2},{4,5},{5,4},{6,7},{7,6},{8,9},{9,8},{10,11... | collective-permute-start | bytes 196616 | tf_op jit(solution)/shard_map/ppermute | solution.py:458
  109.7 6.9 %collective-permute-start.9 = (bf16[1792,128]{1,0:T(8,128)(2,1)S(1)}, bf16[1792,128]{1,0:T(8,128)(2,1)S(1)}, u32[]{:S(2)}, u32[]{:S(2)}) collective-permute-start(bf16[1792,128]{1,0:T(8,128)(2,1)S(1)} %bitcast.15), channel_id=1, source_target_pairs={{0,8},{8,0},{1,9},{9,1},{2,10},{10,2},{3,11},{11,3},{4,12},{12,4},... | collective-permute-start | bytes 1376264 | tf_op jit(solution)/shard_map/ppermute | solution.py:458

commit v4 on v3

--- a/solution.py
+++ b/solution.py
@@ -265,7 +265,16 @@
             out[g, h * 128 : h * 128 + 128, :] = v
 
 
-def gather_hidden(parts, field):
+def gather_hidden(parts, field, section):
+    flt = lax.axis_index("flt_x") * 2 + lax.axis_index("flt_y")
+    for h in (0, 1):
+        row = pl.ds(pl.multiple_of(h * 128 + flt * 16, 16), 16)
+        v = parts[0, row, :].astype(f32)
+        for g in range(1, 8):
+            v = v + parts[g, row, :].astype(f32)
+        v = v * sigmoid(v)
+        for i in range(4):
+            section[0, i, :, h * 128 : h * 128 + 128] = v[4 * i : 4 * i + 4]
     lane = lanes(ROWS)
     for h in (0, 1):
         blocks = [parts[4 * h + m, ROWS:, :].astype(f32) for m in range(4)]
@@ -276,7 +285,7 @@
             field[slot * ROWS : slot * ROWS + ROWS, h * 128 : h * 128 + 128] = v.astype(bf16)
 
 
-def second_error(parts, got, section, err, full):
+def second_error(parts, got, err):
     for h in (0, 1):
         lane = slice(h * 128, h * 128 + 128)
         row = slice(h * 128, h * 128 + 128)
@@ -286,12 +295,7 @@
         cot = jnp.concatenate(
             [got[g, X_ROWS + h * 16 : X_ROWS + h * 16 + 16, :].astype(f32) for g in range(8)], 0
         )
-        full[:, lane] = v * sigmoid(v)
         err[:, lane] = (cot * silu_slope(v)).astype(bf16)
-    flt = lax.axis_index("flt_x") * 2 + lax.axis_index("flt_y")
-    own = full[pl.ds(pl.multiple_of(flt * 16, 16), 16), :]
-    for i in range(4):
-        section[0, i] = own[4 * i : 4 * i + 4]
 
 
 def spread_out(err, full):
@@ -523,16 +527,11 @@
         scratch=[pltpu.VMEM((ROWS, 1152), bf16), pltpu.VMEM((2, ROWS, 128), f32)],
     )
     parts = exchange(partial, FLT)
-    section_out, err = kernel_call(
-        second_error,
-        [shape((1, 4, 4, 256), f32), shape((128, 256), bf16)],
-        0,
-        parts,
-        got,
-        scratch=[pltpu.VMEM((128, 256), f32)],
-    )
+    (err,) = kernel_call(second_error, [shape((128, 256), bf16)], 0, parts, got)
     across, within = next_chip(err), swapped(err)
-    (hidden,) = kernel_call(gather_hidden, [shape((1024, 256), bf16)], 0, parts)
+    hidden, section_out = kernel_call(
+        gather_hidden, [shape((1024, 256), bf16), shape((1, 4, 4, 256), f32)], 0, parts
+    )
     window, kept, sent = kernel_call(
         backward,
         [shape((1024, 1152), bf16), shape((GRAD_PAD, 128), f32), shape((GRAD_PAD, 128), bf16)],

time: 118 us -> 117 us (level)
  no operation moved by 1% of the time
where the time goes in v4:
time: 117 us
  starting transfers between devices  42.6 us (36%)
  waiting for transfers between devices  42.3 us (36%)
  blocking collectives  16.7 us (14%)
  Pallas kernels  14.5 us (12%)
    all_to_all x3, starting transfers between devices, exchange(): return lax.all_to_all(v, axis, 0, 0, tiled=True)  22.9 us
    all_to_all x3, waiting for transfers between devices, exchange(): return lax.all_to_all(v, axis, 0, 0, tiled=True)  21.7 us
    all_to_all x1, blocking collectives, exchange(): return lax.all_to_all(v, axis, 0, 0, tiled=True)  16.7 us
    pallas_call x16, Pallas kernels, kernel_call(): pl.pallas_call(body, out_shape=outs, in_specs=[pl.BlockSpec(memory_space=...  14.5 us
    ppermute x7, waiting for transfers between devices, swapped(): return lax.ppermute(v, axis, [(i, i ^ 1) for i in range(n)])  11.9 us
    ppermute x2, starting transfers between devices, next_chip(): return lax.ppermute(v, SP, pairs + [(b, a) for a, b in pairs])  10.4 us
    ppermute x7, starting transfers between devices, swapped(): return lax.ppermute(v, axis, [(i, i ^ 1) for i in range(n)])  8.38 us
    ppermute x1, waiting for transfers between devices, mirrored(): return lax.ppermute(v, axis, [(i, n - 1 - i) for i in range(n)])  4.49 us
  transfers between devices with their start and end apart: 13, of which 10 were waited for; matrix products, arithmetic and copies ran while one was open for 0% of the time, Pallas kernels for 3%

profile of v4, /device:TPU:1, one launch (start us, length us, event | category | flops | bytes accessed | tf_op | source)
XLA Modules:
  0.0 116.9 jit_solution(1935880823265351518)
XLA Ops:
  0.6 2.4 %shard_map.75 = bf16[8,416,128]{2,1,0:T(8,128)(2,1)} custom-call(bf16[128,256]{1,0:T(8,128)(2,1)} %bitcast.22, bf16[864,256]{1,0:T(8,128)(2,1)} %bitcast.20, bf16[1,4,4,256]{3,2,1,0:T(4,128)(2,1)} %cot_far.1), custom_call_target="tpu_custom_call" | custom-call | bytes 1368064 | tf_op jit(solution)/shard_map/pallas_call | solution.py:32
  3.0 7.5 %all-to-all-start = ((bf16[8,416,128]{2,1,0:T(8,128)(2,1)}), bf16[8,416,128]{2,1,0:T(8,128)(2,1)S(1)}, u32[]{:S(2)}, u32[]{:S(2)}) async-start(bf16[8,416,128]{2,1,0:T(8,128)(2,1)} %shard_map.75), calls=%async_computation | async-start | bytes 1703936 | tf_op jit(solution)/shard_map/all_to_all | solution.py:457
  10.6 13.6 %all-to-all-done.got = bf16[8,416,128]{2,1,0:T(8,128)(2,1)S(1)} async-done(((bf16[8,416,128]{2,1,0:T(8,128)(2,1)}), bf16[8,416,128]{2,1,0:T(8,128)(2,1)S(1)}, u32[]{:S(2)}, u32[]{:S(2)}) %all-to-all-start) | async-done | bytes 852000 | tf_op jit(solution)/shard_map/all_to_all | solution.py:457
  24.2 1.5 %shard_map.77 = (f32[256,128]{1,0:T(8,128)S(1)}, f32[256,128]{1,0:T(8,128)S(1)}, f32[256,128]{1,0:T(8,128)S(1)}, f32[256,128]{1,0:T(8,128)S(1)}, bf16[1024,256]{...) custom-call(bf16[8,416,128]{2,1,0:T(8,128)(2,1)S(1)} %all-to-all-done.got, bf16[384,768]{1,0:T(8,128)(2,1)S(1)} %get-tuple-element.35.wide), custom_call_target="tpu_custom_call" | custom-call | flops 603979776 | bytes 2752512 | tf_op jit(solution)/shard_map/pallas_call | solution.py:32
  25.7 1.3 %collective-permute-start.2 = (bf16[8,128,128]{2,1,0:T(8,128)(2,1)S(1)}, bf16[8,128,128]{2,1,0:T(8,128)(2,1)S(1)}, u32[]{:S(2)}, u32[]{:S(2)}) collective-permute-start(bf16[8,128,128]{2,1,0:T(8,128)(2,1)S(1)} %get-tuple-element.40.own), channel_id=1, source_target_pairs={{0,8},{8,0},{1,9},{9,1},{2,10},{10,2},{3,11},{11,3},{4,12},{12,4},... | collective-permute-start | bytes 786440 | tf_op jit(solution)/shard_map/ppermute | solution.py:462
  27.0 2.6 %collective-permute-start.1 = (f32[256,128]{1,0:T(8,128)S(1)}, f32[256,128]{1,0:T(8,128)S(1)}, u32[]{:S(2)}, u32[]{:S(2)}) collective-permute-start(f32[256,128]{1,0:T(8,128)S(1)} %get-tuple-element.39), channel_id=1, source_target_pairs={{8,16},{24,32},{40,48},{56,64},{72,80},{88,96},{104,112},{120,128}... | collective-permute-start | bytes 393224 | tf_op jit(solution)/shard_map/ppermute | solution.py:472
  29.6 0.2 shard_map.78.w2
  29.8 3.5 %collective-permute-done.1.across = f32[256,128]{1,0:T(8,128)S(1)} collective-permute-done((f32[256,128]{1,0:T(8,128)S(1)}, f32[256,128]{1,0:T(8,128)S(1)}, u32[]{:S(2)}, u32[]{:S(2)}) %collective-permute-start.1) | collective-permute-done | bytes 131104 | tf_op jit(solution)/shard_map/ppermute | solution.py:472
  33.3 0.6 shard_map.79
  33.9 16.7 %all_to_all.20.parts = bf16[8,512,128]{2,1,0:T(8,128)(2,1)S(1)} all-to-all(bf16[8,512,128]{2,1,0:T(8,128)(2,1)S(1)} %get-tuple-element.41), channel_id=1, replica_groups=mesh['sp_z'=8,'sp_y'=2,'core'=2,'flt_x'=4,'flt_y'=2] {'flt_x','flt_y'}, dimensions={0} | all-to-all | bytes 2097152 | tf_op jit(solution)/shard_map/all_to_all | solution.py:457
  50.8 7.8 %collective-permute-start.4 = (bf16[128,256]{1,0:T(8,128)(2,1)S(1)}, bf16[128,256]{1,0:T(8,128)(2,1)S(1)}, u32[]{:S(2)}, u32[]{:S(2)}) collective-permute-start(bf16[128,256]{1,0:T(8,128)(2,1)S(1)} %shard_map.81.own), channel_id=1, source_target_pairs={{8,16},{24,32},{40,48},{56,64},{72,80},{88,96},{104,112},{120,128}... | collective-permute-start | bytes 196616 | tf_op jit(solution)/shard_map/ppermute | solution.py:472
  58.7 1.1 shard_map.80
  59.7 0.8 collective-permute-done.4.across
  60.5 3.3 %shard_map.82 = (bf16[1024,1152]{1,0:T(8,128)(2,1)S(1)}, f32[1792,128]{1,0:T(8,128)S(1)}, bf16[1792,128]{1,0:T(8,128)(2,1)S(1)}) custom-call(bf16[128,256]{1,0:T(8,128)(2,1)S(1)} %shard_map.81.own, bf16[128,256]{1,0:T(8,128)(2,1)S(1)} %collective-permute-done.3.within, bf16[128,256]{1,0:T(8,128)(2,1)S(1)} %collective-permute-done.4.across, ...), custom_call_target="tpu_custom_call" | custom-call | flops 905969664 | bytes 5832704 | tf_op jit(solution)/shard_map/pallas_call | solution.py:32
  64.0 0.9 shard_map.84
  64.9 0.9 collective-permute-done.5.came
  65.8 0.8 shard_map.83
  66.6 10.5 %all-to-all-start.2 = ((bf16[16,112,128]{2,1,0:T(8,128)(2,1)}), bf16[16,112,128]{2,1,0:T(8,128)(2,1)S(1)}, u32[]{:S(2)}, u32[]{:S(2)}) async-start(bf16[16,112,128]{2,1,0:T(8,128)(2,1)} %shard_map.83), calls=%async_computation.2 | async-start | bytes 917504 | tf_op jit(solution)/shard_map/all_to_all | solution.py:457
  77.2 7.2 %collective-permute-done.6.came = bf16[2,2,128,256]{3,2,1,0:T(8,128)(2,1)S(1)} collective-permute-done((bf16[2,2,128,256]{3,2,1,0:T(8,128)(2,1)S(1)}, bf16[2,2,128,256]{3,2,1,0:T(8,128)(2,1)S(1)}, u32[]{:S(2)}, u32[]{:S(2)}) %collective-permute-start.6) | collective-permute-done | bytes 262176 | tf_op jit(solution)/shard_map/ppermute | solution.py:462
  84.4 0.9 collective-permute-start.7
  85.3 4.5 %collective-permute-done.7.came = bf16[2,128,256]{2,1,0:T(8,128)(2,1)S(1)} collective-permute-done((bf16[2,128,256]{2,1,0:T(8,128)(2,1)S(1)}, bf16[2,128,256]{2,1,0:T(8,128)(2,1)S(1)}, u32[]{:S(2)}, u32[]{:S(2)}) %collective-permute-start.7) | collective-permute-done | bytes 131104 | tf_op jit(solution)/shard_map/ppermute | solution.py:467
  89.9 1.9 %all-to-all-done.2.parts = bf16[16,112,128]{2,1,0:T(8,128)(2,1)S(1)} async-done(((bf16[16,112,128]{2,1,0:T(8,128)(2,1)}), bf16[16,112,128]{2,1,0:T(8,128)(2,1)S(1)}, u32[]{:S(2)}, u32[]{:S(2)}) %all-to-all-start.2) | async-done | bytes 458784 | tf_op jit(solution)/shard_map/all_to_all | solution.py:457
  91.8 0.8 shard_map.85
  92.6 4.9 %all-to-all-start.3 = ((bf16[16,112,128]{2,1,0:T(8,128)(2,1)}), bf16[16,112,128]{2,1,0:T(8,128)(2,1)S(1)}, u32[]{:S(2)}, u32[]{:S(2)}) async-start(bf16[16,112,128]{2,1,0:T(8,128)(2,1)} %shard_map.85), calls=%async_computation.3 | async-start | bytes 917504 | tf_op jit(solution)/shard_map/all_to_all | solution.py:457
  97.6 1.3 %collective-permute-start.8 = (bf16[128,256]{1,0:T(8,128)(2,1)S(1)}, bf16[128,256]{1,0:T(8,128)(2,1)S(1)}, u32[]{:S(2)}, u32[]{:S(2)}) collective-permute-start(bf16[128,256]{1,0:T(8,128)(2,1)S(1)} %get-tuple-element.59), channel_id=1, source_target_pairs={{0,1},{1,0},{2,3},{3,2},{4,5},{5,4},{6,7},{7,6},{8,9},{9,8},{10,11... | collective-permute-start | bytes 196616 | tf_op jit(solution)/shard_map/ppermute | solution.py:462
  98.9 3.4 %collective-permute-done.8.came = bf16[128,256]{1,0:T(8,128)(2,1)S(1)} collective-permute-done((bf16[128,256]{1,0:T(8,128)(2,1)S(1)}, bf16[128,256]{1,0:T(8,128)(2,1)S(1)}, u32[]{:S(2)}, u32[]{:S(2)}) %collective-permute-start.8) | collective-permute-done | bytes 65568 | tf_op jit(solution)/shard_map/ppermute | solution.py:462
  102.3 0.7 shard_map.88
  103.0 6.1 %all-to-all-done.3 = bf16[16,112,128]{2,1,0:T(8,128)(2,1)S(1)} async-done(((bf16[16,112,128]{2,1,0:T(8,128)(2,1)}), bf16[16,112,128]{2,1,0:T(8,128)(2,1)S(1)}, u32[]{:S(2)}, u32[]{:S(2)}) %all-to-all-start.3) | async-done | bytes 458784 | tf_op jit(solution)/shard_map/all_to_all | solution.py:457
  109.1 5.4 %collective-permute-start.9 = (bf16[1792,128]{1,0:T(8,128)(2,1)S(1)}, bf16[1792,128]{1,0:T(8,128)(2,1)S(1)}, u32[]{:S(2)}, u32[]{:S(2)}) collective-permute-start(bf16[1792,128]{1,0:T(8,128)(2,1)S(1)} %bitcast.15), channel_id=1, source_target_pairs={{0,8},{8,0},{1,9},{9,1},{2,10},{10,2},{3,11},{11,3},{4,12},{12,4},... | collective-permute-start | bytes 1376264 | tf_op jit(solution)/shard_map/ppermute | solution.py:462
  114.5 1.0 shard_map.89
  115.5 0.5 collective-permute-done.9.rows
  115.9 1.0 shard_map.90
  (13 shorter events, 0.7 us)
Async XLA Ops:
  0.6 9.9 %copy-start = (bf16[32,3,3,3,256]{4,0,3,2,1:T(8,128)(2,1)S(1)}, bf16[32,3,3,3,256]{4,0,3,2,1:T(8,128)(2,1)}, u32[]{:S(2)}) copy-start(bf16[32,3,3,3,256]{4,0,3,2,1:T(8,128)(2,1)} %param.5) | copy-start | bytes 1327108
  3.0 21.2 %all-to-all-start = ((bf16[8,416,128]{2,1,0:T(8,128)(2,1)}), bf16[8,416,128]{2,1,0:T(8,128)(2,1)S(1)}, u32[]{:S(2)}, u32[]{:S(2)}) async-start(bf16[8,416,128]{2,1,0:T(8,128)(2,1)} %shard_map.75), calls=%async_computation | async-start | bytes 1703936 | tf_op jit(solution)/shard_map/all_to_all | solution.py:457
  25.7 4.0 %collective-permute-start.2 = (bf16[8,128,128]{2,1,0:T(8,128)(2,1)S(1)}, bf16[8,128,128]{2,1,0:T(8,128)(2,1)S(1)}, u32[]{:S(2)}, u32[]{:S(2)}) collective-permute-start(bf16[8,128,128]{2,1,0:T(8,128)(2,1)S(1)} %get-tuple-element.40.own), channel_id=1, source_target_pairs={{0,8},{8,0},{1,9},{9,1},{2,10},{10,2},{3,11},{11,3},{4,12},{12,4},... | collective-permute-start | bytes 786440 | tf_op jit(solution)/shard_map/ppermute | solution.py:462
  26.9 2.9 %collective-permute-start = (f32[256,128]{1,0:T(8,128)S(1)}, f32[256,128]{1,0:T(8,128)S(1)}, u32[]{:S(2)}, u32[]{:S(2)}) collective-permute-start(f32[256,128]{1,0:T(8,128)S(1)} %get-tuple-element.38), channel_id=1, source_target_pairs={{0,8},{8,0},{1,9},{9,1},{2,10},{10,2},{3,11},{11,3},{4,12},{12,4},... | collective-permute-start | bytes 393224 | tf_op jit(solution)/shard_map/ppermute | solution.py:462
  27.0 6.3 %collective-permute-start.1 = (f32[256,128]{1,0:T(8,128)S(1)}, f32[256,128]{1,0:T(8,128)S(1)}, u32[]{:S(2)}, u32[]{:S(2)}) collective-permute-start(f32[256,128]{1,0:T(8,128)S(1)} %get-tuple-element.39), channel_id=1, source_target_pairs={{8,16},{24,32},{40,48},{56,64},{72,80},{88,96},{104,112},{120,128}... | collective-permute-start | bytes 393224 | tf_op jit(solution)/shard_map/ppermute | solution.py:472
  50.8 9.7 %collective-permute-start.4 = (bf16[128,256]{1,0:T(8,128)(2,1)S(1)}, bf16[128,256]{1,0:T(8,128)(2,1)S(1)}, u32[]{:S(2)}, u32[]{:S(2)}) collective-permute-start(bf16[128,256]{1,0:T(8,128)(2,1)S(1)} %shard_map.81.own), channel_id=1, source_target_pairs={{8,16},{24,32},{40,48},{56,64},{72,80},{88,96},{104,112},{120,128}... | collective-permute-start | bytes 196616 | tf_op jit(solution)/shard_map/ppermute | solution.py:472
  58.6 1.9 %collective-permute-start.3 = (bf16[128,256]{1,0:T(8,128)(2,1)S(1)}, bf16[128,256]{1,0:T(8,128)(2,1)S(1)}, u32[]{:S(2)}, u32[]{:S(2)}) collective-permute-start(bf16[128,256]{1,0:T(8,128)(2,1)S(1)} %shard_map.81.own), channel_id=1, source_target_pairs={{0,8},{8,0},{1,9},{9,1},{2,10},{10,2},{3,11},{11,3},{4,12},{12,4},... | collective-permute-start | bytes 196616 | tf_op jit(solution)/shard_map/ppermute | solution.py:462
  63.9 1.9 %collective-permute-start.5 = (bf16[1792,128]{1,0:T(8,128)(2,1)S(1)}, bf16[1792,128]{1,0:T(8,128)(2,1)S(1)}, u32[]{:S(2)}, u32[]{:S(2)}) collective-permute-start(bf16[1792,128]{1,0:T(8,128)(2,1)S(1)} %get-tuple-element.47), channel_id=1, source_target_pairs={{0,8},{8,0},{1,9},{9,1},{2,10},{10,2},{3,11},{11,3},{4,12},{12,4},... | collective-permute-start | bytes 1376264 | tf_op jit(solution)/shard_map/ppermute | solution.py:462
  66.6 25.2 %all-to-all-start.2 = ((bf16[16,112,128]{2,1,0:T(8,128)(2,1)}), bf16[16,112,128]{2,1,0:T(8,128)(2,1)S(1)}, u32[]{:S(2)}, u32[]{:S(2)}) async-start(bf16[16,112,128]{2,1,0:T(8,128)(2,1)} %shard_map.83), calls=%async_computation.2 | async-start | bytes 917504 | tf_op jit(solution)/shard_map/all_to_all | solution.py:457
  77.1 7.3 %collective-permute-start.6 = (bf16[2,2,128,256]{3,2,1,0:T(8,128)(2,1)S(1)}, bf16[2,2,128,256]{3,2,1,0:T(8,128)(2,1)S(1)}, u32[]{:S(2)}, u32[]{:S(2)}) collective-permute-start(bf16[2,2,128,256]{3,2,1,0:T(8,128)(2,1)S(1)} %get-tuple-element.53), channel_id=1, source_target_pairs={{0,2},{2,0},{4,6},{6,4},{1,3},{3,1},{5,7},{7,5},{8,10},{10,8},{12,... | collective-permute-start | bytes 786440 | tf_op jit(solution)/shard_map/ppermute | solution.py:462
  84.4 5.4 %collective-permute-start.7 = (bf16[2,128,256]{2,1,0:T(8,128)(2,1)S(1)}, bf16[2,128,256]{2,1,0:T(8,128)(2,1)S(1)}, u32[]{:S(2)}, u32[]{:S(2)}) collective-permute-start(bf16[2,128,256]{2,1,0:T(8,128)(2,1)S(1)} %get-tuple-element.55), channel_id=1, source_target_pairs={{0,6},{2,4},{4,2},{6,0},{1,7},{3,5},{5,3},{7,1},{8,14},{10,12},{12... | collective-permute-start | bytes 393224 | tf_op jit(solution)/shard_map/ppermute | solution.py:467
  92.6 16.4 %all-to-all-start.3 = ((bf16[16,112,128]{2,1,0:T(8,128)(2,1)}), bf16[16,112,128]{2,1,0:T(8,128)(2,1)S(1)}, u32[]{:S(2)}, u32[]{:S(2)}) async-start(bf16[16,112,128]{2,1,0:T(8,128)(2,1)} %shard_map.85), calls=%async_computation.3 | async-start | bytes 917504 | tf_op jit(solution)/shard_map/all_to_all | solution.py:457
  97.6 4.7 %collective-permute-start.8 = (bf16[128,256]{1,0:T(8,128)(2,1)S(1)}, bf16[128,256]{1,0:T(8,128)(2,1)S(1)}, u32[]{:S(2)}, u32[]{:S(2)}) collective-permute-start(bf16[128,256]{1,0:T(8,128)(2,1)S(1)} %get-tuple-element.59), channel_id=1, source_target_pairs={{0,1},{1,0},{2,3},{3,2},{4,5},{5,4},{6,7},{7,6},{8,9},{9,8},{10,11... | collective-permute-start | bytes 196616 | tf_op jit(solution)/shard_map/ppermute | solution.py:462
  109.1 6.9 %collective-permute-start.9 = (bf16[1792,128]{1,0:T(8,128)(2,1)S(1)}, bf16[1792,128]{1,0:T(8,128)(2,1)S(1)}, u32[]{:S(2)}, u32[]{:S(2)}) collective-permute-start(bf16[1792,128]{1,0:T(8,128)(2,1)S(1)} %bitcast.15), channel_id=1, source_target_pairs={{0,8},{8,0},{1,9},{9,1},{2,10},{10,2},{3,11},{11,3},{4,12},{12,4},... | collective-permute-start | bytes 1376264 | tf_op jit(solution)/shard_map/ppermute | solution.py:462

commit v5 on v4

--- a/solution.py
+++ b/solution.py
@@ -562,13 +562,13 @@
     kept_in, sent_in = kernel_call(
         add_pairs, [shape((2, 128, 256), f32), shape((2, 128, 256), bf16)], 0, kept_in, came_in
     )
+    mine, sent_in = lax.optimization_barrier((mine, sent_in))
     came_in = mirrored(sent_in, "flt_x")
+    mine = exchange(mine, CHIPS).reshape(GRAD_PAD, 128)
     kept_in, sent_in = kernel_call(
         add_halves, [shape((128, 256), f32), shape((128, 256), bf16)], 0, kept_in, came_in
     )
-    mine, sent_in = lax.optimization_barrier((mine, sent_in))
     came_in = swapped(sent_in, "flt_y")
-    mine = exchange(mine, CHIPS).reshape(GRAD_PAD, 128)
     (grad_input,) = kernel_call(add_last, [shape((128, 256), f32)], 0, kept_in, came_in)
     mine, grad_input = lax.optimization_barrier((mine, grad_input))
     full = [shape((864, 256), f32)] * 2

time: 117 us -> 117 us (level)
  starting transfers between devices: 42.6 us -> 39.7 us
  waiting for transfers between devices: 42.3 us -> 44.4 us
    ppermute x7, starting transfers between devices: 8.38 us -> 6.17 us  [swapped(): return lax.ppermute(v, axis, [(i, i ^ 1) for i in range(n)])]
    all_to_all x3, waiting for transfers between devices: 21.7 us -> 23.5 us  [exchange(): return lax.all_to_all(v, axis, 0, 0, tiled=True)]
where the time goes in v5:
time: 117 us; the launch traced here: 116 us
  waiting for transfers between devices  44.4 us (38%)
  starting transfers between devices  39.7 us (34%)
  blocking collectives  16.7 us (14%)
  Pallas kernels  14.5 us (12%)
    all_to_all x3, waiting for transfers between devices, exchange(): return lax.all_to_all(v, axis, 0, 0, tiled=True)  23.5 us
    all_to_all x3, starting transfers between devices, exchange(): return lax.all_to_all(v, axis, 0, 0, tiled=True)  22.3 us
    all_to_all x1, blocking collectives, exchange(): return lax.all_to_all(v, axis, 0, 0, tiled=True)  16.7 us
    pallas_call x16, Pallas kernels, kernel_call(): pl.pallas_call(body, out_shape=outs, in_specs=[pl.BlockSpec(memory_space=...  14.5 us
    ppermute x7, waiting for transfers between devices, swapped(): return lax.ppermute(v, axis, [(i, i ^ 1) for i in range(n)])  12.4 us
    ppermute x2, starting transfers between devices, next_chip(): return lax.ppermute(v, SP, pairs + [(b, a) for a, b in pairs])  10.4 us
    ppermute x7, starting transfers between devices, swapped(): return lax.ppermute(v, axis, [(i, i ^ 1) for i in range(n)])  6.17 us
    ppermute x2, waiting for transfers between devices, next_chip(): return lax.ppermute(v, SP, pairs + [(b, a) for a, b in pairs])  4.24 us
  transfers between devices with their start and end apart: 13, of which 10 were waited for; matrix products, arithmetic and copies ran while one was open for 0% of the time, Pallas kernels for 3%

profile of v5, /device:TPU:1, one launch (start us, length us, event | category | flops | bytes accessed | tf_op | source)
XLA Modules:
  0.0 116.1 jit_solution(8284276872027874962)
XLA Ops:
  0.6 2.4 %shard_map.75 = bf16[8,416,128]{2,1,0:T(8,128)(2,1)} custom-call(bf16[128,256]{1,0:T(8,128)(2,1)} %bitcast.22, bf16[864,256]{1,0:T(8,128)(2,1)} %bitcast.20, bf16[1,4,4,256]{3,2,1,0:T(4,128)(2,1)} %cot_far.1), custom_call_target="tpu_custom_call" | custom-call | bytes 1368064 | tf_op jit(solution)/shard_map/pallas_call | solution.py:32
  3.0 7.5 %all-to-all-start = ((bf16[8,416,128]{2,1,0:T(8,128)(2,1)}), bf16[8,416,128]{2,1,0:T(8,128)(2,1)S(1)}, u32[]{:S(2)}, u32[]{:S(2)}) async-start(bf16[8,416,128]{2,1,0:T(8,128)(2,1)} %shard_map.75), calls=%async_computation | async-start | bytes 1703936 | tf_op jit(solution)/shard_map/all_to_all | solution.py:457
  10.6 13.6 %all-to-all-done.got = bf16[8,416,128]{2,1,0:T(8,128)(2,1)S(1)} async-done(((bf16[8,416,128]{2,1,0:T(8,128)(2,1)}), bf16[8,416,128]{2,1,0:T(8,128)(2,1)S(1)}, u32[]{:S(2)}, u32[]{:S(2)}) %all-to-all-start) | async-done | bytes 852000 | tf_op jit(solution)/shard_map/all_to_all | solution.py:457
  24.2 1.5 %shard_map.77 = (f32[256,128]{1,0:T(8,128)S(1)}, f32[256,128]{1,0:T(8,128)S(1)}, f32[256,128]{1,0:T(8,128)S(1)}, f32[256,128]{1,0:T(8,128)S(1)}, bf16[1024,256]{...) custom-call(bf16[8,416,128]{2,1,0:T(8,128)(2,1)S(1)} %all-to-all-done.got, bf16[384,768]{1,0:T(8,128)(2,1)S(1)} %get-tuple-element.35.wide), custom_call_target="tpu_custom_call" | custom-call | flops 603979776 | bytes 2752512 | tf_op jit(solution)/shard_map/pallas_call | solution.py:32
  25.7 1.3 %collective-permute-start.2 = (bf16[8,128,128]{2,1,0:T(8,128)(2,1)S(1)}, bf16[8,128,128]{2,1,0:T(8,128)(2,1)S(1)}, u32[]{:S(2)}, u32[]{:S(2)}) collective-permute-start(bf16[8,128,128]{2,1,0:T(8,128)(2,1)S(1)} %get-tuple-element.40.own), channel_id=1, source_target_pairs={{0,8},{8,0},{1,9},{9,1},{2,10},{10,2},{3,11},{11,3},{4,12},{12,4},... | collective-permute-start | bytes 786440 | tf_op jit(solution)/shard_map/ppermute | solution.py:462
  27.0 2.6 %collective-permute-start.1 = (f32[256,128]{1,0:T(8,128)S(1)}, f32[256,128]{1,0:T(8,128)S(1)}, u32[]{:S(2)}, u32[]{:S(2)}) collective-permute-start(f32[256,128]{1,0:T(8,128)S(1)} %get-tuple-element.39), channel_id=1, source_target_pairs={{8,16},{24,32},{40,48},{56,64},{72,80},{88,96},{104,112},{120,128}... | collective-permute-start | bytes 393224 | tf_op jit(solution)/shard_map/ppermute | solution.py:472
  29.6 0.2 shard_map.78.w2
  29.8 3.5 %collective-permute-done.1.across = f32[256,128]{1,0:T(8,128)S(1)} collective-permute-done((f32[256,128]{1,0:T(8,128)S(1)}, f32[256,128]{1,0:T(8,128)S(1)}, u32[]{:S(2)}, u32[]{:S(2)}) %collective-permute-start.1) | collective-permute-done | bytes 131104 | tf_op jit(solution)/shard_map/ppermute | solution.py:472
  33.3 0.6 shard_map.79
  33.9 16.7 %all_to_all.20.parts = bf16[8,512,128]{2,1,0:T(8,128)(2,1)S(1)} all-to-all(bf16[8,512,128]{2,1,0:T(8,128)(2,1)S(1)} %get-tuple-element.41), channel_id=1, replica_groups=mesh['sp_z'=8,'sp_y'=2,'core'=2,'flt_x'=4,'flt_y'=2] {'flt_x','flt_y'}, dimensions={0} | all-to-all | bytes 2097152 | tf_op jit(solution)/shard_map/all_to_all | solution.py:457
  50.8 7.8 %collective-permute-start.4 = (bf16[128,256]{1,0:T(8,128)(2,1)S(1)}, bf16[128,256]{1,0:T(8,128)(2,1)S(1)}, u32[]{:S(2)}, u32[]{:S(2)}) collective-permute-start(bf16[128,256]{1,0:T(8,128)(2,1)S(1)} %shard_map.81.own), channel_id=1, source_target_pairs={{8,16},{24,32},{40,48},{56,64},{72,80},{88,96},{104,112},{120,128}... | collective-permute-start | bytes 196616 | tf_op jit(solution)/shard_map/ppermute | solution.py:472
  58.7 1.1 shard_map.80
  59.7 0.8 collective-permute-done.4.across
  60.5 3.3 %shard_map.82 = (bf16[1024,1152]{1,0:T(8,128)(2,1)S(1)}, f32[1792,128]{1,0:T(8,128)S(1)}, bf16[1792,128]{1,0:T(8,128)(2,1)S(1)}) custom-call(bf16[128,256]{1,0:T(8,128)(2,1)S(1)} %shard_map.81.own, bf16[128,256]{1,0:T(8,128)(2,1)S(1)} %collective-permute-done.3.within, bf16[128,256]{1,0:T(8,128)(2,1)S(1)} %collective-permute-done.4.across, ...), custom_call_target="tpu_custom_call" | custom-call | flops 905969664 | bytes 5832704 | tf_op jit(solution)/shard_map/pallas_call | solution.py:32
  64.0 0.9 shard_map.84
  64.9 0.9 collective-permute-done.5.came
  65.8 0.8 shard_map.83
  66.6 10.5 %all-to-all-start.2 = ((bf16[16,112,128]{2,1,0:T(8,128)(2,1)}), bf16[16,112,128]{2,1,0:T(8,128)(2,1)S(1)}, u32[]{:S(2)}, u32[]{:S(2)}) async-start(bf16[16,112,128]{2,1,0:T(8,128)(2,1)} %shard_map.83), calls=%async_computation.2 | async-start | bytes 917504 | tf_op jit(solution)/shard_map/all_to_all | solution.py:457
  77.2 7.2 %collective-permute-done.6.came = bf16[2,2,128,256]{3,2,1,0:T(8,128)(2,1)S(1)} collective-permute-done((bf16[2,2,128,256]{3,2,1,0:T(8,128)(2,1)S(1)}, bf16[2,2,128,256]{3,2,1,0:T(8,128)(2,1)S(1)}, u32[]{:S(2)}, u32[]{:S(2)}) %collective-permute-start.6) | collective-permute-done | bytes 262176 | tf_op jit(solution)/shard_map/ppermute | solution.py:462
  84.4 7.4 %all-to-all-done.2.parts = bf16[16,112,128]{2,1,0:T(8,128)(2,1)S(1)} async-done(((bf16[16,112,128]{2,1,0:T(8,128)(2,1)}), bf16[16,112,128]{2,1,0:T(8,128)(2,1)S(1)}, u32[]{:S(2)}, u32[]{:S(2)}) %all-to-all-start.2) | async-done | bytes 458784 | tf_op jit(solution)/shard_map/all_to_all | solution.py:457
  91.8 0.8 shard_map.85
  92.6 4.3 %all-to-all-start.3 = ((bf16[16,112,128]{2,1,0:T(8,128)(2,1)}), bf16[16,112,128]{2,1,0:T(8,128)(2,1)S(1)}, u32[]{:S(2)}, u32[]{:S(2)}) async-start(bf16[16,112,128]{2,1,0:T(8,128)(2,1)} %shard_map.85), calls=%async_computation.3 | async-start | bytes 917504 | tf_op jit(solution)/shard_map/all_to_all | solution.py:457
  97.0 0.9 collective-permute-start.7
  97.9 4.2 %collective-permute-done.7.came = bf16[2,128,256]{2,1,0:T(8,128)(2,1)S(1)} collective-permute-done((bf16[2,128,256]{2,1,0:T(8,128)(2,1)S(1)}, bf16[2,128,256]{2,1,0:T(8,128)(2,1)S(1)}, u32[]{:S(2)}, u32[]{:S(2)}) %collective-permute-start.7) | collective-permute-done | bytes 131104 | tf_op jit(solution)/shard_map/ppermute | solution.py:467
  102.1 1.3 %collective-permute-start.8 = (bf16[128,256]{1,0:T(8,128)(2,1)S(1)}, bf16[128,256]{1,0:T(8,128)(2,1)S(1)}, u32[]{:S(2)}, u32[]{:S(2)}) collective-permute-start(bf16[128,256]{1,0:T(8,128)(2,1)S(1)} %get-tuple-element.59), channel_id=1, source_target_pairs={{0,1},{1,0},{2,3},{3,2},{4,5},{5,4},{6,7},{7,6},{8,9},{9,8},{10,11... | collective-permute-start | bytes 196616 | tf_op jit(solution)/shard_map/ppermute | solution.py:462
  103.4 3.9 %collective-permute-done.8.came = bf16[128,256]{1,0:T(8,128)(2,1)S(1)} collective-permute-done((bf16[128,256]{1,0:T(8,128)(2,1)S(1)}, bf16[128,256]{1,0:T(8,128)(2,1)S(1)}, u32[]{:S(2)}, u32[]{:S(2)}) %collective-permute-start.8) | collective-permute-done | bytes 65568 | tf_op jit(solution)/shard_map/ppermute | solution.py:462
  107.3 0.7 shard_map.88
  108.0 2.6 %all-to-all-done.3 = bf16[16,112,128]{2,1,0:T(8,128)(2,1)S(1)} async-done(((bf16[16,112,128]{2,1,0:T(8,128)(2,1)}), bf16[16,112,128]{2,1,0:T(8,128)(2,1)S(1)}, u32[]{:S(2)}, u32[]{:S(2)}) %all-to-all-start.3) | async-done | bytes 458784 | tf_op jit(solution)/shard_map/all_to_all | solution.py:457
  110.5 3.2 %collective-permute-start.9 = (bf16[1792,128]{1,0:T(8,128)(2,1)S(1)}, bf16[1792,128]{1,0:T(8,128)(2,1)S(1)}, u32[]{:S(2)}, u32[]{:S(2)}) collective-permute-start(bf16[1792,128]{1,0:T(8,128)(2,1)S(1)} %bitcast.15), channel_id=1, source_target_pairs={{0,8},{8,0},{1,9},{9,1},{2,10},{10,2},{3,11},{11,3},{4,12},{12,4},... | collective-permute-start | bytes 1376264 | tf_op jit(solution)/shard_map/ppermute | solution.py:462
  113.7 1.0 shard_map.89
  114.7 0.5 collective-permute-done.9.rows
  115.2 1.0 shard_map.90
  (13 shorter events, 0.7 us)
Async XLA Ops:
  0.6 9.9 %copy-start = (bf16[32,3,3,3,256]{4,0,3,2,1:T(8,128)(2,1)S(1)}, bf16[32,3,3,3,256]{4,0,3,2,1:T(8,128)(2,1)}, u32[]{:S(2)}) copy-start(bf16[32,3,3,3,256]{4,0,3,2,1:T(8,128)(2,1)} %param.5) | copy-start | bytes 1327108
  3.0 21.2 %all-to-all-start = ((bf16[8,416,128]{2,1,0:T(8,128)(2,1)}), bf16[8,416,128]{2,1,0:T(8,128)(2,1)S(1)}, u32[]{:S(2)}, u32[]{:S(2)}) async-start(bf16[8,416,128]{2,1,0:T(8,128)(2,1)} %shard_map.75), calls=%async_computation | async-start | bytes 1703936 | tf_op jit(solution)/shard_map/all_to_all | solution.py:457
  25.7 4.0 %collective-permute-start.2 = (bf16[8,128,128]{2,1,0:T(8,128)(2,1)S(1)}, bf16[8,128,128]{2,1,0:T(8,128)(2,1)S(1)}, u32[]{:S(2)}, u32[]{:S(2)}) collective-permute-start(bf16[8,128,128]{2,1,0:T(8,128)(2,1)S(1)} %get-tuple-element.40.own), channel_id=1, source_target_pairs={{0,8},{8,0},{1,9},{9,1},{2,10},{10,2},{3,11},{11,3},{4,12},{12,4},... | collective-permute-start | bytes 786440 | tf_op jit(solution)/shard_map/ppermute | solution.py:462
  26.9 2.9 %collective-permute-start = (f32[256,128]{1,0:T(8,128)S(1)}, f32[256,128]{1,0:T(8,128)S(1)}, u32[]{:S(2)}, u32[]{:S(2)}) collective-permute-start(f32[256,128]{1,0:T(8,128)S(1)} %get-tuple-element.38), channel_id=1, source_target_pairs={{0,8},{8,0},{1,9},{9,1},{2,10},{10,2},{3,11},{11,3},{4,12},{12,4},... | collective-permute-start | bytes 393224 | tf_op jit(solution)/shard_map/ppermute | solution.py:462
  27.0 6.3 %collective-permute-start.1 = (f32[256,128]{1,0:T(8,128)S(1)}, f32[256,128]{1,0:T(8,128)S(1)}, u32[]{:S(2)}, u32[]{:S(2)}) collective-permute-start(f32[256,128]{1,0:T(8,128)S(1)} %get-tuple-element.39), channel_id=1, source_target_pairs={{8,16},{24,32},{40,48},{56,64},{72,80},{88,96},{104,112},{120,128}... | collective-permute-start | bytes 393224 | tf_op jit(solution)/shard_map/ppermute | solution.py:472
  50.8 9.7 %collective-permute-start.4 = (bf16[128,256]{1,0:T(8,128)(2,1)S(1)}, bf16[128,256]{1,0:T(8,128)(2,1)S(1)}, u32[]{:S(2)}, u32[]{:S(2)}) collective-permute-start(bf16[128,256]{1,0:T(8,128)(2,1)S(1)} %shard_map.81.own), channel_id=1, source_target_pairs={{8,16},{24,32},{40,48},{56,64},{72,80},{88,96},{104,112},{120,128}... | collective-permute-start | bytes 196616 | tf_op jit(solution)/shard_map/ppermute | solution.py:472
  58.6 1.9 %collective-permute-start.3 = (bf16[128,256]{1,0:T(8,128)(2,1)S(1)}, bf16[128,256]{1,0:T(8,128)(2,1)S(1)}, u32[]{:S(2)}, u32[]{:S(2)}) collective-permute-start(bf16[128,256]{1,0:T(8,128)(2,1)S(1)} %shard_map.81.own), channel_id=1, source_target_pairs={{0,8},{8,0},{1,9},{9,1},{2,10},{10,2},{3,11},{11,3},{4,12},{12,4},... | collective-permute-start | bytes 196616 | tf_op jit(solution)/shard_map/ppermute | solution.py:462
  63.9 1.9 %collective-permute-start.5 = (bf16[1792,128]{1,0:T(8,128)(2,1)S(1)}, bf16[1792,128]{1,0:T(8,128)(2,1)S(1)}, u32[]{:S(2)}, u32[]{:S(2)}) collective-permute-start(bf16[1792,128]{1,0:T(8,128)(2,1)S(1)} %get-tuple-element.47), channel_id=1, source_target_pairs={{0,8},{8,0},{1,9},{9,1},{2,10},{10,2},{3,11},{11,3},{4,12},{12,4},... | collective-permute-start | bytes 1376264 | tf_op jit(solution)/shard_map/ppermute | solution.py:462
  66.6 25.2 %all-to-all-start.2 = ((bf16[16,112,128]{2,1,0:T(8,128)(2,1)}), bf16[16,112,128]{2,1,0:T(8,128)(2,1)S(1)}, u32[]{:S(2)}, u32[]{:S(2)}) async-start(bf16[16,112,128]{2,1,0:T(8,128)(2,1)} %shard_map.83), calls=%async_computation.2 | async-start | bytes 917504 | tf_op jit(solution)/shard_map/all_to_all | solution.py:457
  77.1 7.3 %collective-permute-start.6 = (bf16[2,2,128,256]{3,2,1,0:T(8,128)(2,1)S(1)}, bf16[2,2,128,256]{3,2,1,0:T(8,128)(2,1)S(1)}, u32[]{:S(2)}, u32[]{:S(2)}) collective-permute-start(bf16[2,2,128,256]{3,2,1,0:T(8,128)(2,1)S(1)} %get-tuple-element.53), channel_id=1, source_target_pairs={{0,2},{2,0},{4,6},{6,4},{1,3},{3,1},{5,7},{7,5},{8,10},{10,8},{12,... | collective-permute-start | bytes 786440 | tf_op jit(solution)/shard_map/ppermute | solution.py:462
  92.6 17.9 %all-to-all-start.3 = ((bf16[16,112,128]{2,1,0:T(8,128)(2,1)}), bf16[16,112,128]{2,1,0:T(8,128)(2,1)S(1)}, u32[]{:S(2)}, u32[]{:S(2)}) async-start(bf16[16,112,128]{2,1,0:T(8,128)(2,1)} %shard_map.85), calls=%async_computation.3 | async-start | bytes 917504 | tf_op jit(solution)/shard_map/all_to_all | solution.py:457
  97.0 5.1 %collective-permute-start.7 = (bf16[2,128,256]{2,1,0:T(8,128)(2,1)S(1)}, bf16[2,128,256]{2,1,0:T(8,128)(2,1)S(1)}, u32[]{:S(2)}, u32[]{:S(2)}) collective-permute-start(bf16[2,128,256]{2,1,0:T(8,128)(2,1)S(1)} %get-tuple-element.57), channel_id=1, source_target_pairs={{0,6},{2,4},{4,2},{6,0},{1,7},{3,5},{5,3},{7,1},{8,14},{10,12},{12... | collective-permute-start | bytes 393224 | tf_op jit(solution)/shard_map/ppermute | solution.py:467
  102.1 5.2 %collective-permute-start.8 = (bf16[128,256]{1,0:T(8,128)(2,1)S(1)}, bf16[128,256]{1,0:T(8,128)(2,1)S(1)}, u32[]{:S(2)}, u32[]{:S(2)}) collective-permute-start(bf16[128,256]{1,0:T(8,128)(2,1)S(1)} %get-tuple-element.59), channel_id=1, source_target_pairs={{0,1},{1,0},{2,3},{3,2},{4,5},{5,4},{6,7},{7,6},{8,9},{9,8},{10,11... | collective-permute-start | bytes 196616 | tf_op jit(solution)/shard_map/ppermute | solution.py:462
  110.5 4.6 %collective-permute-start.9 = (bf16[1792,128]{1,0:T(8,128)(2,1)S(1)}, bf16[1792,128]{1,0:T(8,128)(2,1)S(1)}, u32[]{:S(2)}, u32[]{:S(2)}) collective-permute-start(bf16[1792,128]{1,0:T(8,128)(2,1)S(1)} %bitcast.15), channel_id=1, source_target_pairs={{0,8},{8,0},{1,9},{9,1},{2,10},{10,2},{3,11},{11,3},{4,12},{12,4},... | collective-permute-start | bytes 1376264 | tf_op jit(solution)/shard_map/ppermute | solution.py:462

commit v6 on v5

--- a/solution.py
+++ b/solution.py
@@ -163,8 +163,10 @@
                 tall[row : row + 32, :] = v
 
 
-def first_conv(got, wide, low, high, within, across, field, part, window):
-    part[...] = got[:, X_ROWS + COT_ROWS :, :]
+def first_conv(got, wide, low, high, within, across, field, window):
+    for g in range(8):
+        at = ROWS + g * W_ROWS
+        within[at : at + W_ROWS, :] = got[g, X_ROWS + COT_ROWS :, :].astype(f32)
     parts = {}
     for h in (0, 1):
         for p in (0, 1):
@@ -202,18 +204,20 @@
     first_core = lax.axis_index("core") == 0
     low[...] = a
     high[...] = b
-    within[...] = jnp.where(first_core, b, a)
+    within[:ROWS, :] = jnp.where(first_core, b, a)
     across[...] = jnp.where(first_core, a, b)
 
 
-def gather_second(own, other, w2):
+def gather_second(got, within, w2):
     first_core = lax.axis_index("core") == 0
     for g in range(8):
         row = slice(g * 32, g * 32 + 32)
         blocks = []
         for b in range(4):
-            at = slice(b * 32, b * 32 + 32)
-            x, y = own[g, at, :].astype(f32), other[g, at, :].astype(f32)
+            at = X_ROWS + COT_ROWS + b * 32
+            x = got[g, at : at + 32, :].astype(f32)
+            at = ROWS + g * W_ROWS + b * 32
+            y = within[at : at + 32, :]
             early, late = jnp.where(first_core, x, y), jnp.where(first_core, y, x)
             w2[row, b * 128 : b * 128 + 128] = early.astype(bf16)
             w2[row, (b + 5) * 128 : (b + 6) * 128] = late.astype(bf16)
@@ -232,7 +236,7 @@
 
 def below_above(within, across):
     first_core = lax.axis_index("core") == 0
-    a, b = within[...], across[...]
+    a, b = within[: across.shape[0], :], across[...]
     return jnp.where(first_core, b, a), jnp.where(first_core, a, b)
 
 
@@ -505,16 +509,17 @@
     )
     got = exchange(packed, FLT)
     pair = shape((ROWS, 128), f32)
-    low, high, within, across, field, part = kernel_call(
+    with_filters = shape((ROWS + 8 * W_ROWS, 128), f32)
+    low, high, within, across, field = kernel_call(
         first_conv,
-        [pair, pair, pair, pair, shape((1024, 256), bf16), shape((8, W_ROWS, 128), bf16)],
+        [pair, pair, with_filters, pair, shape((1024, 256), bf16)],
         2 * 1024 * 768 * 384,
         got,
         wide,
         scratch=[pltpu.VMEM((1024, 768), bf16)],
     )
     across, within = next_chip(across), swapped(within)
-    (w2,) = kernel_call(gather_second, [shape((256, 1152), bf16)], 0, part, swapped(part))
+    (w2,) = kernel_call(gather_second, [shape((256, 1152), bf16)], 0, got, within)
     pre, partial = kernel_call(
         second_conv,
         [shape((512, 128), f32), shape((8, 512, 128), bf16)],

time: 117 us -> 116 us (level)
    ppermute x2, starting transfers between devices: 10.4 us -> 8.9 us  [next_chip(): return lax.ppermute(v, SP, pairs + [(b, a) for a, b in pairs])]
    ppermute x7 -> x6, starting transfers between devices: 6.17 us -> 6 us  [swapped(): return lax.ppermute(v, axis, [(i, i ^ 1) for i in range(n)])]
    ppermute x7 -> x6, waiting for transfers between devices: 12.4 us -> 12.5 us  [swapped(): return lax.ppermute(v, axis, [(i, i ^ 1) for i in range(n)])]
  transfers between devices with their start and end apart: 13 -> 12, of which waited for: 10 -> 10; matrix products, arithmetic and copies ran while one was open for 0% -> 0% of each run, Pallas kernels for 3% -> 3%
where the time goes in v6:
time: 116 us
  waiting for transfers between devices  44.8 us (39%)
  starting transfers between devices  38.6 us (33%)
  blocking collectives  17.4 us (15%)
  Pallas kernels  14.5 us (12%)
    all_to_all x3, waiting for transfers between devices, exchange(): return lax.all_to_all(v, axis, 0, 0, tiled=True)  23.5 us
    all_to_all x3, starting transfers between devices, exchange(): return lax.all_to_all(v, axis, 0, 0, tiled=True)  22.7 us
    all_to_all x1, blocking collectives, exchange(): return lax.all_to_all(v, axis, 0, 0, tiled=True)  17.4 us
    pallas_call x16, Pallas kernels, kernel_call(): pl.pallas_call(body, out_shape=outs, in_specs=[pl.BlockSpec(memory_space=...  14.5 us
    ppermute x6, waiting for transfers between devices, swapped(): return lax.ppermute(v, axis, [(i, i ^ 1) for i in range(n)])  12.5 us
    ppermute x2, starting transfers between devices, next_chip(): return lax.ppermute(v, SP, pairs + [(b, a) for a, b in pairs])  8.9 us
    ppermute x6, starting transfers between devices, swapped(): return lax.ppermute(v, axis, [(i, i ^ 1) for i in range(n)])  6 us
    ppermute x2, waiting for transfers between devices, next_chip(): return lax.ppermute(v, SP, pairs + [(b, a) for a, b in pairs])  4.66 us
  transfers between devices with their start and end apart: 12, of which 10 were waited for; matrix products, arithmetic and copies ran while one was open for 0% of the time, Pallas kernels for 3%

profile of v6, /device:TPU:1, one launch (start us, length us, event | category | flops | bytes accessed | tf_op | source)
XLA Modules:
  0.0 116.0 jit_solution(12325165650347269493)
XLA Ops:
  0.6 2.4 %shard_map.75 = bf16[8,416,128]{2,1,0:T(8,128)(2,1)} custom-call(bf16[128,256]{1,0:T(8,128)(2,1)} %bitcast.22, bf16[864,256]{1,0:T(8,128)(2,1)} %bitcast.20, bf16[1,4,4,256]{3,2,1,0:T(4,128)(2,1)} %cot_far.1), custom_call_target="tpu_custom_call" | custom-call | bytes 1368064 | tf_op jit(solution)/shard_map/pallas_call | solution.py:32
  3.0 7.5 %all-to-all-start = ((bf16[8,416,128]{2,1,0:T(8,128)(2,1)}), bf16[8,416,128]{2,1,0:T(8,128)(2,1)S(1)}, u32[]{:S(2)}, u32[]{:S(2)}) async-start(bf16[8,416,128]{2,1,0:T(8,128)(2,1)} %shard_map.75), calls=%async_computation | async-start | bytes 1703936 | tf_op jit(solution)/shard_map/all_to_all | solution.py:461
  10.6 13.6 %all-to-all-done.got = bf16[8,416,128]{2,1,0:T(8,128)(2,1)S(1)} async-done(((bf16[8,416,128]{2,1,0:T(8,128)(2,1)}), bf16[8,416,128]{2,1,0:T(8,128)(2,1)S(1)}, u32[]{:S(2)}, u32[]{:S(2)}) %all-to-all-start) | async-done | bytes 852000 | tf_op jit(solution)/shard_map/all_to_all | solution.py:461
  24.2 1.5 %shard_map.77 = (f32[256,128]{1,0:T(8,128)S(1)}, f32[256,128]{1,0:T(8,128)S(1)}, f32[1280,128]{1,0:T(8,128)S(1)}, f32[256,128]{1,0:T(8,128)S(1)}, bf16[1024,256]{1,0:T(8,128)(2,1)S(1)}) custom-call(bf16[8,416,128]{2,1,0:T(8,128)(2,1)S(1)} %all-to-all-done.got, bf16[384,768]{1,0:T(8,128)(2,1)S(1)} %get-tuple-element.34.wide), custom_call_target="tpu_custom_call" | custom-call | flops 603979776 | bytes 3014656 | tf_op jit(solution)/shard_map/pallas_call | solution.py:32
  25.7 1.3 %collective-permute-start = (f32[1280,128]{1,0:T(8,128)S(1)}, f32[1280,128]{1,0:T(8,128)S(1)}, u32[]{:S(2)}, u32[]{:S(2)}) collective-permute-start(f32[1280,128]{1,0:T(8,128)S(1)} %get-tuple-element.37), channel_id=1, source_target_pairs={{0,8},{8,0},{1,9},{9,1},{2,10},{10,2},{3,11},{11,3},{4,12},{12,4},... | collective-permute-start | bytes 1966088 | tf_op jit(solution)/shard_map/ppermute | solution.py:466
  26.9 2.2 %collective-permute-start.1 = (f32[256,128]{1,0:T(8,128)S(1)}, f32[256,128]{1,0:T(8,128)S(1)}, u32[]{:S(2)}, u32[]{:S(2)}) collective-permute-start(f32[256,128]{1,0:T(8,128)S(1)} %get-tuple-element.38), channel_id=1, source_target_pairs={{8,16},{24,32},{40,48},{56,64},{72,80},{88,96},{104,112},{120,128}... | collective-permute-start | bytes 393224 | tf_op jit(solution)/shard_map/ppermute | solution.py:476
  29.2 0.2 shard_map.78.w2
  29.3 3.9 %collective-permute-done.1.across = f32[256,128]{1,0:T(8,128)S(1)} collective-permute-done((f32[256,128]{1,0:T(8,128)S(1)}, f32[256,128]{1,0:T(8,128)S(1)}, u32[]{:S(2)}, u32[]{:S(2)}) %collective-permute-start.1) | collective-permute-done | bytes 131104 | tf_op jit(solution)/shard_map/ppermute | solution.py:476
  33.2 0.6 shard_map.79
  33.9 17.4 %all_to_all.20.parts = bf16[8,512,128]{2,1,0:T(8,128)(2,1)S(1)} all-to-all(bf16[8,512,128]{2,1,0:T(8,128)(2,1)S(1)} %get-tuple-element.39), channel_id=1, replica_groups=mesh['sp_z'=8,'sp_y'=2,'core'=2,'flt_x'=4,'flt_y'=2] {'flt_x','flt_y'}, dimensions={0} | all-to-all | bytes 2097152 | tf_op jit(solution)/shard_map/all_to_all | solution.py:461
  51.3 6.7 %collective-permute-start.3 = (bf16[128,256]{1,0:T(8,128)(2,1)S(1)}, bf16[128,256]{1,0:T(8,128)(2,1)S(1)}, u32[]{:S(2)}, u32[]{:S(2)}) collective-permute-start(bf16[128,256]{1,0:T(8,128)(2,1)S(1)} %shard_map.81.own), channel_id=1, source_target_pairs={{8,16},{24,32},{40,48},{56,64},{72,80},{88,96},{104,112},{120,128}... | collective-permute-start | bytes 196616 | tf_op jit(solution)/shard_map/ppermute | solution.py:476
  58.1 1.1 shard_map.80
  59.2 0.8 collective-permute-done.3.across
  60.0 3.3 %shard_map.82 = (bf16[1024,1152]{1,0:T(8,128)(2,1)S(1)}, f32[1792,128]{1,0:T(8,128)S(1)}, bf16[1792,128]{1,0:T(8,128)(2,1)S(1)}) custom-call(bf16[128,256]{1,0:T(8,128)(2,1)S(1)} %shard_map.81.own, bf16[128,256]{1,0:T(8,128)(2,1)S(1)} %collective-permute-done.2.within, bf16[128,256]{1,0:T(8,128)(2,1)S(1)} %collective-permute-done.3.across, ...), custom_call_target="tpu_custom_call" | custom-call | flops 905969664 | bytes 5832704 | tf_op jit(solution)/shard_map/pallas_call | solution.py:32
  63.4 0.9 shard_map.84
  64.3 0.9 collective-permute-done.4.came
  65.2 0.8 shard_map.83
  66.1 10.9 %all-to-all-start.2 = ((bf16[16,112,128]{2,1,0:T(8,128)(2,1)}), bf16[16,112,128]{2,1,0:T(8,128)(2,1)S(1)}, u32[]{:S(2)}, u32[]{:S(2)}) async-start(bf16[16,112,128]{2,1,0:T(8,128)(2,1)} %shard_map.83), calls=%async_computation.2 | async-start | bytes 917504 | tf_op jit(solution)/shard_map/all_to_all | solution.py:461
  77.1 7.2 %collective-permute-done.5.came = bf16[2,2,128,256]{3,2,1,0:T(8,128)(2,1)S(1)} collective-permute-done((bf16[2,2,128,256]{3,2,1,0:T(8,128)(2,1)S(1)}, bf16[2,2,128,256]{3,2,1,0:T(8,128)(2,1)S(1)}, u32[]{:S(2)}, u32[]{:S(2)}) %collective-permute-start.5) | collective-permute-done | bytes 262176 | tf_op jit(solution)/shard_map/ppermute | solution.py:466
  84.3 7.4 %all-to-all-done.2.parts = bf16[16,112,128]{2,1,0:T(8,128)(2,1)S(1)} async-done(((bf16[16,112,128]{2,1,0:T(8,128)(2,1)}), bf16[16,112,128]{2,1,0:T(8,128)(2,1)S(1)}, u32[]{:S(2)}, u32[]{:S(2)}) %all-to-all-start.2) | async-done | bytes 458784 | tf_op jit(solution)/shard_map/all_to_all | solution.py:461
  91.7 0.8 shard_map.85
  92.6 4.3 %all-to-all-start.3 = ((bf16[16,112,128]{2,1,0:T(8,128)(2,1)}), bf16[16,112,128]{2,1,0:T(8,128)(2,1)S(1)}, u32[]{:S(2)}, u32[]{:S(2)}) async-start(bf16[16,112,128]{2,1,0:T(8,128)(2,1)} %shard_map.85), calls=%async_computation.3 | async-start | bytes 917504 | tf_op jit(solution)/shard_map/all_to_all | solution.py:461
  96.9 1.0 collective-permute-start.6
  97.8 4.2 %collective-permute-done.6.came = bf16[2,128,256]{2,1,0:T(8,128)(2,1)S(1)} collective-permute-done((bf16[2,128,256]{2,1,0:T(8,128)(2,1)S(1)}, bf16[2,128,256]{2,1,0:T(8,128)(2,1)S(1)}, u32[]{:S(2)}, u32[]{:S(2)}) %collective-permute-start.6) | collective-permute-done | bytes 131104 | tf_op jit(solution)/shard_map/ppermute | solution.py:471
  102.0 1.3 %collective-permute-start.7 = (bf16[128,256]{1,0:T(8,128)(2,1)S(1)}, bf16[128,256]{1,0:T(8,128)(2,1)S(1)}, u32[]{:S(2)}, u32[]{:S(2)}) collective-permute-start(bf16[128,256]{1,0:T(8,128)(2,1)S(1)} %get-tuple-element.57), channel_id=1, source_target_pairs={{0,1},{1,0},{2,3},{3,2},{4,5},{5,4},{6,7},{7,6},{8,9},{9,8},{10,11... | collective-permute-start | bytes 196616 | tf_op jit(solution)/shard_map/ppermute | solution.py:466
  103.3 3.9 %collective-permute-done.7.came = bf16[128,256]{1,0:T(8,128)(2,1)S(1)} collective-permute-done((bf16[128,256]{1,0:T(8,128)(2,1)S(1)}, bf16[128,256]{1,0:T(8,128)(2,1)S(1)}, u32[]{:S(2)}, u32[]{:S(2)}) %collective-permute-start.7) | collective-permute-done | bytes 65568 | tf_op jit(solution)/shard_map/ppermute | solution.py:466
  107.2 0.7 shard_map.88
  107.8 2.6 %all-to-all-done.3 = bf16[16,112,128]{2,1,0:T(8,128)(2,1)S(1)} async-done(((bf16[16,112,128]{2,1,0:T(8,128)(2,1)}), bf16[16,112,128]{2,1,0:T(8,128)(2,1)S(1)}, u32[]{:S(2)}, u32[]{:S(2)}) %all-to-all-start.3) | async-done | bytes 458784 | tf_op jit(solution)/shard_map/all_to_all | solution.py:461
  110.4 3.2 %collective-permute-start.8 = (bf16[1792,128]{1,0:T(8,128)(2,1)S(1)}, bf16[1792,128]{1,0:T(8,128)(2,1)S(1)}, u32[]{:S(2)}, u32[]{:S(2)}) collective-permute-start(bf16[1792,128]{1,0:T(8,128)(2,1)S(1)} %bitcast.15), channel_id=1, source_target_pairs={{0,8},{8,0},{1,9},{9,1},{2,10},{10,2},{3,11},{11,3},{4,12},{12,4},... | collective-permute-start | bytes 1376264 | tf_op jit(solution)/shard_map/ppermute | solution.py:466
  113.6 1.0 shard_map.89
  114.6 0.5 collective-permute-done.8.rows
  115.1 1.0 shard_map.90
  (11 shorter events, 0.6 us)
Async XLA Ops:
  0.6 9.9 %copy-start = (bf16[32,3,3,3,256]{4,0,3,2,1:T(8,128)(2,1)S(1)}, bf16[32,3,3,3,256]{4,0,3,2,1:T(8,128)(2,1)}, u32[]{:S(2)}) copy-start(bf16[32,3,3,3,256]{4,0,3,2,1:T(8,128)(2,1)} %param.5) | copy-start | bytes 1327108
  3.0 21.2 %all-to-all-start = ((bf16[8,416,128]{2,1,0:T(8,128)(2,1)}), bf16[8,416,128]{2,1,0:T(8,128)(2,1)S(1)}, u32[]{:S(2)}, u32[]{:S(2)}) async-start(bf16[8,416,128]{2,1,0:T(8,128)(2,1)} %shard_map.75), calls=%async_computation | async-start | bytes 1703936 | tf_op jit(solution)/shard_map/all_to_all | solution.py:461
  25.7 3.5 %collective-permute-start = (f32[1280,128]{1,0:T(8,128)S(1)}, f32[1280,128]{1,0:T(8,128)S(1)}, u32[]{:S(2)}, u32[]{:S(2)}) collective-permute-start(f32[1280,128]{1,0:T(8,128)S(1)} %get-tuple-element.37), channel_id=1, source_target_pairs={{0,8},{8,0},{1,9},{9,1},{2,10},{10,2},{3,11},{11,3},{4,12},{12,4},... | collective-permute-start | bytes 1966088 | tf_op jit(solution)/shard_map/ppermute | solution.py:466
  26.9 6.3 %collective-permute-start.1 = (f32[256,128]{1,0:T(8,128)S(1)}, f32[256,128]{1,0:T(8,128)S(1)}, u32[]{:S(2)}, u32[]{:S(2)}) collective-permute-start(f32[256,128]{1,0:T(8,128)S(1)} %get-tuple-element.38), channel_id=1, source_target_pairs={{8,16},{24,32},{40,48},{56,64},{72,80},{88,96},{104,112},{120,128}... | collective-permute-start | bytes 393224 | tf_op jit(solution)/shard_map/ppermute | solution.py:476
  51.3 8.6 %collective-permute-start.3 = (bf16[128,256]{1,0:T(8,128)(2,1)S(1)}, bf16[128,256]{1,0:T(8,128)(2,1)S(1)}, u32[]{:S(2)}, u32[]{:S(2)}) collective-permute-start(bf16[128,256]{1,0:T(8,128)(2,1)S(1)} %shard_map.81.own), channel_id=1, source_target_pairs={{8,16},{24,32},{40,48},{56,64},{72,80},{88,96},{104,112},{120,128}... | collective-permute-start | bytes 196616 | tf_op jit(solution)/shard_map/ppermute | solution.py:476
  58.0 1.9 %collective-permute-start.2 = (bf16[128,256]{1,0:T(8,128)(2,1)S(1)}, bf16[128,256]{1,0:T(8,128)(2,1)S(1)}, u32[]{:S(2)}, u32[]{:S(2)}) collective-permute-start(bf16[128,256]{1,0:T(8,128)(2,1)S(1)} %shard_map.81.own), channel_id=1, source_target_pairs={{0,8},{8,0},{1,9},{9,1},{2,10},{10,2},{3,11},{11,3},{4,12},{12,4},... | collective-permute-start | bytes 196616 | tf_op jit(solution)/shard_map/ppermute | solution.py:466
  63.3 1.9 %collective-permute-start.4 = (bf16[1792,128]{1,0:T(8,128)(2,1)S(1)}, bf16[1792,128]{1,0:T(8,128)(2,1)S(1)}, u32[]{:S(2)}, u32[]{:S(2)}) collective-permute-start(bf16[1792,128]{1,0:T(8,128)(2,1)S(1)} %get-tuple-element.45), channel_id=1, source_target_pairs={{0,8},{8,0},{1,9},{9,1},{2,10},{10,2},{3,11},{11,3},{4,12},{12,4},... | collective-permute-start | bytes 1376264 | tf_op jit(solution)/shard_map/ppermute | solution.py:466
  66.1 25.6 %all-to-all-start.2 = ((bf16[16,112,128]{2,1,0:T(8,128)(2,1)}), bf16[16,112,128]{2,1,0:T(8,128)(2,1)S(1)}, u32[]{:S(2)}, u32[]{:S(2)}) async-start(bf16[16,112,128]{2,1,0:T(8,128)(2,1)} %shard_map.83), calls=%async_computation.2 | async-start | bytes 917504 | tf_op jit(solution)/shard_map/all_to_all | solution.py:461
  77.0 7.3 %collective-permute-start.5 = (bf16[2,2,128,256]{3,2,1,0:T(8,128)(2,1)S(1)}, bf16[2,2,128,256]{3,2,1,0:T(8,128)(2,1)S(1)}, u32[]{:S(2)}, u32[]{:S(2)}) collective-permute-start(bf16[2,2,128,256]{3,2,1,0:T(8,128)(2,1)S(1)} %get-tuple-element.51), channel_id=1, source_target_pairs={{0,2},{2,0},{4,6},{6,4},{1,3},{3,1},{5,7},{7,5},{8,10},{10,8},{12,... | collective-permute-start | bytes 786440 | tf_op jit(solution)/shard_map/ppermute | solution.py:466
  92.6 17.9 %all-to-all-start.3 = ((bf16[16,112,128]{2,1,0:T(8,128)(2,1)}), bf16[16,112,128]{2,1,0:T(8,128)(2,1)S(1)}, u32[]{:S(2)}, u32[]{:S(2)}) async-start(bf16[16,112,128]{2,1,0:T(8,128)(2,1)} %shard_map.85), calls=%async_computation.3 | async-start | bytes 917504 | tf_op jit(solution)/shard_map/all_to_all | solution.py:461
  96.9 5.1 %collective-permute-start.6 = (bf16[2,128,256]{2,1,0:T(8,128)(2,1)S(1)}, bf16[2,128,256]{2,1,0:T(8,128)(2,1)S(1)}, u32[]{:S(2)}, u32[]{:S(2)}) collective-permute-start(bf16[2,128,256]{2,1,0:T(8,128)(2,1)S(1)} %get-tuple-element.55), channel_id=1, source_target_pairs={{0,6},{2,4},{4,2},{6,0},{1,7},{3,5},{5,3},{7,1},{8,14},{10,12},{12... | collective-permute-start | bytes 393224 | tf_op jit(solution)/shard_map/ppermute | solution.py:471
  102.0 5.2 %collective-permute-start.7 = (bf16[128,256]{1,0:T(8,128)(2,1)S(1)}, bf16[128,256]{1,0:T(8,128)(2,1)S(1)}, u32[]{:S(2)}, u32[]{:S(2)}) collective-permute-start(bf16[128,256]{1,0:T(8,128)(2,1)S(1)} %get-tuple-element.57), channel_id=1, source_target_pairs={{0,1},{1,0},{2,3},{3,2},{4,5},{5,4},{6,7},{7,6},{8,9},{9,8},{10,11... | collective-permute-start | bytes 196616 | tf_op jit(solution)/shard_map/ppermute | solution.py:466
  110.4 4.6 %collective-permute-start.8 = (bf16[1792,128]{1,0:T(8,128)(2,1)S(1)}, bf16[1792,128]{1,0:T(8,128)(2,1)S(1)}, u32[]{:S(2)}, u32[]{:S(2)}) collective-permute-start(bf16[1792,128]{1,0:T(8,128)(2,1)S(1)} %bitcast.15), channel_id=1, source_target_pairs={{0,8},{8,0},{1,9},{9,1},{2,10},{10,2},{3,11},{11,3},{4,12},{12,4},... | collective-permute-start | bytes 1376264 | tf_op jit(solution)/shard_map/ppermute | solution.py:466

commit v7 on v5

--- a/solution.py
+++ b/solution.py
@@ -546,6 +546,9 @@
         scratch=[pltpu.VMEM((ROWS, 128), f32)],
     )
     came = swapped(sent)
+    chunk = shape((16, GRAD_PAD // 16, 128), bf16)
+    (mine,) = kernel_call(add_core, [chunk], 0, kept, came)
+    mine, window = lax.optimization_barrier((mine, window))
     kept_in, sent_in = kernel_call(
         input_grad,
         [shape((2, 2, 128, 256), f32), shape((2, 2, 128, 256), bf16)],
@@ -554,9 +557,6 @@
         tall,
         scratch=[pltpu.VMEM((4, 2, 128, 256), f32)],
     )
-    chunk = shape((16, GRAD_PAD // 16, 128), bf16)
-    (mine,) = kernel_call(add_core, [chunk], 0, kept, came)
-    mine, sent_in = lax.optimization_barrier((mine, sent_in))
     came_in = swapped(sent_in, "flt_x")
     (mine,) = kernel_call(add_chips, [chunk], 0, exchange(mine, CHIPS))
     kept_in, sent_in = kernel_call(

time: 117 us -> 117 us (level)
  no operation moved by 1% of the time
where the time goes in v7:
time: 117 us; the launch traced here: 116 us
  waiting for transfers between devices  44.4 us (38%)
  starting transfers between devices  39.7 us (34%)
  blocking collectives  16.7 us (14%)
  Pallas kernels  14.5 us (12%)
    all_to_all x3, waiting for transfers between devices, exchange(): return lax.all_to_all(v, axis, 0, 0, tiled=True)  22.6 us
    all_to_all x3, starting transfers between devices, exchange(): return lax.all_to_all(v, axis, 0, 0, tiled=True)  22.3 us
    all_to_all x1, blocking collectives, exchange(): return lax.all_to_all(v, axis, 0, 0, tiled=True)  16.7 us
    pallas_call x16, Pallas kernels, kernel_call(): pl.pallas_call(body, out_shape=outs, in_specs=[pl.BlockSpec(memory_space=...  14.5 us
    ppermute x7, waiting for transfers between devices, swapped(): return lax.ppermute(v, axis, [(i, i ^ 1) for i in range(n)])  13.3 us
    ppermute x2, starting transfers between devices, next_chip(): return lax.ppermute(v, SP, pairs + [(b, a) for a, b in pairs])  10.4 us
    ppermute x7, starting transfers between devices, swapped(): return lax.ppermute(v, axis, [(i, i ^ 1) for i in range(n)])  6.17 us
    ppermute x2, waiting for transfers between devices, next_chip(): return lax.ppermute(v, SP, pairs + [(b, a) for a, b in pairs])  4.24 us
  transfers between devices with their start and end apart: 13, of which 10 were waited for; matrix products, arithmetic and copies ran while one was open for 0% of the time, Pallas kernels for 3%

profile of v7, /device:TPU:1, one launch (start us, length us, event | category | flops | bytes accessed | tf_op | source)
XLA Modules:
  0.0 116.1 jit_solution(10699023269757322833)
XLA Ops:
  0.6 2.4 %shard_map.75 = bf16[8,416,128]{2,1,0:T(8,128)(2,1)} custom-call(bf16[128,256]{1,0:T(8,128)(2,1)} %bitcast.22, bf16[864,256]{1,0:T(8,128)(2,1)} %bitcast.20, bf16[1,4,4,256]{3,2,1,0:T(4,128)(2,1)} %cot_far.1), custom_call_target="tpu_custom_call" | custom-call | bytes 1368064 | tf_op jit(solution)/shard_map/pallas_call | solution.py:32
  3.0 7.5 %all-to-all-start = ((bf16[8,416,128]{2,1,0:T(8,128)(2,1)}), bf16[8,416,128]{2,1,0:T(8,128)(2,1)S(1)}, u32[]{:S(2)}, u32[]{:S(2)}) async-start(bf16[8,416,128]{2,1,0:T(8,128)(2,1)} %shard_map.75), calls=%async_computation | async-start | bytes 1703936 | tf_op jit(solution)/shard_map/all_to_all | solution.py:457
  10.6 13.6 %all-to-all-done.got = bf16[8,416,128]{2,1,0:T(8,128)(2,1)S(1)} async-done(((bf16[8,416,128]{2,1,0:T(8,128)(2,1)}), bf16[8,416,128]{2,1,0:T(8,128)(2,1)S(1)}, u32[]{:S(2)}, u32[]{:S(2)}) %all-to-all-start) | async-done | bytes 852000 | tf_op jit(solution)/shard_map/all_to_all | solution.py:457
  24.2 1.5 %shard_map.77 = (f32[256,128]{1,0:T(8,128)S(1)}, f32[256,128]{1,0:T(8,128)S(1)}, f32[256,128]{1,0:T(8,128)S(1)}, f32[256,128]{1,0:T(8,128)S(1)}, bf16[1024,256]{...) custom-call(bf16[8,416,128]{2,1,0:T(8,128)(2,1)S(1)} %all-to-all-done.got, bf16[384,768]{1,0:T(8,128)(2,1)S(1)} %get-tuple-element.35.wide), custom_call_target="tpu_custom_call" | custom-call | flops 603979776 | bytes 2752512 | tf_op jit(solution)/shard_map/pallas_call | solution.py:32
  25.7 1.3 %collective-permute-start.2 = (bf16[8,128,128]{2,1,0:T(8,128)(2,1)S(1)}, bf16[8,128,128]{2,1,0:T(8,128)(2,1)S(1)}, u32[]{:S(2)}, u32[]{:S(2)}) collective-permute-start(bf16[8,128,128]{2,1,0:T(8,128)(2,1)S(1)} %get-tuple-element.40.own), channel_id=1, source_target_pairs={{0,8},{8,0},{1,9},{9,1},{2,10},{10,2},{3,11},{11,3},{4,12},{12,4},... | collective-permute-start | bytes 786440 | tf_op jit(solution)/shard_map/ppermute | solution.py:462
  27.0 2.6 %collective-permute-start.1 = (f32[256,128]{1,0:T(8,128)S(1)}, f32[256,128]{1,0:T(8,128)S(1)}, u32[]{:S(2)}, u32[]{:S(2)}) collective-permute-start(f32[256,128]{1,0:T(8,128)S(1)} %get-tuple-element.39), channel_id=1, source_target_pairs={{8,16},{24,32},{40,48},{56,64},{72,80},{88,96},{104,112},{120,128}... | collective-permute-start | bytes 393224 | tf_op jit(solution)/shard_map/ppermute | solution.py:472
  29.6 0.2 shard_map.78.w2
  29.8 3.5 %collective-permute-done.1.across = f32[256,128]{1,0:T(8,128)S(1)} collective-permute-done((f32[256,128]{1,0:T(8,128)S(1)}, f32[256,128]{1,0:T(8,128)S(1)}, u32[]{:S(2)}, u32[]{:S(2)}) %collective-permute-start.1) | collective-permute-done | bytes 131104 | tf_op jit(solution)/shard_map/ppermute | solution.py:472
  33.3 0.6 shard_map.79
  33.9 16.7 %all_to_all.20.parts = bf16[8,512,128]{2,1,0:T(8,128)(2,1)S(1)} all-to-all(bf16[8,512,128]{2,1,0:T(8,128)(2,1)S(1)} %get-tuple-element.41), channel_id=1, replica_groups=mesh['sp_z'=8,'sp_y'=2,'core'=2,'flt_x'=4,'flt_y'=2] {'flt_x','flt_y'}, dimensions={0} | all-to-all | bytes 2097152 | tf_op jit(solution)/shard_map/all_to_all | solution.py:457
  50.8 7.8 %collective-permute-start.4 = (bf16[128,256]{1,0:T(8,128)(2,1)S(1)}, bf16[128,256]{1,0:T(8,128)(2,1)S(1)}, u32[]{:S(2)}, u32[]{:S(2)}) collective-permute-start(bf16[128,256]{1,0:T(8,128)(2,1)S(1)} %shard_map.81.own), channel_id=1, source_target_pairs={{8,16},{24,32},{40,48},{56,64},{72,80},{88,96},{104,112},{120,128}... | collective-permute-start | bytes 196616 | tf_op jit(solution)/shard_map/ppermute | solution.py:472
  58.7 1.1 shard_map.80
  59.7 0.8 collective-permute-done.4.across
  60.5 3.3 %shard_map.82 = (bf16[1024,1152]{1,0:T(8,128)(2,1)S(1)}, f32[1792,128]{1,0:T(8,128)S(1)}, bf16[1792,128]{1,0:T(8,128)(2,1)S(1)}) custom-call(bf16[128,256]{1,0:T(8,128)(2,1)S(1)} %shard_map.81.own, bf16[128,256]{1,0:T(8,128)(2,1)S(1)} %collective-permute-done.3.within, bf16[128,256]{1,0:T(8,128)(2,1)S(1)} %collective-permute-done.4.across, ...), custom_call_target="tpu_custom_call" | custom-call | flops 905969664 | bytes 5832704 | tf_op jit(solution)/shard_map/pallas_call | solution.py:32
  64.0 1.8 %collective-permute-done.5.came = bf16[1792,128]{1,0:T(8,128)(2,1)S(1)} collective-permute-done((bf16[1792,128]{1,0:T(8,128)(2,1)S(1)}, bf16[1792,128]{1,0:T(8,128)(2,1)S(1)}, u32[]{:S(2)}, u32[]{:S(2)}) %collective-permute-start.5) | collective-permute-done | bytes 458784 | tf_op jit(solution)/shard_map/ppermute | solution.py:462
  65.8 0.8 shard_map.83
  66.6 10.5 %all-to-all-start.2 = ((bf16[16,112,128]{2,1,0:T(8,128)(2,1)}), bf16[16,112,128]{2,1,0:T(8,128)(2,1)S(1)}, u32[]{:S(2)}, u32[]{:S(2)}) async-start(bf16[16,112,128]{2,1,0:T(8,128)(2,1)} %shard_map.83), calls=%async_computation.2 | async-start | bytes 917504 | tf_op jit(solution)/shard_map/all_to_all | solution.py:457
  77.1 0.9 shard_map.85
  78.1 7.2 %collective-permute-done.6.came = bf16[2,2,128,256]{3,2,1,0:T(8,128)(2,1)S(1)} collective-permute-done((bf16[2,2,128,256]{3,2,1,0:T(8,128)(2,1)S(1)}, bf16[2,2,128,256]{3,2,1,0:T(8,128)(2,1)S(1)}, u32[]{:S(2)}, u32[]{:S(2)}) %collective-permute-start.6) | collective-permute-done | bytes 262176 | tf_op jit(solution)/shard_map/ppermute | solution.py:462
  85.3 6.5 %all-to-all-done.2.parts = bf16[16,112,128]{2,1,0:T(8,128)(2,1)S(1)} async-done(((bf16[16,112,128]{2,1,0:T(8,128)(2,1)}), bf16[16,112,128]{2,1,0:T(8,128)(2,1)S(1)}, u32[]{:S(2)}, u32[]{:S(2)}) %all-to-all-start.2) | async-done | bytes 458784 | tf_op jit(solution)/shard_map/all_to_all | solution.py:457
  91.8 0.8 shard_map.84
  92.6 4.3 %all-to-all-start.3 = ((bf16[16,112,128]{2,1,0:T(8,128)(2,1)}), bf16[16,112,128]{2,1,0:T(8,128)(2,1)S(1)}, u32[]{:S(2)}, u32[]{:S(2)}) async-start(bf16[16,112,128]{2,1,0:T(8,128)(2,1)} %shard_map.84), calls=%async_computation.3 | async-start | bytes 917504 | tf_op jit(solution)/shard_map/all_to_all | solution.py:457
  97.0 0.9 collective-permute-start.7
  97.9 4.2 %collective-permute-done.7.came = bf16[2,128,256]{2,1,0:T(8,128)(2,1)S(1)} collective-permute-done((bf16[2,128,256]{2,1,0:T(8,128)(2,1)S(1)}, bf16[2,128,256]{2,1,0:T(8,128)(2,1)S(1)}, u32[]{:S(2)}, u32[]{:S(2)}) %collective-permute-start.7) | collective-permute-done | bytes 131104 | tf_op jit(solution)/shard_map/ppermute | solution.py:467
  102.1 1.3 %collective-permute-start.8 = (bf16[128,256]{1,0:T(8,128)(2,1)S(1)}, bf16[128,256]{1,0:T(8,128)(2,1)S(1)}, u32[]{:S(2)}, u32[]{:S(2)}) collective-permute-start(bf16[128,256]{1,0:T(8,128)(2,1)S(1)} %get-tuple-element.59), channel_id=1, source_target_pairs={{0,1},{1,0},{2,3},{3,2},{4,5},{5,4},{6,7},{7,6},{8,9},{9,8},{10,11... | collective-permute-start | bytes 196616 | tf_op jit(solution)/shard_map/ppermute | solution.py:462
  103.4 3.9 %collective-permute-done.8.came = bf16[128,256]{1,0:T(8,128)(2,1)S(1)} collective-permute-done((bf16[128,256]{1,0:T(8,128)(2,1)S(1)}, bf16[128,256]{1,0:T(8,128)(2,1)S(1)}, u32[]{:S(2)}, u32[]{:S(2)}) %collective-permute-start.8) | collective-permute-done | bytes 65568 | tf_op jit(solution)/shard_map/ppermute | solution.py:462
  107.3 0.7 shard_map.88
  108.0 2.6 %all-to-all-done.3 = bf16[16,112,128]{2,1,0:T(8,128)(2,1)S(1)} async-done(((bf16[16,112,128]{2,1,0:T(8,128)(2,1)}), bf16[16,112,128]{2,1,0:T(8,128)(2,1)S(1)}, u32[]{:S(2)}, u32[]{:S(2)}) %all-to-all-start.3) | async-done | bytes 458784 | tf_op jit(solution)/shard_map/all_to_all | solution.py:457
  110.5 3.2 %collective-permute-start.9 = (bf16[1792,128]{1,0:T(8,128)(2,1)S(1)}, bf16[1792,128]{1,0:T(8,128)(2,1)S(1)}, u32[]{:S(2)}, u32[]{:S(2)}) collective-permute-start(bf16[1792,128]{1,0:T(8,128)(2,1)S(1)} %bitcast.15), channel_id=1, source_target_pairs={{0,8},{8,0},{1,9},{9,1},{2,10},{10,2},{3,11},{11,3},{4,12},{12,4},... | collective-permute-start | bytes 1376264 | tf_op jit(solution)/shard_map/ppermute | solution.py:462
  113.7 1.0 shard_map.89
  114.7 0.5 collective-permute-done.9.rows
  115.2 1.0 shard_map.90
  (13 shorter events, 0.7 us)
Async XLA Ops:
  0.6 9.9 %copy-start = (bf16[32,3,3,3,256]{4,0,3,2,1:T(8,128)(2,1)S(1)}, bf16[32,3,3,3,256]{4,0,3,2,1:T(8,128)(2,1)}, u32[]{:S(2)}) copy-start(bf16[32,3,3,3,256]{4,0,3,2,1:T(8,128)(2,1)} %param.5) | copy-start | bytes 1327108
  3.0 21.2 %all-to-all-start = ((bf16[8,416,128]{2,1,0:T(8,128)(2,1)}), bf16[8,416,128]{2,1,0:T(8,128)(2,1)S(1)}, u32[]{:S(2)}, u32[]{:S(2)}) async-start(bf16[8,416,128]{2,1,0:T(8,128)(2,1)} %shard_map.75), calls=%async_computation | async-start | bytes 1703936 | tf_op jit(solution)/shard_map/all_to_all | solution.py:457
  25.7 4.0 %collective-permute-start.2 = (bf16[8,128,128]{2,1,0:T(8,128)(2,1)S(1)}, bf16[8,128,128]{2,1,0:T(8,128)(2,1)S(1)}, u32[]{:S(2)}, u32[]{:S(2)}) collective-permute-start(bf16[8,128,128]{2,1,0:T(8,128)(2,1)S(1)} %get-tuple-element.40.own), channel_id=1, source_target_pairs={{0,8},{8,0},{1,9},{9,1},{2,10},{10,2},{3,11},{11,3},{4,12},{12,4},... | collective-permute-start | bytes 786440 | tf_op jit(solution)/shard_map/ppermute | solution.py:462
  26.9 2.9 %collective-permute-start = (f32[256,128]{1,0:T(8,128)S(1)}, f32[256,128]{1,0:T(8,128)S(1)}, u32[]{:S(2)}, u32[]{:S(2)}) collective-permute-start(f32[256,128]{1,0:T(8,128)S(1)} %get-tuple-element.38), channel_id=1, source_target_pairs={{0,8},{8,0},{1,9},{9,1},{2,10},{10,2},{3,11},{11,3},{4,12},{12,4},... | collective-permute-start | bytes 393224 | tf_op jit(solution)/shard_map/ppermute | solution.py:462
  27.0 6.3 %collective-permute-start.1 = (f32[256,128]{1,0:T(8,128)S(1)}, f32[256,128]{1,0:T(8,128)S(1)}, u32[]{:S(2)}, u32[]{:S(2)}) collective-permute-start(f32[256,128]{1,0:T(8,128)S(1)} %get-tuple-element.39), channel_id=1, source_target_pairs={{8,16},{24,32},{40,48},{56,64},{72,80},{88,96},{104,112},{120,128}... | collective-permute-start | bytes 393224 | tf_op jit(solution)/shard_map/ppermute | solution.py:472
  50.8 9.7 %collective-permute-start.4 = (bf16[128,256]{1,0:T(8,128)(2,1)S(1)}, bf16[128,256]{1,0:T(8,128)(2,1)S(1)}, u32[]{:S(2)}, u32[]{:S(2)}) collective-permute-start(bf16[128,256]{1,0:T(8,128)(2,1)S(1)} %shard_map.81.own), channel_id=1, source_target_pairs={{8,16},{24,32},{40,48},{56,64},{72,80},{88,96},{104,112},{120,128}... | collective-permute-start | bytes 196616 | tf_op jit(solution)/shard_map/ppermute | solution.py:472
  58.6 1.9 %collective-permute-start.3 = (bf16[128,256]{1,0:T(8,128)(2,1)S(1)}, bf16[128,256]{1,0:T(8,128)(2,1)S(1)}, u32[]{:S(2)}, u32[]{:S(2)}) collective-permute-start(bf16[128,256]{1,0:T(8,128)(2,1)S(1)} %shard_map.81.own), channel_id=1, source_target_pairs={{0,8},{8,0},{1,9},{9,1},{2,10},{10,2},{3,11},{11,3},{4,12},{12,4},... | collective-permute-start | bytes 196616 | tf_op jit(solution)/shard_map/ppermute | solution.py:462
  63.9 1.9 %collective-permute-start.5 = (bf16[1792,128]{1,0:T(8,128)(2,1)S(1)}, bf16[1792,128]{1,0:T(8,128)(2,1)S(1)}, u32[]{:S(2)}, u32[]{:S(2)}) collective-permute-start(bf16[1792,128]{1,0:T(8,128)(2,1)S(1)} %get-tuple-element.47), channel_id=1, source_target_pairs={{0,8},{8,0},{1,9},{9,1},{2,10},{10,2},{3,11},{11,3},{4,12},{12,4},... | collective-permute-start | bytes 1376264 | tf_op jit(solution)/shard_map/ppermute | solution.py:462
  66.6 25.2 %all-to-all-start.2 = ((bf16[16,112,128]{2,1,0:T(8,128)(2,1)}), bf16[16,112,128]{2,1,0:T(8,128)(2,1)S(1)}, u32[]{:S(2)}, u32[]{:S(2)}) async-start(bf16[16,112,128]{2,1,0:T(8,128)(2,1)} %shard_map.83), calls=%async_computation.2 | async-start | bytes 917504 | tf_op jit(solution)/shard_map/all_to_all | solution.py:457
  78.0 7.3 %collective-permute-start.6 = (bf16[2,2,128,256]{3,2,1,0:T(8,128)(2,1)S(1)}, bf16[2,2,128,256]{3,2,1,0:T(8,128)(2,1)S(1)}, u32[]{:S(2)}, u32[]{:S(2)}) collective-permute-start(bf16[2,2,128,256]{3,2,1,0:T(8,128)(2,1)S(1)} %get-tuple-element.53), channel_id=1, source_target_pairs={{0,2},{2,0},{4,6},{6,4},{1,3},{3,1},{5,7},{7,5},{8,10},{10,8},{12,... | collective-permute-start | bytes 786440 | tf_op jit(solution)/shard_map/ppermute | solution.py:462
  92.6 17.9 %all-to-all-start.3 = ((bf16[16,112,128]{2,1,0:T(8,128)(2,1)}), bf16[16,112,128]{2,1,0:T(8,128)(2,1)S(1)}, u32[]{:S(2)}, u32[]{:S(2)}) async-start(bf16[16,112,128]{2,1,0:T(8,128)(2,1)} %shard_map.84), calls=%async_computation.3 | async-start | bytes 917504 | tf_op jit(solution)/shard_map/all_to_all | solution.py:457
  97.0 5.1 %collective-permute-start.7 = (bf16[2,128,256]{2,1,0:T(8,128)(2,1)S(1)}, bf16[2,128,256]{2,1,0:T(8,128)(2,1)S(1)}, u32[]{:S(2)}, u32[]{:S(2)}) collective-permute-start(bf16[2,128,256]{2,1,0:T(8,128)(2,1)S(1)} %get-tuple-element.57), channel_id=1, source_target_pairs={{0,6},{2,4},{4,2},{6,0},{1,7},{3,5},{5,3},{7,1},{8,14},{10,12},{12... | collective-permute-start | bytes 393224 | tf_op jit(solution)/shard_map/ppermute | solution.py:467
  102.1 5.2 %collective-permute-start.8 = (bf16[128,256]{1,0:T(8,128)(2,1)S(1)}, bf16[128,256]{1,0:T(8,128)(2,1)S(1)}, u32[]{:S(2)}, u32[]{:S(2)}) collective-permute-start(bf16[128,256]{1,0:T(8,128)(2,1)S(1)} %get-tuple-element.59), channel_id=1, source_target_pairs={{0,1},{1,0},{2,3},{3,2},{4,5},{5,4},{6,7},{7,6},{8,9},{9,8},{10,11... | collective-permute-start | bytes 196616 | tf_op jit(solution)/shard_map/ppermute | solution.py:462
  110.5 4.6 %collective-permute-start.9 = (bf16[1792,128]{1,0:T(8,128)(2,1)S(1)}, bf16[1792,128]{1,0:T(8,128)(2,1)S(1)}, u32[]{:S(2)}, u32[]{:S(2)}) collective-permute-start(bf16[1792,128]{1,0:T(8,128)(2,1)S(1)} %bitcast.15), channel_id=1, source_target_pairs={{0,8},{8,0},{1,9},{9,1},{2,10},{10,2},{3,11},{11,3},{4,12},{12,4},... | collective-permute-start | bytes 1376264 | tf_op jit(solution)/shard_map/ppermute | solution.py:462

commit v8 on v5

--- a/solution.py
+++ b/solution.py
@@ -265,7 +265,7 @@
             out[g, h * 128 : h * 128 + 128, :] = v
 
 
-def gather_hidden(parts, field, section):
+def section_rows(parts, section):
     flt = lax.axis_index("flt_x") * 2 + lax.axis_index("flt_y")
     for h in (0, 1):
         row = pl.ds(pl.multiple_of(h * 128 + flt * 16, 16), 16)
@@ -275,6 +275,9 @@
         v = v * sigmoid(v)
         for i in range(4):
             section[0, i, :, h * 128 : h * 128 + 128] = v[4 * i : 4 * i + 4]
+
+
+def gather_hidden(parts, field):
     lane = lanes(ROWS)
     for h in (0, 1):
         blocks = [parts[4 * h + m, ROWS:, :].astype(f32) for m in range(4)]
@@ -529,9 +532,7 @@
     parts = exchange(partial, FLT)
     (err,) = kernel_call(second_error, [shape((128, 256), bf16)], 0, parts, got)
     across, within = next_chip(err), swapped(err)
-    hidden, section_out = kernel_call(
-        gather_hidden, [shape((1024, 256), bf16), shape((1, 4, 4, 256), f32)], 0, parts
-    )
+    (hidden,) = kernel_call(gather_hidden, [shape((1024, 256), bf16)], 0, parts)
     window, kept, sent = kernel_call(
         backward,
         [shape((1024, 1152), bf16), shape((GRAD_PAD, 128), f32), shape((GRAD_PAD, 128), bf16)],
@@ -556,13 +557,14 @@
     )
     chunk = shape((16, GRAD_PAD // 16, 128), bf16)
     (mine,) = kernel_call(add_core, [chunk], 0, kept, came)
-    mine, sent_in = lax.optimization_barrier((mine, sent_in))
+    mine, sent_in, parts = lax.optimization_barrier((mine, sent_in, parts))
+    (section_out,) = kernel_call(section_rows, [shape((1, 4, 4, 256), f32)], 0, parts)
     came_in = swapped(sent_in, "flt_x")
     (mine,) = kernel_call(add_chips, [chunk], 0, exchange(mine, CHIPS))
     kept_in, sent_in = kernel_call(
         add_pairs, [shape((2, 128, 256), f32), shape((2, 128, 256), bf16)], 0, kept_in, came_in
     )
-    mine, sent_in = lax.optimization_barrier((mine, sent_in))
+    mine, sent_in, section_out = lax.optimization_barrier((mine, sent_in, section_out))
     came_in = mirrored(sent_in, "flt_x")
     mine = exchange(mine, CHIPS).reshape(GRAD_PAD, 128)
     kept_in, sent_in = kernel_call(

time: 117 us -> 117 us (level)
    pallas_call x16 -> x17, Pallas kernels: 14.5 us -> 14.6 us  [kernel_call(): pl.pallas_call(body, out_shape=outs, in_specs=[pl.BlockSpec(memory_space=...]
where the time goes in v8:
time: 117 us; the launch traced here: 116 us
  waiting for transfers between devices  44.3 us (38%)
  starting transfers between devices  39.7 us (34%)
  blocking collectives  16.7 us (14%)
  Pallas kernels  14.6 us (12%)
    all_to_all x3, waiting for transfers between devices, exchange(): return lax.all_to_all(v, axis, 0, 0, tiled=True)  23.5 us
    all_to_all x3, starting transfers between devices, exchange(): return lax.all_to_all(v, axis, 0, 0, tiled=True)  22.3 us
    all_to_all x1, blocking collectives, exchange(): return lax.all_to_all(v, axis, 0, 0, tiled=True)  16.7 us
    pallas_call x17, Pallas kernels, kernel_call(): pl.pallas_call(body, out_shape=outs, in_specs=[pl.BlockSpec(memory_space=...  14.6 us
    ppermute x7, waiting for transfers between devices, swapped(): return lax.ppermute(v, axis, [(i, i ^ 1) for i in range(n)])  11.8 us
    ppermute x2, starting transfers between devices, next_chip(): return lax.ppermute(v, SP, pairs + [(b, a) for a, b in pairs])  10.4 us
    ppermute x7, starting transfers between devices, swapped(): return lax.ppermute(v, axis, [(i, i ^ 1) for i in range(n)])  6.17 us
    ppermute x2, waiting for transfers between devices, next_chip(): return lax.ppermute(v, SP, pairs + [(b, a) for a, b in pairs])  4.8 us
  transfers between devices with their start and end apart: 13, of which 10 were waited for; matrix products, arithmetic and copies ran while one was open for 0% of the time, Pallas kernels for 3%

profile of v8, /device:TPU:1, one launch (start us, length us, event | category | flops | bytes accessed | tf_op | source)
XLA Modules:
  0.0 116.1 jit_solution(8613627236230886229)
XLA Ops:
  0.6 2.4 %shard_map.75 = bf16[8,416,128]{2,1,0:T(8,128)(2,1)} custom-call(bf16[128,256]{1,0:T(8,128)(2,1)} %bitcast.22, bf16[864,256]{1,0:T(8,128)(2,1)} %bitcast.20, bf16[1,4,4,256]{3,2,1,0:T(4,128)(2,1)} %cot_far.1), custom_call_target="tpu_custom_call" | custom-call | bytes 1368064 | tf_op jit(solution)/shard_map/pallas_call | solution.py:32
  3.0 7.5 %all-to-all-start = ((bf16[8,416,128]{2,1,0:T(8,128)(2,1)}), bf16[8,416,128]{2,1,0:T(8,128)(2,1)S(1)}, u32[]{:S(2)}, u32[]{:S(2)}) async-start(bf16[8,416,128]{2,1,0:T(8,128)(2,1)} %shard_map.75), calls=%async_computation | async-start | bytes 1703936 | tf_op jit(solution)/shard_map/all_to_all | solution.py:460
  10.6 13.6 %all-to-all-done.got = bf16[8,416,128]{2,1,0:T(8,128)(2,1)S(1)} async-done(((bf16[8,416,128]{2,1,0:T(8,128)(2,1)}), bf16[8,416,128]{2,1,0:T(8,128)(2,1)S(1)}, u32[]{:S(2)}, u32[]{:S(2)}) %all-to-all-start) | async-done | bytes 852000 | tf_op jit(solution)/shard_map/all_to_all | solution.py:460
  24.2 1.5 %shard_map.77 = (f32[256,128]{1,0:T(8,128)S(1)}, f32[256,128]{1,0:T(8,128)S(1)}, f32[256,128]{1,0:T(8,128)S(1)}, f32[256,128]{1,0:T(8,128)S(1)}, bf16[1024,256]{...) custom-call(bf16[8,416,128]{2,1,0:T(8,128)(2,1)S(1)} %all-to-all-done.got, bf16[384,768]{1,0:T(8,128)(2,1)S(1)} %get-tuple-element.35.wide), custom_call_target="tpu_custom_call" | custom-call | flops 603979776 | bytes 2752512 | tf_op jit(solution)/shard_map/pallas_call | solution.py:32
  25.7 1.3 %collective-permute-start.2 = (bf16[8,128,128]{2,1,0:T(8,128)(2,1)S(1)}, bf16[8,128,128]{2,1,0:T(8,128)(2,1)S(1)}, u32[]{:S(2)}, u32[]{:S(2)}) collective-permute-start(bf16[8,128,128]{2,1,0:T(8,128)(2,1)S(1)} %get-tuple-element.40.own), channel_id=1, source_target_pairs={{0,8},{8,0},{1,9},{9,1},{2,10},{10,2},{3,11},{11,3},{4,12},{12,4},... | collective-permute-start | bytes 786440 | tf_op jit(solution)/shard_map/ppermute | solution.py:465
  27.0 2.6 %collective-permute-start.1 = (f32[256,128]{1,0:T(8,128)S(1)}, f32[256,128]{1,0:T(8,128)S(1)}, u32[]{:S(2)}, u32[]{:S(2)}) collective-permute-start(f32[256,128]{1,0:T(8,128)S(1)} %get-tuple-element.39), channel_id=1, source_target_pairs={{8,16},{24,32},{40,48},{56,64},{72,80},{88,96},{104,112},{120,128}... | collective-permute-start | bytes 393224 | tf_op jit(solution)/shard_map/ppermute | solution.py:475
  29.8 3.5 %collective-permute-done.1.across = f32[256,128]{1,0:T(8,128)S(1)} collective-permute-done((f32[256,128]{1,0:T(8,128)S(1)}, f32[256,128]{1,0:T(8,128)S(1)}, u32[]{:S(2)}, u32[]{:S(2)}) %collective-permute-start.1) | collective-permute-done | bytes 131104 | tf_op jit(solution)/shard_map/ppermute | solution.py:475
  33.3 0.6 shard_map.79
  33.9 16.7 %all_to_all.20.parts = bf16[8,512,128]{2,1,0:T(8,128)(2,1)S(1)} all-to-all(bf16[8,512,128]{2,1,0:T(8,128)(2,1)S(1)} %get-tuple-element.41), channel_id=1, replica_groups=mesh['sp_z'=8,'sp_y'=2,'core'=2,'flt_x'=4,'flt_y'=2] {'flt_x','flt_y'}, dimensions={0} | all-to-all | bytes 2097152 | tf_op jit(solution)/shard_map/all_to_all | solution.py:460
  50.8 7.8 %collective-permute-start.4 = (bf16[128,256]{1,0:T(8,128)(2,1)S(1)}, bf16[128,256]{1,0:T(8,128)(2,1)S(1)}, u32[]{:S(2)}, u32[]{:S(2)}) collective-permute-start(bf16[128,256]{1,0:T(8,128)(2,1)S(1)} %shard_map.80.own), channel_id=1, source_target_pairs={{8,16},{24,32},{40,48},{56,64},{72,80},{88,96},{104,112},{120,128}... | collective-permute-start | bytes 196616 | tf_op jit(solution)/shard_map/ppermute | solution.py:475
  58.7 0.5 shard_map.81.hidden
  59.2 1.3 %collective-permute-done.4.across = bf16[128,256]{1,0:T(8,128)(2,1)S(1)} collective-permute-done((bf16[128,256]{1,0:T(8,128)(2,1)S(1)}, bf16[128,256]{1,0:T(8,128)(2,1)S(1)}, u32[]{:S(2)}, u32[]{:S(2)}) %collective-permute-start.4) | collective-permute-done | bytes 65568 | tf_op jit(solution)/shard_map/ppermute | solution.py:475
  60.5 3.3 %shard_map.82 = (bf16[1024,1152]{1,0:T(8,128)(2,1)S(1)}, f32[1792,128]{1,0:T(8,128)S(1)}, bf16[1792,128]{1,0:T(8,128)(2,1)S(1)}) custom-call(bf16[128,256]{1,0:T(8,128)(2,1)S(1)} %shard_map.80.own, bf16[128,256]{1,0:T(8,128)(2,1)S(1)} %collective-permute-done.3.within, bf16[128,256]{1,0:T(8,128)(2,1)S(1)} %collective-permute-done.4.across, ...), custom_call_target="tpu_custom_call" | custom-call | flops 905969664 | bytes 5832704 | tf_op jit(solution)/shard_map/pallas_call | solution.py:32
  64.0 0.9 shard_map.84
  64.9 0.9 collective-permute-done.5.came
  65.8 0.8 shard_map.83
  66.6 10.5 %all-to-all-start.2 = ((bf16[16,112,128]{2,1,0:T(8,128)(2,1)}), bf16[16,112,128]{2,1,0:T(8,128)(2,1)S(1)}, u32[]{:S(2)}, u32[]{:S(2)}) async-start(bf16[16,112,128]{2,1,0:T(8,128)(2,1)} %shard_map.83), calls=%async_computation.2 | async-start | bytes 917504 | tf_op jit(solution)/shard_map/all_to_all | solution.py:460
  77.2 0.6 shard_map.87
  77.8 6.5 %collective-permute-done.6.came = bf16[2,2,128,256]{3,2,1,0:T(8,128)(2,1)S(1)} collective-permute-done((bf16[2,2,128,256]{3,2,1,0:T(8,128)(2,1)S(1)}, bf16[2,2,128,256]{3,2,1,0:T(8,128)(2,1)S(1)}, u32[]{:S(2)}, u32[]{:S(2)}) %collective-permute-start.6) | collective-permute-done | bytes 262176 | tf_op jit(solution)/shard_map/ppermute | solution.py:465
  84.4 7.4 %all-to-all-done.2.parts = bf16[16,112,128]{2,1,0:T(8,128)(2,1)S(1)} async-done(((bf16[16,112,128]{2,1,0:T(8,128)(2,1)}), bf16[16,112,128]{2,1,0:T(8,128)(2,1)S(1)}, u32[]{:S(2)}, u32[]{:S(2)}) %all-to-all-start.2) | async-done | bytes 458784 | tf_op jit(solution)/shard_map/all_to_all | solution.py:460
  91.8 0.8 shard_map.85
  92.6 4.3 %all-to-all-start.3 = ((bf16[16,112,128]{2,1,0:T(8,128)(2,1)}), bf16[16,112,128]{2,1,0:T(8,128)(2,1)S(1)}, u32[]{:S(2)}, u32[]{:S(2)}) async-start(bf16[16,112,128]{2,1,0:T(8,128)(2,1)} %shard_map.85), calls=%async_computation.3 | async-start | bytes 917504 | tf_op jit(solution)/shard_map/all_to_all | solution.py:460
  97.0 0.9 collective-permute-start.7
  97.9 4.2 %collective-permute-done.7.came = bf16[2,128,256]{2,1,0:T(8,128)(2,1)S(1)} collective-permute-done((bf16[2,128,256]{2,1,0:T(8,128)(2,1)S(1)}, bf16[2,128,256]{2,1,0:T(8,128)(2,1)S(1)}, u32[]{:S(2)}, u32[]{:S(2)}) %collective-permute-start.7) | collective-permute-done | bytes 131104 | tf_op jit(solution)/shard_map/ppermute | solution.py:470
  102.1 1.3 %collective-permute-start.8 = (bf16[128,256]{1,0:T(8,128)(2,1)S(1)}, bf16[128,256]{1,0:T(8,128)(2,1)S(1)}, u32[]{:S(2)}, u32[]{:S(2)}) collective-permute-start(bf16[128,256]{1,0:T(8,128)(2,1)S(1)} %get-tuple-element.59), channel_id=1, source_target_pairs={{0,1},{1,0},{2,3},{3,2},{4,5},{5,4},{6,7},{7,6},{8,9},{9,8},{10,11... | collective-permute-start | bytes 196616 | tf_op jit(solution)/shard_map/ppermute | solution.py:465
  103.4 3.9 %collective-permute-done.8.came = bf16[128,256]{1,0:T(8,128)(2,1)S(1)} collective-permute-done((bf16[128,256]{1,0:T(8,128)(2,1)S(1)}, bf16[128,256]{1,0:T(8,128)(2,1)S(1)}, u32[]{:S(2)}, u32[]{:S(2)}) %collective-permute-start.8) | collective-permute-done | bytes 65568 | tf_op jit(solution)/shard_map/ppermute | solution.py:465
  107.3 0.7 shard_map.89
  108.0 2.6 %all-to-all-done.3 = bf16[16,112,128]{2,1,0:T(8,128)(2,1)S(1)} async-done(((bf16[16,112,128]{2,1,0:T(8,128)(2,1)}), bf16[16,112,128]{2,1,0:T(8,128)(2,1)S(1)}, u32[]{:S(2)}, u32[]{:S(2)}) %all-to-all-start.3) | async-done | bytes 458784 | tf_op jit(solution)/shard_map/all_to_all | solution.py:460
  110.5 3.2 %collective-permute-start.9 = (bf16[1792,128]{1,0:T(8,128)(2,1)S(1)}, bf16[1792,128]{1,0:T(8,128)(2,1)S(1)}, u32[]{:S(2)}, u32[]{:S(2)}) collective-permute-start(bf16[1792,128]{1,0:T(8,128)(2,1)S(1)} %bitcast.15), channel_id=1, source_target_pairs={{0,8},{8,0},{1,9},{9,1},{2,10},{10,2},{3,11},{11,3},{4,12},{12,4},... | collective-permute-start | bytes 1376264 | tf_op jit(solution)/shard_map/ppermute | solution.py:465
  113.7 1.0 shard_map.90
  114.7 0.5 collective-permute-done.9.rows
  115.2 1.0 shard_map.91
  (14 shorter events, 0.8 us)
Async XLA Ops:
  0.6 9.9 %copy-start = (bf16[32,3,3,3,256]{4,0,3,2,1:T(8,128)(2,1)S(1)}, bf16[32,3,3,3,256]{4,0,3,2,1:T(8,128)(2,1)}, u32[]{:S(2)}) copy-start(bf16[32,3,3,3,256]{4,0,3,2,1:T(8,128)(2,1)} %param.5) | copy-start | bytes 1327108
  3.0 21.2 %all-to-all-start = ((bf16[8,416,128]{2,1,0:T(8,128)(2,1)}), bf16[8,416,128]{2,1,0:T(8,128)(2,1)S(1)}, u32[]{:S(2)}, u32[]{:S(2)}) async-start(bf16[8,416,128]{2,1,0:T(8,128)(2,1)} %shard_map.75), calls=%async_computation | async-start | bytes 1703936 | tf_op jit(solution)/shard_map/all_to_all | solution.py:460
  25.7 4.0 %collective-permute-start.2 = (bf16[8,128,128]{2,1,0:T(8,128)(2,1)S(1)}, bf16[8,128,128]{2,1,0:T(8,128)(2,1)S(1)}, u32[]{:S(2)}, u32[]{:S(2)}) collective-permute-start(bf16[8,128,128]{2,1,0:T(8,128)(2,1)S(1)} %get-tuple-element.40.own), channel_id=1, source_target_pairs={{0,8},{8,0},{1,9},{9,1},{2,10},{10,2},{3,11},{11,3},{4,12},{12,4},... | collective-permute-start | bytes 786440 | tf_op jit(solution)/shard_map/ppermute | solution.py:465
  26.9 2.9 %collective-permute-start = (f32[256,128]{1,0:T(8,128)S(1)}, f32[256,128]{1,0:T(8,128)S(1)}, u32[]{:S(2)}, u32[]{:S(2)}) collective-permute-start(f32[256,128]{1,0:T(8,128)S(1)} %get-tuple-element.38), channel_id=1, source_target_pairs={{0,8},{8,0},{1,9},{9,1},{2,10},{10,2},{3,11},{11,3},{4,12},{12,4},... | collective-permute-start | bytes 393224 | tf_op jit(solution)/shard_map/ppermute | solution.py:465
  27.0 6.3 %collective-permute-start.1 = (f32[256,128]{1,0:T(8,128)S(1)}, f32[256,128]{1,0:T(8,128)S(1)}, u32[]{:S(2)}, u32[]{:S(2)}) collective-permute-start(f32[256,128]{1,0:T(8,128)S(1)} %get-tuple-element.39), channel_id=1, source_target_pairs={{8,16},{24,32},{40,48},{56,64},{72,80},{88,96},{104,112},{120,128}... | collective-permute-start | bytes 393224 | tf_op jit(solution)/shard_map/ppermute | solution.py:475
  50.8 9.7 %collective-permute-start.4 = (bf16[128,256]{1,0:T(8,128)(2,1)S(1)}, bf16[128,256]{1,0:T(8,128)(2,1)S(1)}, u32[]{:S(2)}, u32[]{:S(2)}) collective-permute-start(bf16[128,256]{1,0:T(8,128)(2,1)S(1)} %shard_map.80.own), channel_id=1, source_target_pairs={{8,16},{24,32},{40,48},{56,64},{72,80},{88,96},{104,112},{120,128}... | collective-permute-start | bytes 196616 | tf_op jit(solution)/shard_map/ppermute | solution.py:475
  58.6 1.9 %collective-permute-start.3 = (bf16[128,256]{1,0:T(8,128)(2,1)S(1)}, bf16[128,256]{1,0:T(8,128)(2,1)S(1)}, u32[]{:S(2)}, u32[]{:S(2)}) collective-permute-start(bf16[128,256]{1,0:T(8,128)(2,1)S(1)} %shard_map.80.own), channel_id=1, source_target_pairs={{0,8},{8,0},{1,9},{9,1},{2,10},{10,2},{3,11},{11,3},{4,12},{12,4},... | collective-permute-start | bytes 196616 | tf_op jit(solution)/shard_map/ppermute | solution.py:465
  63.9 1.9 %collective-permute-start.5 = (bf16[1792,128]{1,0:T(8,128)(2,1)S(1)}, bf16[1792,128]{1,0:T(8,128)(2,1)S(1)}, u32[]{:S(2)}, u32[]{:S(2)}) collective-permute-start(bf16[1792,128]{1,0:T(8,128)(2,1)S(1)} %get-tuple-element.45), channel_id=1, source_target_pairs={{0,8},{8,0},{1,9},{9,1},{2,10},{10,2},{3,11},{11,3},{4,12},{12,4},... | collective-permute-start | bytes 1376264 | tf_op jit(solution)/shard_map/ppermute | solution.py:465
  66.6 25.2 %all-to-all-start.2 = ((bf16[16,112,128]{2,1,0:T(8,128)(2,1)}), bf16[16,112,128]{2,1,0:T(8,128)(2,1)S(1)}, u32[]{:S(2)}, u32[]{:S(2)}) async-start(bf16[16,112,128]{2,1,0:T(8,128)(2,1)} %shard_map.83), calls=%async_computation.2 | async-start | bytes 917504 | tf_op jit(solution)/shard_map/all_to_all | solution.py:460
  77.1 7.3 %collective-permute-start.6 = (bf16[2,2,128,256]{3,2,1,0:T(8,128)(2,1)S(1)}, bf16[2,2,128,256]{3,2,1,0:T(8,128)(2,1)S(1)}, u32[]{:S(2)}, u32[]{:S(2)}) collective-permute-start(bf16[2,2,128,256]{3,2,1,0:T(8,128)(2,1)S(1)} %get-tuple-element.51), channel_id=1, source_target_pairs={{0,2},{2,0},{4,6},{6,4},{1,3},{3,1},{5,7},{7,5},{8,10},{10,8},{12,... | collective-permute-start | bytes 786440 | tf_op jit(solution)/shard_map/ppermute | solution.py:465
  92.6 17.9 %all-to-all-start.3 = ((bf16[16,112,128]{2,1,0:T(8,128)(2,1)}), bf16[16,112,128]{2,1,0:T(8,128)(2,1)S(1)}, u32[]{:S(2)}, u32[]{:S(2)}) async-start(bf16[16,112,128]{2,1,0:T(8,128)(2,1)} %shard_map.85), calls=%async_computation.3 | async-start | bytes 917504 | tf_op jit(solution)/shard_map/all_to_all | solution.py:460
  97.0 5.1 %collective-permute-start.7 = (bf16[2,128,256]{2,1,0:T(8,128)(2,1)S(1)}, bf16[2,128,256]{2,1,0:T(8,128)(2,1)S(1)}, u32[]{:S(2)}, u32[]{:S(2)}) collective-permute-start(bf16[2,128,256]{2,1,0:T(8,128)(2,1)S(1)} %get-tuple-element.57), channel_id=1, source_target_pairs={{0,6},{2,4},{4,2},{6,0},{1,7},{3,5},{5,3},{7,1},{8,14},{10,12},{12... | collective-permute-start | bytes 393224 | tf_op jit(solution)/shard_map/ppermute | solution.py:470
  102.1 5.2 %collective-permute-start.8 = (bf16[128,256]{1,0:T(8,128)(2,1)S(1)}, bf16[128,256]{1,0:T(8,128)(2,1)S(1)}, u32[]{:S(2)}, u32[]{:S(2)}) collective-permute-start(bf16[128,256]{1,0:T(8,128)(2,1)S(1)} %get-tuple-element.59), channel_id=1, source_target_pairs={{0,1},{1,0},{2,3},{3,2},{4,5},{5,4},{6,7},{7,6},{8,9},{9,8},{10,11... | collective-permute-start | bytes 196616 | tf_op jit(solution)/shard_map/ppermute | solution.py:465
  110.5 4.6 %collective-permute-start.9 = (bf16[1792,128]{1,0:T(8,128)(2,1)S(1)}, bf16[1792,128]{1,0:T(8,128)(2,1)S(1)}, u32[]{:S(2)}, u32[]{:S(2)}) collective-permute-start(bf16[1792,128]{1,0:T(8,128)(2,1)S(1)} %bitcast.15), channel_id=1, source_target_pairs={{0,8},{8,0},{1,9},{9,1},{2,10},{10,2},{3,11},{11,3},{4,12},{12,4},... | collective-permute-start | bytes 1376264 | tf_op jit(solution)/shard_map/ppermute | solution.py:465
